TPU v7x, 32 devices: a whole 2x2x4 slice. The times are simulated.
32 devices in a mesh: case: 2 (over y), mode: 4 (over z), harm: 2 (over x), rad: 2 (over core).
Axes of the slice: x: 2, y: 2, z: 4, core: 2. Of those that a mesh axis runs over, the one named last changes fastest.
Arguments:
- direct_field: bfloat16 [16, 16, 2, 5, 16, 256], P(('case', 'harm'), 'mode', None, None, None, 'rad'), parts along dimension 0, may hold values from -6 to 6
- adjoint_field: bfloat16 [16, 16, 2, 5, 16, 256], P(('case', 'harm'), 'mode', None, None, None, 'rad'), parts along dimension 0, may hold values from -6 to 6
- triad_slots: int32 [16, 4, 2], P('mode'), may hold values from 0 to 3
Outputs:
- sensitivity: float32 [32, 2, 5, 16, 256], P(('case', 'harm'), None, None, 'mode', 'rad'), parts along dimension 0
There are 2 independent parts, one for each index of `case`. A program takes and returns all parts, laid end to end along the dimension named above; an argument that names none is the same for every part. Nothing has to cross between parts.
Inputs may be any that keep to these rules, and one draw needn't show every extreme that they name: triad_slots[m, s, 0] is the slot, within the block of 4 modes holding m, of the adjoint factor; triad_slots[m, s, 1] is the slot of the direct factor within the block s blocks below m's block, counted cyclically over 4 blocks.
All inputs are finite; a program needn't handle non-finite values.
Results may differ from a plain program's by a relative error of at most 0.0003.
Values may be sent and summed in bfloat16 or wider, within the bound.
No kernel may reach another device: no remote copies, remote signals or barrier semaphores. Data moves between devices by JAX's collectives and lax.ppermute only.
A program may use at most 64 MiB of HBM per device.

v0:
```python
import math

import jax
import jax.numpy as jnp
from jax import lax
from jax.sharding import PartitionSpec as P

HARMS = 8


def padded_2(block, sides, width):
    for axis, dim in sides:
        count = lax.axis_size(axis)
        forward = [(i, i + 1) for i in range(count - 1)]
        backward = [(target, source) for source, target in forward]
        low = lax.ppermute(
            lax.slice_in_dim(block, block.shape[dim] - width, None, axis=dim), axis, forward
        )
        high = lax.ppermute(lax.slice_in_dim(block, 0, width, axis=dim), axis, backward)
        block = jnp.concatenate([low, block, high], axis=dim)
    return block


def passed_along(value, axis, steps):
    count = lax.axis_size(axis)
    pairs = [(source, (source + steps) % count) for source in range(count)]
    return lax.ppermute(value, axis, pairs)


def stencil(padded, axis, length):

    def shifted(offset):
        return lax.slice_in_dim(padded, offset, offset + length, axis=axis)

    return (shifted(0) - 8.0 * shifted(1) + 8.0 * shifted(3) - shifted(4)) / 12.0


def derivative(source, axis):
    length = source.shape[axis]
    widths = [(0, 0)] * source.ndim
    widths[axis] = (2, 2)
    return stencil(jnp.pad(source, widths), axis, length)


def conj_product(left_side, right_side):
    left_real = left_side[..., 0, :, :, :]
    left_imag = left_side[..., 1, :, :, :]
    right_real = right_side[..., 0, :, :, :]
    right_imag = right_side[..., 1, :, :, :]
    return jnp.stack(
        [
            left_real * right_real + left_imag * right_imag,
            left_real * right_imag - left_imag * right_real,
        ],
        axis=-4,
    )


def triad_term(adjoint, adjoint_axial, adjoint_radial, direct, direct_axial, direct_radial):
    total_sum = conj_product(direct[..., 1:2, :, :], adjoint_axial)
    total_sum = total_sum + conj_product(direct[..., 2:3, :, :], adjoint_radial)
    total_sum = total_sum + conj_product(direct_axial, adjoint[..., 1:2, :, :])
    return total_sum + conj_product(direct_radial, adjoint[..., 2:3, :, :])


def choose(source, picked_rows):
    slot_count = source.shape[1]
    wanted = picked_rows.reshape((1, slot_count, 1, 1, 1, 1))
    picked = jnp.zeros(source.shape, jnp.float32)
    for slot_index in range(slot_count):
        candidate = lax.slice_in_dim(source, slot_index, slot_index + 1, axis=1)
        picked = picked + jnp.where(wanted == slot_index, candidate, 0.0)
    return picked


def body(direct_field, adjoint_field, triad_slots):
    stop_count = lax.axis_size("mode")
    radial_cells = adjoint_field.shape[5]
    adjoint = adjoint_field.astype(jnp.float32)
    adjoint_axial = derivative(adjoint, 4)
    adjoint_wide = padded_2(adjoint_field, (("rad", 5),), 2)
    adjoint_radial = stencil(adjoint_wide.astype(jnp.float32), 5, radial_cells)
    adjoint_slots = triad_slots[:, :, 0]
    direct_slots = triad_slots[:, :, 1]

    def add_stop(running, visiting, stop_index):
        direct_core = lax.slice_in_dim(visiting, 2, 2 + radial_cells, axis=5)
        direct = direct_core.astype(jnp.float32)
        direct_axial = derivative(direct, 4)
        direct_radial = stencil(visiting.astype(jnp.float32), 5, radial_cells)
        adjoint_rows = lax.dynamic_index_in_dim(adjoint_slots, stop_index, axis=1, keepdims=False)
        direct_rows = lax.dynamic_index_in_dim(direct_slots, stop_index, axis=1, keepdims=False)
        term = triad_term(
            choose(adjoint, adjoint_rows),
            choose(adjoint_axial, adjoint_rows),
            choose(adjoint_radial, adjoint_rows),
            choose(direct, direct_rows),
            choose(direct_axial, direct_rows),
            choose(direct_radial, direct_rows),
        )
        return running + jnp.sum(term, axis=0)

    start_block = padded_2(direct_field, (("rad", 5),), 2)
    running = jnp.zeros(adjoint.shape[1:], jnp.float32)

    def one_side(step_index, carry):
        running_sum, visiting = carry
        arriving = passed_along(visiting, "mode", 1)
        running_sum = add_stop(running_sum, visiting, step_index)
        return (running_sum, arriving)

    running, visiting = lax.fori_loop(0, stop_count - 1, one_side, (running, start_block))
    running = add_stop(running, visiting, stop_count - 1)
    slabs = lax.all_to_all(running, "mode", split_axis=3, concat_axis=0, tiled=True)
    summed = lax.psum_scatter(slabs, "harm", scatter_dimension=0, tiled=True)
    return summed * (1.0 / math.sqrt(8.0 * stop_count * HARMS))


def solution(mesh):
    return jax.shard_map(
        body,
        mesh=mesh,
        in_specs=(
            P(("case", "harm"), "mode", None, None, None, "rad"),
            P(("case", "harm"), "mode", None, None, None, "rad"),
            P("mode", None, None),
        ),
        out_specs=P(("case", "harm"), None, None, "mode", "rad"),
        check_vma=False,
    )
```

profile of v0, /device:TPU:0, one launch (start us, length us, event | category | flops | bytes accessed | tf_op | source)
XLA Modules:
  0.0 197.8 jit_solution(2446714134375759526)
XLA Ops:
  6.5 1.6 fusion.35
  8.1 1.0 copy.50
  9.1 1.3 collective-permute-start.2
  10.5 1.0 copy.49
  11.5 3.7 %collective-permute-start.1 = (bf16[4,4,2,5,16,2]{4,1,5,3,2,0:T(4,128)(2,1)S(1)}, bf16[4,4,2,5,16,2]{4,1,5,3,2,0:T(4,128)(2,1)}, u32[]{:S(2)}, u32[]{:S(2)}) collective-permute-start(bf16[4,4,2,5,16,2]{4,1,5,3,2,0:T(4,128)(2,1)S(1)} %copy.49), channel_id=1, source_target_pairs={{0,1},{2,3},{4,5},{6,7},{8,9},{10,11},{12,13},{14,15},{16,17},{18,... | collective-permute-start | bytes 30728 | tf_op jit(solution)/shard_map/ppermute | solution.py:16
  15.4 1.0 copy.52
  16.5 1.3 collective-permute-start.4
  17.8 1.0 copy.51
  18.8 4.0 %collective-permute-start.3 = (bf16[4,4,2,5,16,2]{4,1,5,3,2,0:T(4,128)(2,1)S(1)}, bf16[4,4,2,5,16,2]{4,1,5,3,2,0:T(4,128)(2,1)S(1)}, u32[]{:S(2)}, u32[]{:S(2)}) collective-permute-start(bf16[4,4,2,5,16,2]{4,1,5,3,2,0:T(4,128)(2,1)S(1)} %copy.51), channel_id=1, source_target_pairs={{0,1},{2,3},{4,5},{6,7},{8,9},{10,11},{12,13},{14,15},{16,17},{18,... | collective-permute-start | bytes 30728 | tf_op jit(solution)/shard_map/ppermute | solution.py:16
  23.0 1.1 slice_bitcast_fusion.39
  24.1 1.3 compare_reduce_fusion.7
  25.6 1.0 copy.42
  26.7 1.9 copy.44
  29.3 2.7 %fusion.15 = (f32[4,4,2,5,16,128]{5,4,3,2,0,1:T(8,128)}, f32[4,4,2,5,16,128]{5,4,3,2,0,1:T(8,128)}) fusion(f32[4,4,2,5,16,128]{5,4,3,2,0,1:T(8,128)S(1)} %get-tuple-element.587, f32[4,4,2,5,16,132]{5,4,3,2,0,1:T(8,128)S(1)} %maximum_convert_fusion), kind=kLoop, calls=%fused_computation.89 | loop fusion | flops 3932160 | bytes 9175040 | tf_op jit(solution)/shard_map/div | solution.py:35
  32.0 2.0 %copy.36 = bf16[4,4,2,5,16,2]{5,4,3,2,0,1:T(8,128)(2,1)S(1)} copy(bf16[4,4,2,5,16,2]{4,1,5,3,2,0:T(4,128)(2,1)} %collective-permute-done.1) | data formatting | bytes 20480 | tf_op jit(solution)/shard_map/ppermute | solution.py:16
  34.0 1.0 copy.38
  35.0 1.8 pad_maximum_fusion
  36.8 105.0 %while.18 = (s32[]{:T(128)}, f32[4,2,5,16,128]{4,3,2,1,0:T(8,128)}, bf16[4,4,2,5,16,132]{5,4,3,2,0,1:T(8,128)(2,1)}, s32[4,4]{0,1:T(4,128)S(1)}, s32[4,4]{0,1:T(...) while((s32[]{:T(128)}, f32[4,2,5,16,128]{4,3,2,1,0:T(8,128)}, ...), condition=%wide.region_2.3_spmd.clone, body=%wide.region_0.2_spmd.clone.sunk | while | flops 24995872 | bytes 105566816 | solution.py:112
  36.8 3.0 %copy.62 = bf16[4,4,2,5,16,132]{5,4,3,2,0,1:T(8,128)(2,1)} copy(bf16[4,4,2,5,16,132]{5,4,3,2,0,1:T(8,128)(2,1)} %get-tuple-element.592) | data formatting | bytes 1351680 | tf_op jit(solution)/shard_map/while
  39.9 3.0 %collective-permute-start = (bf16[4,4,2,5,16,132]{5,4,3,2,0,1:T(8,128)(2,1)}, bf16[4,4,2,5,16,132]{5,4,3,2,0,1:T(8,128)(2,1)}, u32[]{:S(2)}, u32[]{:S(2)}) collective-permute-start(bf16[4,4,2,5,16,132]{5,4,3,2,0,1:T(8,128)(2,1)} %copy.62), channel_id=1, source_target_pairs={{0,4},{4,8},{8,12},{12,0},{1,5},{5,9},{9,13},{13,1},{2,6},{6,10},{... | collective-permute-start | bytes 2027528 | tf_op jit(solution)/shard_map/while/body/eval_jaxpr/ppermute | solution.py:27
  42.9 1.6 slice_convert_fusion.3
  44.5 1.7 fusion.42
  47.2 1.7 convert_element_type.55
  48.9 1.4 slice_bitcast_fusion.71
  50.3 1.1 fusion.41
  52.6 1.1 select_add_fusion.17
  54.5 1.1 select_add_fusion.16
  55.8 1.0 multiply_add_fusion.14
  56.8 1.3 multiply_add_fusion.15
  61.0 12.6 %collective-permute-done = bf16[4,4,2,5,16,132]{5,4,3,2,0,1:T(8,128)(2,1)} collective-permute-done((bf16[4,4,2,5,16,132]{5,4,3,2,0,1:T(8,128)(2,1)}, bf16[4,4,2,5,16,132]{5,4,3,2,0,1:T(8,128)(2,1)}, u32[]{:S(2)}, u32[]{:S(2)}) %collective-permute-start) | collective-permute-done | bytes 675872 | tf_op jit(solution)/shard_map/while/body/eval_jaxpr/ppermute | solution.py:27
  73.6 3.0 %copy.62 = bf16[4,4,2,5,16,132]{5,4,3,2,0,1:T(8,128)(2,1)} copy(bf16[4,4,2,5,16,132]{5,4,3,2,0,1:T(8,128)(2,1)} %get-tuple-element.592) | data formatting | bytes 1351680 | tf_op jit(solution)/shard_map/while
  76.6 1.6 slice_convert_fusion.3
  78.2 1.7 fusion.42
  80.9 1.7 convert_element_type.55
  82.6 1.4 slice_bitcast_fusion.71
  84.0 1.1 fusion.41
  86.3 1.1 select_add_fusion.17
  88.2 1.1 select_add_fusion.16
  89.5 1.0 multiply_add_fusion.14
  90.5 1.3 multiply_add_fusion.15
  93.9 1.8 select_add_fusion.18
  95.6 12.5 %collective-permute-done = bf16[4,4,2,5,16,132]{5,4,3,2,0,1:T(8,128)(2,1)} collective-permute-done((bf16[4,4,2,5,16,132]{5,4,3,2,0,1:T(8,128)(2,1)}, bf16[4,4,2,5,16,132]{5,4,3,2,0,1:T(8,128)(2,1)}, u32[]{:S(2)}, u32[]{:S(2)}) %collective-permute-start) | collective-permute-done | bytes 675872 | tf_op jit(solution)/shard_map/while/body/eval_jaxpr/ppermute | solution.py:27
  108.1 3.0 %copy.62 = bf16[4,4,2,5,16,132]{5,4,3,2,0,1:T(8,128)(2,1)} copy(bf16[4,4,2,5,16,132]{5,4,3,2,0,1:T(8,128)(2,1)} %get-tuple-element.592) | data formatting | bytes 1351680 | tf_op jit(solution)/shard_map/while
  111.2 1.6 slice_convert_fusion.3
  112.8 1.7 fusion.42
  115.4 1.7 convert_element_type.55
  117.2 1.4 slice_bitcast_fusion.71
  118.5 1.1 fusion.41
  120.9 1.1 select_add_fusion.17
  122.8 1.1 select_add_fusion.16
  125.1 1.3 multiply_add_fusion.15
  128.4 1.8 select_add_fusion.18
  130.2 11.6 %collective-permute-done = bf16[4,4,2,5,16,132]{5,4,3,2,0,1:T(8,128)(2,1)} collective-permute-done((bf16[4,4,2,5,16,132]{5,4,3,2,0,1:T(8,128)(2,1)}, bf16[4,4,2,5,16,132]{5,4,3,2,0,1:T(8,128)(2,1)}, u32[]{:S(2)}, u32[]{:S(2)}) %collective-permute-start) | collective-permute-done | bytes 675872 | tf_op jit(solution)/shard_map/while/body/eval_jaxpr/ppermute | solution.py:27
  141.8 1.6 slice_convert_fusion.1
  143.4 1.7 convert_element_type.45
  145.8 1.2 copy-done.9
  147.1 1.2 copy-done.8
  148.4 1.1 fusion.24
  150.3 1.1 select_add_fusion.7
  151.5 1.1 select_add_fusion.8
  153.8 1.0 add.447
  155.1 10.4 %all_to_all.18 = f32[4,2,5,16,128]{4,0,2,1,3:T(4,128)S(1)} all-to-all(f32[4,2,5,16,128]{4,0,2,1,3:T(4,128)S(1)} %copy.47), channel_id=1, replica_groups=mesh['case'=2,'mode'=4,'harm'=2,'rad'=2] {'mode'}, dimensions={3} | all-to-all | bytes 655360 | tf_op jit(solution)/shard_map/all_to_all | solution.py:114
  167.5 21.8 %all-reduce.6.cloned.1.call-done = f32[16,2,5,4,128]{4,3,2,1,0:T(4,128)} async-done(((f32[16,2,5,4,128]{4,3,2,1,0:T(4,128)}), f32[16,2,5,4,128]{4,3,2,1,0:T(4,128)}) %all-reduce.6.cloned.1.call-update) | async-done | bytes 327696
  189.3 1.6 dynamic-slice_multiply_fusion
  (156 shorter events, 23.7 us)
Async XLA Ops:
  6.5 182.8 %all-reduce.6.cloned.1.call-start = ((), (), s32[]{:S(2)}) async-start(), calls=%async_computation.1 | async-start | bytes 655360
  8.1 7.1 %copy-start.12 = (bf16[4,4,2,5,16,128]{5,4,3,2,1,0:T(8,128)(2,1)S(1)}, bf16[4,4,2,5,16,128]{5,4,3,2,1,0:T(8,128)(2,1)}, u32[]{:S(2)}) copy-start(bf16[4,4,2,5,16,128]{5,4,3,2,1,0:T(8,128)(2,1)} %param.6) | copy-start | bytes 1966084
  9.1 24.8 %collective-permute-start.2 = (bf16[4,4,2,5,16,2]{4,1,5,3,2,0:T(4,128)(2,1)S(1)}, bf16[4,4,2,5,16,2]{4,1,5,3,2,0:T(4,128)(2,1)S(1)}, u32[]{:S(2)}, u32[]{:S(2)}) collective-permute-start(bf16[4,4,2,5,16,2]{4,1,5,3,2,0:T(4,128)(2,1)S(1)} %copy.50), channel_id=1, source_target_pairs={{1,0},{3,2},{5,4},{7,6},{9,8},{11,10},{13,12},{15,14},{17,16},{19,... | collective-permute-start | bytes 30728 | tf_op jit(solution)/shard_map/ppermute | solution.py:19
  11.5 20.5 %collective-permute-start.1 = (bf16[4,4,2,5,16,2]{4,1,5,3,2,0:T(4,128)(2,1)S(1)}, bf16[4,4,2,5,16,2]{4,1,5,3,2,0:T(4,128)(2,1)}, u32[]{:S(2)}, u32[]{:S(2)}) collective-permute-start(bf16[4,4,2,5,16,2]{4,1,5,3,2,0:T(4,128)(2,1)S(1)} %copy.49), channel_id=1, source_target_pairs={{0,1},{2,3},{4,5},{6,7},{8,9},{10,11},{12,13},{14,15},{16,17},{18,... | collective-permute-start | bytes 30728 | tf_op jit(solution)/shard_map/ppermute | solution.py:16
  16.5 10.2 %collective-permute-start.4 = (bf16[4,4,2,5,16,2]{4,1,5,3,2,0:T(4,128)(2,1)S(1)}, bf16[4,4,2,5,16,2]{4,1,5,3,2,0:T(4,128)(2,1)}, u32[]{:S(2)}, u32[]{:S(2)}) collective-permute-start(bf16[4,4,2,5,16,2]{4,1,5,3,2,0:T(4,128)(2,1)S(1)} %copy.52), channel_id=1, source_target_pairs={{1,0},{3,2},{5,4},{7,6},{9,8},{11,10},{13,12},{15,14},{17,16},{19,... | collective-permute-start | bytes 30728 | tf_op jit(solution)/shard_map/ppermute | solution.py:19
  18.8 4.2 %copy-start.18 = (s32[4,4,2]{1,2,0:T(2,128)S(1)}, s32[4,4,2]{1,2,0:T(2,128)}, u32[]{:S(2)}) copy-start(s32[4,4,2]{1,2,0:T(2,128)} %param.7) | copy-start | bytes 388
  18.8 6.8 %collective-permute-start.3 = (bf16[4,4,2,5,16,2]{4,1,5,3,2,0:T(4,128)(2,1)S(1)}, bf16[4,4,2,5,16,2]{4,1,5,3,2,0:T(4,128)(2,1)S(1)}, u32[]{:S(2)}, u32[]{:S(2)}) collective-permute-start(bf16[4,4,2,5,16,2]{4,1,5,3,2,0:T(4,128)(2,1)S(1)} %copy.51), channel_id=1, source_target_pairs={{0,1},{2,3},{4,5},{6,7},{8,9},{10,11},{12,13},{14,15},{16,17},{18,... | collective-permute-start | bytes 30728 | tf_op jit(solution)/shard_map/ppermute | solution.py:16
  32.0 3.0 %copy-start.13 = (bf16[4,4,2,5,16,128]{5,4,3,2,1,0:T(8,128)(2,1)S(1)}, bf16[4,4,2,5,16,128]{5,4,3,2,1,0:T(8,128)(2,1)}, u32[]{:S(2)}) copy-start(bf16[4,4,2,5,16,128]{5,4,3,2,1,0:T(8,128)(2,1)} %param.5) | copy-start | bytes 1966084
  36.8 3.0 %copy-start.1 = (f32[4,4,2,5,16,128]{5,4,3,2,0,1:T(8,128)}, f32[4,4,2,5,16,128]{5,4,3,2,0,1:T(8,128)S(1)}, u32[]{:S(2)}) copy-start(f32[4,4,2,5,16,128]{5,4,3,2,0,1:T(8,128)S(1)} %get-tuple-element.607) | copy-start | bytes 3932164 | tf_op jit(solution)/shard_map/while
  39.9 33.7 %collective-permute-start = (bf16[4,4,2,5,16,132]{5,4,3,2,0,1:T(8,128)(2,1)}, bf16[4,4,2,5,16,132]{5,4,3,2,0,1:T(8,128)(2,1)}, u32[]{:S(2)}, u32[]{:S(2)}) collective-permute-start(bf16[4,4,2,5,16,132]{5,4,3,2,0,1:T(8,128)(2,1)} %copy.62), channel_id=1, source_target_pairs={{0,4},{4,8},{8,12},{12,0},{1,5},{5,9},{9,13},{13,1},{2,6},{6,10},{... | collective-permute-start | bytes 2027528 | tf_op jit(solution)/shard_map/while/body/eval_jaxpr/ppermute | solution.py:27
  50.3 1.3 copy-start
  51.6 1.0 copy-start.10
  51.6 1.1 copy-start.11
  52.6 1.3 copy-start.2
  52.6 1.7 copy-start.7
  58.2 1.1 copy-start.4
  58.2 1.3 copy-start.5
  58.2 1.5 copy-start.6
  59.6 13.9 %copy-start.3 = (f32[4,4,2,5,16,128]{5,4,3,2,0,1:T(8,128)S(1)}, f32[4,4,2,5,16,128]{5,4,3,2,0,1:T(8,128)}, u32[]{:S(2)}) copy-start(f32[4,4,2,5,16,128]{5,4,3,2,0,1:T(8,128)} %copy-done.1) | copy-start | bytes 3932164 | tf_op jit(solution)/shard_map/while
  73.6 3.0 %copy-start.1 = (f32[4,4,2,5,16,128]{5,4,3,2,0,1:T(8,128)}, f32[4,4,2,5,16,128]{5,4,3,2,0,1:T(8,128)S(1)}, u32[]{:S(2)}) copy-start(f32[4,4,2,5,16,128]{5,4,3,2,0,1:T(8,128)S(1)} %get-tuple-element.607) | copy-start | bytes 3932164 | tf_op jit(solution)/shard_map/while
  76.6 31.6 %collective-permute-start = (bf16[4,4,2,5,16,132]{5,4,3,2,0,1:T(8,128)(2,1)}, bf16[4,4,2,5,16,132]{5,4,3,2,0,1:T(8,128)(2,1)}, u32[]{:S(2)}, u32[]{:S(2)}) collective-permute-start(bf16[4,4,2,5,16,132]{5,4,3,2,0,1:T(8,128)(2,1)} %copy.62), channel_id=1, source_target_pairs={{0,4},{4,8},{8,12},{12,0},{1,5},{5,9},{9,13},{13,1},{2,6},{6,10},{... | collective-permute-start | bytes 2027528 | tf_op jit(solution)/shard_map/while/body/eval_jaxpr/ppermute | solution.py:27
  83.9 1.3 copy-start
  85.3 1.0 copy-start.10
  85.3 1.1 copy-start.11
  86.3 1.3 copy-start.2
  86.3 1.7 copy-start.7
  91.8 1.1 copy-start.4
  91.9 1.3 copy-start.5
  91.9 1.5 copy-start.6
  93.3 14.8 %copy-start.3 = (f32[4,4,2,5,16,128]{5,4,3,2,0,1:T(8,128)S(1)}, f32[4,4,2,5,16,128]{5,4,3,2,0,1:T(8,128)}, u32[]{:S(2)}) copy-start(f32[4,4,2,5,16,128]{5,4,3,2,0,1:T(8,128)} %copy-done.1) | copy-start | bytes 3932164 | tf_op jit(solution)/shard_map/while
  108.1 3.0 %copy-start.1 = (f32[4,4,2,5,16,128]{5,4,3,2,0,1:T(8,128)}, f32[4,4,2,5,16,128]{5,4,3,2,0,1:T(8,128)S(1)}, u32[]{:S(2)}) copy-start(f32[4,4,2,5,16,128]{5,4,3,2,0,1:T(8,128)S(1)} %get-tuple-element.607) | copy-start | bytes 3932164 | tf_op jit(solution)/shard_map/while
  111.2 30.6 %collective-permute-start = (bf16[4,4,2,5,16,132]{5,4,3,2,0,1:T(8,128)(2,1)}, bf16[4,4,2,5,16,132]{5,4,3,2,0,1:T(8,128)(2,1)}, u32[]{:S(2)}, u32[]{:S(2)}) collective-permute-start(bf16[4,4,2,5,16,132]{5,4,3,2,0,1:T(8,128)(2,1)} %copy.62), channel_id=1, source_target_pairs={{0,4},{4,8},{8,12},{12,0},{1,5},{5,9},{9,13},{13,1},{2,6},{6,10},{... | collective-permute-start | bytes 2027528 | tf_op jit(solution)/shard_map/while/body/eval_jaxpr/ppermute | solution.py:27
  118.5 1.3 copy-start
  119.9 1.0 copy-start.10
  119.9 1.1 copy-start.11
  120.9 1.3 copy-start.2
  120.9 1.7 copy-start.7
  126.4 1.1 copy-start.4
  126.4 1.3 copy-start.5
  126.4 1.5 copy-start.6
  127.9 13.9 %copy-start.3 = (f32[4,4,2,5,16,128]{5,4,3,2,0,1:T(8,128)S(1)}, f32[4,4,2,5,16,128]{5,4,3,2,0,1:T(8,128)}, u32[]{:S(2)}) copy-start(f32[4,4,2,5,16,128]{5,4,3,2,0,1:T(8,128)} %copy-done.1) | copy-start | bytes 3932164 | tf_op jit(solution)/shard_map/while
  145.7 1.3 copy-start.9
  147.0 1.3 copy-start.8
  149.6 0.6 copy-start.21
  149.6 0.6 copy-start.22
  149.6 0.7 copy-start.23
  149.6 0.7 copy-start.24
  150.3 1.2 copy-start.14
  150.3 1.2 copy-start.15
  150.3 1.2 copy-start.16
  150.3 1.3 copy-start.17
  150.3 1.3 copy-start.19
  150.3 1.2 copy-start.20
  154.8 11.5 %copy-start.25 = (u32[32]{0:T(128)S(1)}, u32[32]{0:T(128)}, u32[]{:S(2)}) copy-start(u32[32]{0:T(128)} %constant.132) | copy-start | bytes 388
Sparse Core Ops, SparseCore 0:
  166.4 22.8 all-reduce.5
where the time goes:
time: 199 us; the launch traced here: 198 us
  waiting for transfers between devices  58.5 us (29%)
  other arithmetic  56 us (28%)
  local copies, waits for them, and re-layouts  44.9 us (23%)
  between operations  14.4 us (7%)
  starting transfers between devices  13.3 us (7%)
  blocking collectives  10.4 us (5%)
    ppermute x3, waiting for transfers between devices, passed_along(): return lax.ppermute(value, axis, pairs)  36.7 us
    unnamed x2, waiting for transfers between devices  21.8 us
    while x63, local copies, waits for them, and re-layouts  17.8 us
    div x9, other arithmetic, stencil(): (shifted(0) - 8.0 * shifted(1) + 8.0 * shifted(3) - shifted(4)) / 12.0  12.6 us
    all_to_all x1, blocking collectives, body(): lax.all_to_all(running, 'mode', split_axis=3, concat_axis=0, tiled=True)  10.4 us
    broadcast_in_dim x18, local copies, waits for them, and re-layouts, choose(): picked = picked + jnp.where(wanted == slot_index, candidate, 0.0)  9.97 us
    add x8, other arithmetic, choose(): picked = picked + jnp.where(wanted == slot_index, candidate, 0.0)  8.58 us
    add x16, other arithmetic, conj_product(): left_real * right_real + left_imag * right_imag  8.58 us
  transfers between devices with their start and end apart: 8, of which 4 were waited for; matrix products, arithmetic and copies ran while one was open for 31% of the time, Pallas kernels for 0%

commit v1 on v0

v1 whole, which is shorter than its diff:
```python
import functools
import math

import jax
import jax.numpy as jnp
from jax import lax
from jax.experimental import pallas as pl
from jax.experimental.pallas import tpu as pltpu
from jax.sharding import PartitionSpec as P

HARMS = 8
LANES = 128
HALO = 4
VMEM_LIMIT = 48 * 1024 * 1024


def iota(shape, axis):
    return lax.broadcasted_iota(jnp.int32, shape, axis)


def one_hot(mask):
    return jnp.where(mask, 1.0, 0.0).astype(jnp.bfloat16)


def halo_offset(index, width):
    return jnp.where(index < 2, index - 2, index - 2 + width)


def pack_kernel(sizes, rad_ref, own_d, own_a, far_d, far_a, out_ref, main_m, halo_m):
    harms, blocks, groups, group_rows, width = sizes
    shift = jnp.where(rad_ref[0] == 0, LANES, -LANES)
    depth, span = harms * LANES, blocks * LANES
    row, col = iota((depth, span), 0), iota((depth, span), 1)
    harm_in, cell_in = row // LANES, row % LANES
    owner, lane = col // LANES, col % LANES
    main_m[...] = one_hot((lane // width == harm_in) & (cell_in == owner * width + lane % width))
    span_h = harms * HALO
    part = lane % span_h
    wanted = owner * width + halo_offset(part % HALO, width)
    same = (part // HALO == harm_in) & (lane < groups * span_h)
    halo_m[0:depth, :] = one_hot(same & (cell_in == wanted))
    halo_m[depth:, :] = one_hot(same & (cell_in + shift == wanted))
    lane_group = (iota((group_rows, span), 1) % LANES) // span_h
    for array, (own, far) in enumerate(((own_d, far_d), (own_a, far_a))):
        held = jnp.zeros((group_rows, span), jnp.float32)
        for group in range(groups):
            rows = slice(group * group_rows, (group + 1) * group_rows)
            near = jnp.concatenate([own[k, rows, :] for k in range(harms)], axis=1)
            both = jnp.concatenate([near] + [far[k, rows, :] for k in range(harms)], axis=1)
            main = jnp.dot(near, main_m[...], preferred_element_type=jnp.float32)
            ends = jnp.dot(both, halo_m[...], preferred_element_type=jnp.float32)
            held = jnp.where(lane_group == group, ends, held)
            for block in range(blocks):
                out_ref[block, array, rows, :] = main[
                    :, block * LANES : (block + 1) * LANES
                ].astype(jnp.bfloat16)
        tail = slice(groups * group_rows, (groups + 1) * group_rows)
        for block in range(blocks):
            out_ref[block, array, tail, :] = held[
                :, block * LANES : (block + 1) * LANES
            ].astype(jnp.bfloat16)


def coefficient(distance):
    near = jnp.where(distance == 1, 8.0, jnp.where(distance == -1, -8.0, 0.0))
    return jnp.where(distance == 2, -1.0, jnp.where(distance == -2, 1.0, near))


def triad_kernel(sizes, slots_ref, in_ref, out_ref, radial_m, axial_m, axial_v, radial_v, sums):
    harms, blocks, groups, group_rows, width, slots, fields, cells, harm_devices = sizes
    span_h = harms * HALO
    used = harms * width
    shape = (LANES, LANES)
    row, col = iota(shape, 0), iota(shape, 1)
    inside = (row // width == col // width) & (row < used) & (col < used)
    radial_m[:, 0:LANES, :] = jnp.broadcast_to(
        jnp.where(inside, coefficient(row - col), 0.0).astype(jnp.bfloat16), (groups, LANES, LANES)
    )
    for group in range(groups):
        part = row - group * span_h
        mine = (part >= 0) & (part < span_h) & (col < used) & (part // HALO == col // width)
        place = halo_offset(part % HALO, width)
        radial_m[group, LANES:, :] = jnp.where(mine, coefficient(place - col % width), 0.0).astype(
            jnp.bfloat16
        )
    square = (group_rows, group_rows)
    row, col = iota(square, 0), iota(square, 1)
    axial_m[...] = jnp.where(row // cells == col // cells, coefficient(col - row), 0.0).astype(
        jnp.bfloat16
    )

    @pl.loop(0, blocks)
    def _(block):
        for array in range(2):
            tail = in_ref[block, array, groups * group_rows :, :]
            for group in range(groups):
                here = in_ref[block, array, group * group_rows : (group + 1) * group_rows, :]
                wide = jnp.concatenate([here, tail], axis=1)
                radial_v[array, block * groups + group] = jnp.dot(
                    wide, radial_m[group], preferred_element_type=jnp.float32
                )
                axial_v[array, block * groups + group] = jnp.dot(
                    axial_m[...], here, preferred_element_type=jnp.float32
                )

    def values(array, block, slot, part, field):
        start = (slot * 2 + part) * group_rows + field * cells
        rows = pl.ds(pl.multiple_of(start, cells), cells)
        return in_ref[block, array, rows, :].astype(jnp.float32)

    @pl.loop(0, blocks * slots)
    def _(mode):
        block = mode // slots

        def add_stop(stop, running):
            adjoint_slot = slots_ref[(mode * blocks + stop) * 2]
            direct_slot = slots_ref[(mode * blocks + stop) * 2 + 1]
            source = lax.rem(block - stop + blocks, blocks)
            at_a = block * groups + adjoint_slot * 2
            at_d = source * groups + direct_slot * 2
            d1r, d1i, d2r, d2i = (
                values(0, source, direct_slot, part, field) for field in (1, 2) for part in (0, 1)
            )
            a1r, a1i, a2r, a2i = (
                values(1, block, adjoint_slot, part, field) for field in (1, 2) for part in (0, 1)
            )
            result = []
            for field in range(fields):
                rows = slice(field * cells, (field + 1) * cells)
                xar, xai = axial_v[1, at_a, rows, :], axial_v[1, at_a + 1, rows, :]
                rar, rai = radial_v[1, at_a, rows, :], radial_v[1, at_a + 1, rows, :]
                xdr, xdi = axial_v[0, at_d, rows, :], axial_v[0, at_d + 1, rows, :]
                rdr, rdi = radial_v[0, at_d, rows, :], radial_v[0, at_d + 1, rows, :]
                real = (d1r * xar + d1i * xai) + (d2r * rar + d2i * rai)
                real = real + ((xdr * a1r + xdi * a1i) + (rdr * a2r + rdi * a2i))
                imag = (d1r * xai - d1i * xar) + (d2r * rai - d2i * rar)
                imag = imag + ((xdr * a1i - xdi * a1r) + (rdr * a2i - rdi * a2r))
                old_real, old_imag = running[field]
                result.append((old_real + real, old_imag + imag))
            return tuple(result)

        zero = jnp.zeros((cells, LANES), jnp.float32)
        running = tuple((zero, zero) for _ in range(fields))
        if blocks <= 4:
            for stop in range(blocks):
                running = add_stop(stop, running)
        else:
            running = lax.fori_loop(0, blocks, add_stop, running)
        for field in range(fields):
            for part in range(2):
                sums[mode, part, field * cells : (field + 1) * cells, :] = running[field][part]

    scale = 1.0 / (12.0 * math.sqrt(8.0 * blocks * HARMS))
    per_harm = blocks // harm_devices
    own_cells = cells // blocks

    @pl.loop(0, blocks)
    def _(block):
        lane_slot = iota((group_rows, LANES), 1) // width
        for part in range(2):
            packed = jnp.zeros((group_rows, LANES), jnp.float32)
            for slot in range(slots):
                value = sums[block * slots + slot, part]
                reach = harms // 2
                while reach:
                    value = value + pltpu.roll(value, reach * width, axis=1)
                    reach //= 2
                if used < LANES and slot:
                    value = pltpu.roll(value, slot * width, axis=1)
                packed = jnp.where(lane_slot == slot, value, packed)
            packed = packed * scale
            for owner in range(blocks):
                for field in range(fields):
                    start = (part * fields + field) * own_cells
                    source = field * cells + owner * own_cells
                    out_ref[
                        owner * harm_devices + block // per_harm,
                        lax.rem(block, per_harm),
                        start : start + own_cells,
                        :,
                    ] = packed[source : source + own_cells, :]


def unpack_kernel(sizes, in_ref, out_ref):
    blocks, harm_devices, slots, width, per_harm = sizes
    rows = in_ref.shape[2]
    lane_block = iota((rows, LANES), 1) // width
    for local in range(per_harm):
        totals = []
        for block in range(blocks):
            total = in_ref[block * harm_devices, local]
            for harm in range(1, harm_devices):
                total = total + in_ref[block * harm_devices + harm, local]
            totals.append(total)
        for slot in range(slots):
            packed = jnp.zeros((rows, LANES), jnp.float32)
            for block in range(blocks):
                amount = (block - slot) * width % LANES
                moved = pltpu.roll(totals[block], amount, axis=1) if amount else totals[block]
                packed = jnp.where(lane_block == block, moved, packed)
            out_ref[local * slots + slot] = packed


def vmem(count):
    return [pl.BlockSpec(memory_space=pltpu.VMEM)] * count


def body(direct_field, adjoint_field, triad_slots):
    blocks, harm_devices = lax.axis_size("mode"), lax.axis_size("harm")
    harms, slots, _, fields, cells, radial = direct_field.shape
    width = radial // blocks
    groups, group_rows = slots * 2, fields * cells
    rows = groups * group_rows
    params = pltpu.CompilerParams(vmem_limit_bytes=VMEM_LIMIT)

    direct = direct_field.reshape(harms, rows, radial)
    adjoint = adjoint_field.reshape(harms, rows, radial)
    swap = [(0, 1), (1, 0)]
    far_direct = lax.ppermute(direct, "rad", swap)
    far_adjoint = lax.ppermute(adjoint, "rad", swap)
    slot_list = lax.all_gather(triad_slots, "mode", axis=0, tiled=True).reshape(-1)
    rad = lax.axis_index("rad").astype(jnp.int32).reshape(1)

    packed = pl.pallas_call(
        functools.partial(pack_kernel, (harms, blocks, groups, group_rows, width)),
        out_shape=jax.ShapeDtypeStruct((blocks, 2, rows + group_rows, LANES), jnp.bfloat16),
        in_specs=[pl.BlockSpec(memory_space=pltpu.SMEM)] + vmem(4),
        out_specs=vmem(1)[0],
        scratch_shapes=[
            pltpu.VMEM((harms * LANES, blocks * LANES), jnp.bfloat16),
            pltpu.VMEM((2 * harms * LANES, blocks * LANES), jnp.bfloat16),
        ],
        compiler_params=params,
    )(rad, direct, adjoint, far_direct, far_adjoint)

    slabs = lax.all_to_all(packed, "mode", split_axis=0, concat_axis=0, tiled=True)

    per_harm, own_cells = blocks // harm_devices, cells // blocks
    sizes = (harms, blocks, groups, group_rows, width, slots, fields, cells, harm_devices)
    out_rows = 2 * fields * own_cells
    parts = pl.pallas_call(
        functools.partial(triad_kernel, sizes),
        out_shape=jax.ShapeDtypeStruct(
            (blocks * harm_devices, per_harm, out_rows, LANES), jnp.float32
        ),
        in_specs=[pl.BlockSpec(memory_space=pltpu.SMEM)] + vmem(1),
        out_specs=vmem(1)[0],
        scratch_shapes=[
            pltpu.VMEM((groups, 2 * LANES, LANES), jnp.bfloat16),
            pltpu.VMEM((group_rows, group_rows), jnp.bfloat16),
            pltpu.VMEM((2, blocks * groups, group_rows, LANES), jnp.float32),
            pltpu.VMEM((2, blocks * groups, group_rows, LANES), jnp.float32),
            pltpu.VMEM((blocks * slots, 2, group_rows, LANES), jnp.float32),
        ],
        compiler_params=params,
    )(slot_list, slabs)

    owned = lax.all_to_all(parts, ("mode", "harm"), split_axis=0, concat_axis=0, tiled=True)

    result = pl.pallas_call(
        functools.partial(unpack_kernel, (blocks, harm_devices, slots, width, per_harm)),
        out_shape=jax.ShapeDtypeStruct((per_harm * slots, out_rows, LANES), jnp.float32),
        in_specs=vmem(1),
        out_specs=vmem(1)[0],
        compiler_params=params,
    )(owned)
    return result.reshape(per_harm * slots, 2, fields, own_cells, radial)


def solution(mesh):
    return jax.shard_map(
        body,
        mesh=mesh,
        in_specs=(
            P(("case", "harm"), "mode", None, None, None, "rad"),
            P(("case", "harm"), "mode", None, None, None, "rad"),
            P("mode", None, None),
        ),
        out_specs=P(("case", "harm"), None, None, "mode", "rad"),
        check_vma=False,
    )
```

time: 199 us -> 81.4 us (0.41)
  other arithmetic: 56 us -> 0 us
  waiting for transfers between devices: 58.5 us -> 2.82 us
  blocking collectives: 10.4 us -> 54 us
  local copies, waits for them, and re-layouts: 44.9 us -> 2.53 us
  Pallas kernels: 0 us -> 14.8 us
  between operations: 14.4 us -> 0.03 us
  starting transfers between devices: 13.3 us -> 6.88 us
    all_gather x0 -> x1, blocking collectives: none -> 40.6 us  [body(): lax.all_gather(triad_slots, 'mode', axis=0, tiled=True).reshape(-1)]
    ppermute x7 -> x2, waiting for transfers between devices: 36.7 us -> 2.81 us  [the longest x1 1.88 us: body(): far_direct = lax.ppermute(direct, 'rad', swap)]
    add x28 -> x0, other arithmetic: 22.6 us -> none  [the longest x8 8.58 us: choose(): picked = picked + jnp.where(wanted == slot_index, candidate, 0.0)]
    unnamed x2 -> x0, waiting for transfers between devices: 21.8 us -> none
    while x63 -> x0, local copies, waits for them, and re-layouts: 17.8 us -> none
    pallas_call x0 -> x3, Pallas kernels: none -> 14.8 us  [the longest x1 8.06 us: body(): pl.pallas_call(functools.partial(triad_kernel, sizes), out_shape=jax.Shap...]
    convert_element_type x9 -> x0, other arithmetic: 13.7 us -> none  [the longest x4 6.67 us: add_stop(): direct_radial = stencil(visiting.astype(jnp.float32), 5, radial_cells)]
    ppermute x7 -> x2, starting transfers between devices: 13.3 us -> 0.51 us  [the longest x1 0.45 us: body(): far_direct = lax.ppermute(direct, 'rad', swap)]
  transfers between devices with their start and end apart: 8 -> 3, of which waited for: 4 -> 2; matrix products, arithmetic and copies ran while one was open for 31% -> 0% of each run, Pallas kernels for 0% -> 0%
where the time goes in v1:
time: 81.4 us; the launch traced here: 81 us
  blocking collectives  54 us (66%)
  Pallas kernels  14.8 us (18%)
  starting transfers between devices  6.88 us (8%)
  waiting for transfers between devices  2.82 us (3%)
  local copies, waits for them, and re-layouts  2.53 us (3%)
    all_gather x1, blocking collectives, body(): lax.all_gather(triad_slots, 'mode', axis=0, tiled=True).reshape(-1)  40.6 us
    all_to_all x1, blocking collectives, body(): lax.all_to_all(parts, ('mode', 'harm'), split_axis=0, concat_axis=0, tile...  13.4 us
    pallas_call x1, Pallas kernels, body(): pl.pallas_call(functools.partial(triad_kernel, sizes), out_shape=jax.Shap...  8.06 us
    all_to_all x1, starting transfers between devices, body(): lax.all_to_all(packed, 'mode', split_axis=0, concat_axis=0, tiled=True)  6.37 us
    pallas_call x1, Pallas kernels, body(): pl.pallas_call(functools.partial(pack_kernel, (harms, blocks, groups, gro...  5.92 us
    unnamed x6, local copies, waits for them, and re-layouts  2.18 us
    ppermute x1, waiting for transfers between devices, body(): far_direct = lax.ppermute(direct, 'rad', swap)  1.88 us
  transfers between devices with their start and end apart: 3, of which 2 were waited for; matrix products, arithmetic and copies ran while one was open for 0% of the time, Pallas kernels for 0%

profile of v1, /device:TPU:0, one launch (start us, length us, event | category | flops | bytes accessed | tf_op | source)
XLA Modules:
  0.0 81.0 jit_solution(9896316026515547950)
XLA Ops:
  0.0 0.5 collective-permute-start
  0.5 0.1 collective-permute-start.1
  0.5 1.9 %collective-permute-done.far_d = bf16[4,640,128]{2,1,0:T(8,128)(2,1)S(1)} collective-permute-done((bf16[4,640,128]{2,1,0:T(8,128)(2,1)}, bf16[4,640,128]{2,1,0:T(8,128)(2,1)S(1)}, u32[]{:S(2)}, u32[]{:S(2)}) %collective-permute-start) | collective-permute-done | bytes 655392 | tf_op jit(solution)/shard_map/ppermute | solution.py:219
  2.4 0.9 %collective-permute-done.1.far_a = bf16[4,640,128]{2,1,0:T(8,128)(2,1)S(1)} collective-permute-done((bf16[4,640,128]{2,1,0:T(8,128)(2,1)}, bf16[4,640,128]{2,1,0:T(8,128)(2,1)S(1)}, u32[]{:S(2)}, u32[]{:S(2)}) %collective-permute-start.1) | collective-permute-done | bytes 655392 | tf_op jit(solution)/shard_map/ppermute | solution.py:220
  3.3 0.0 copy-start
  3.3 1.1 %copy-done = bf16[4,4,2,5,16,128]{5,4,3,2,1,0:T(8,128)(2,1)S(1)} copy-done((bf16[4,4,2,5,16,128]{5,4,3,2,1,0:T(8,128)(2,1)S(1)}, bf16[4,4,2,5,16,128]{5,4,3,2,1,0:T(8,128)(2,1)}, u32[]{:S(2)}) %copy-start) | copy-done | bytes 655384
  4.4 0.0 copy-start.1
  4.4 1.1 %copy-done.1 = bf16[4,4,2,5,16,128]{5,4,3,2,1,0:T(8,128)(2,1)S(1)} copy-done((bf16[4,4,2,5,16,128]{5,4,3,2,1,0:T(8,128)(2,1)S(1)}, bf16[4,4,2,5,16,128]{5,4,3,2,1,0:T(8,128)(2,1)}, u32[]{:S(2)}) %copy-start.1) | copy-done | bytes 655384
  5.5 5.9 %shard_map.37 = bf16[4,2,720,128]{3,2,1,0:T(8,128)(2,1)} custom-call(s32[1]{0:T(128)} %bitcast.rad_ref, bf16[4,640,128]{2,1,0:T(8,128)(2,1)S(1)} %bitcast.5, bf16[4,640,128]{2,1,0:T(8,128)(2,1)S(1)} %bitcast.7, bf16[4,640,128]{2,1,0:T(8,128)(2,1)S(1)} %collective-permute-done.far_d, bf16[4,640,128]{2,1,0:T(8,128)(2,1)S(1)} %collective-permute-done.1.far_a), custom_call_target="tpu_custom_call" | custom-call | tf_op jit(solution)/shard_map/pallas_call | solution.py:224
  11.4 0.0 copy-start.2
  11.4 6.4 %all-to-all-start = ((bf16[4,2,720,128]{3,2,1,0:T(8,128)(2,1)}), bf16[4,2,720,128]{3,2,1,0:T(8,128)(2,1)S(1)}, u32[]{:S(2)}, u32[]{:S(2)}) async-start(bf16[4,2,720,128]{3,2,1,0:T(8,128)(2,1)} %shard_map.37), calls=%async_computation | async-start | bytes 2949120 | tf_op jit(solution)/shard_map/all_to_all | solution.py:236
  17.8 0.0 copy-done.2
  17.8 40.6 %all_gather.3 = s32[16,4,2]{1,2,0:T(2,128)S(1)} all-gather(s32[4,4,2]{1,2,0:T(2,128)S(1)} %copy-done.2), channel_id=1, replica_groups=mesh['case'=2,'mode'=4,'harm'=2,'rad'=2] {'mode'}, dimensions={0}, use_global_device_ids=true | all-gather | bytes 640 | tf_op jit(solution)/shard_map/all_gather | solution.py:221
  58.4 0.2 copy.6
  58.6 0.1 reshape.15.slots_ref
  58.7 0.0 all-to-all-done.in_ref
  58.7 8.1 %shard_map.38 = f32[8,2,40,128]{3,2,1,0:T(8,128)S(1)} custom-call(s32[128]{0:T(128)S(1)} %reshape.15.slots_ref, bf16[4,2,720,128]{3,2,1,0:T(8,128)(2,1)S(1)} %all-to-all-done.in_ref), custom_call_target="tpu_custom_call" | custom-call | tf_op jit(solution)/shard_map/pallas_call | solution.py:241
  66.8 13.4 %all_to_all.10.in_ref = f32[8,2,40,128]{3,2,1,0:T(8,128)S(1)} all-to-all(f32[8,2,40,128]{3,2,1,0:T(8,128)S(1)} %shard_map.38), channel_id=1, replica_groups=mesh['case'=2,'mode'=4,'harm'=2,'rad'=2] {'mode','harm'}, dimensions={0} | all-to-all | bytes 655360 | tf_op jit(solution)/shard_map/all_to_all | solution.py:258
  80.2 0.9 %shard_map.39 = f32[8,40,128]{2,1,0:T(8,128)} custom-call(f32[8,2,40,128]{3,2,1,0:T(8,128)S(1)} %all_to_all.10.in_ref), custom_call_target="tpu_custom_call" | custom-call | tf_op jit(solution)/shard_map/pallas_call | solution.py:260
Async XLA Ops:
  0.0 2.4 %collective-permute-start = (bf16[4,640,128]{2,1,0:T(8,128)(2,1)}, bf16[4,640,128]{2,1,0:T(8,128)(2,1)S(1)}, u32[]{:S(2)}, u32[]{:S(2)}) collective-permute-start(bf16[4,640,128]{2,1,0:T(8,128)(2,1)} %bitcast.4), channel_id=1, source_target_pairs={{0,1},{1,0},{2,3},{3,2},{4,5},{5,4},{6,7},{7,6},{8,9},{9,8},{10,11... | collective-permute-start | bytes 1966088 | tf_op jit(solution)/shard_map/ppermute | solution.py:219
  0.5 2.9 %collective-permute-start.1 = (bf16[4,640,128]{2,1,0:T(8,128)(2,1)}, bf16[4,640,128]{2,1,0:T(8,128)(2,1)S(1)}, u32[]{:S(2)}, u32[]{:S(2)}) collective-permute-start(bf16[4,640,128]{2,1,0:T(8,128)(2,1)} %bitcast.6), channel_id=1, source_target_pairs={{0,1},{1,0},{2,3},{3,2},{4,5},{5,4},{6,7},{7,6},{8,9},{9,8},{10,11... | collective-permute-start | bytes 1966088 | tf_op jit(solution)/shard_map/ppermute | solution.py:220
  3.3 1.1 %copy-start = (bf16[4,4,2,5,16,128]{5,4,3,2,1,0:T(8,128)(2,1)S(1)}, bf16[4,4,2,5,16,128]{5,4,3,2,1,0:T(8,128)(2,1)}, u32[]{:S(2)}) copy-start(bf16[4,4,2,5,16,128]{5,4,3,2,1,0:T(8,128)(2,1)} %param.3) | copy-start | bytes 1966084
  4.4 1.1 %copy-start.1 = (bf16[4,4,2,5,16,128]{5,4,3,2,1,0:T(8,128)(2,1)S(1)}, bf16[4,4,2,5,16,128]{5,4,3,2,1,0:T(8,128)(2,1)}, u32[]{:S(2)}) copy-start(bf16[4,4,2,5,16,128]{5,4,3,2,1,0:T(8,128)(2,1)} %param.4) | copy-start | bytes 1966084
  11.4 6.4 %copy-start.2 = (s32[4,4,2]{1,2,0:T(2,128)S(1)}, s32[4,4,2]{1,2,0:T(2,128)}, u32[]{:S(2)}) copy-start(s32[4,4,2]{1,2,0:T(2,128)} %param.5) | copy-start | bytes 388
  11.4 47.3 %all-to-all-start = ((bf16[4,2,720,128]{3,2,1,0:T(8,128)(2,1)}), bf16[4,2,720,128]{3,2,1,0:T(8,128)(2,1)S(1)}, u32[]{:S(2)}, u32[]{:S(2)}) async-start(bf16[4,2,720,128]{3,2,1,0:T(8,128)(2,1)} %shard_map.37), calls=%async_computation | async-start | bytes 2949120 | tf_op jit(solution)/shard_map/all_to_all | solution.py:236

commit v2 on v1

v2 whole, which is shorter than its diff:
```python
import functools
import math

import jax
import jax.numpy as jnp
from jax import lax
from jax.experimental import pallas as pl
from jax.experimental.pallas import tpu as pltpu
from jax.sharding import PartitionSpec as P

HARMS = 8
LANES = 128
HALO = 4
GROUPS = ((1, 2), (0, 3), (4,))
VMEM_LIMIT = 40 * 1024 * 1024


def iota(shape, axis):
    return lax.broadcasted_iota(jnp.int32, shape, axis)


def one_hot(mask):
    return jnp.where(mask, 1.0, 0.0).astype(jnp.bfloat16)


def halo_offset(index, width):
    return jnp.where(index < 2, index - 2, index - 2 + width)


def wrapped(index, count):
    return jnp.where(index >= count, index - count, index)


def columns(harms, blocks, mode):
    shape = (harms * LANES, blocks * LANES)
    row, col = iota(shape, 0), iota(shape, 1)
    owner = wrapped(col // LANES + mode, blocks)
    return row // LANES, row % LANES, owner, col % LANES


def side_by_side(ref, group, rows):
    return jnp.concatenate([ref[k, group, rows, :] for k in range(ref.shape[0])], axis=1)


def fill_main(matrix, sizes, mode):
    harms, blocks, width = sizes
    harm_in, cell_in, owner, lane = columns(harms, blocks, mode)
    matrix[...] = one_hot(
        (lane // width == harm_in) & (cell_in == owner * width + lane % width)
    )


def write_main(arrays, fields, cells, matrix, outs):
    groups = arrays[0].shape[1]
    pieces = []
    for array in arrays:
        for field in fields:
            rows = slice(field * cells, (field + 1) * cells)
            pieces += [side_by_side(array, group, rows) for group in range(groups)]
    main = jnp.dot(
        jnp.concatenate(pieces, axis=0), matrix[...], preferred_element_type=jnp.float32
    )
    for step, out in enumerate(outs):
        out[...] = main[:, step * LANES : (step + 1) * LANES].astype(jnp.bfloat16)


def first_pack_kernel(sizes, cells, where, *refs):
    blocks = sizes[1]
    fields = len(GROUPS[0])
    ins, outs, matrix = refs[: 2 * fields], refs[2 * fields : -1], refs[-1]
    fill_main(matrix, sizes, where[0])
    groups = ins[0].shape[1]
    pieces = [
        side_by_side(ref, group, slice(0, cells)) for ref in ins for group in range(groups)
    ]
    main = jnp.dot(
        jnp.concatenate(pieces, axis=0), matrix[...], preferred_element_type=jnp.float32
    )
    for step in range(blocks):
        outs[step][...] = main[:, step * LANES : (step + 1) * LANES].astype(jnp.bfloat16)


def second_pack_kernel(sizes, cells, where, own_d, own_a, far_d, far_a, *refs):
    harms, blocks, width = sizes
    outs, main_m, halo_m = refs[:-2], refs[-2], refs[-1]
    groups, group_rows = own_d.shape[1], own_d.shape[2]
    mode = where[0]
    shift = jnp.where(where[2] == 0, LANES, -LANES)
    depth = harms * LANES
    span_h = harms * HALO
    harm_in, cell_in, owner, lane = columns(harms, blocks, mode)
    part = lane % span_h
    wanted = owner * width + halo_offset(part % HALO, width)
    same = (part // HALO == harm_in) & (lane < groups * span_h)
    halo_m[0:depth, :] = one_hot(same & (cell_in == wanted))
    halo_m[depth:, :] = one_hot(same & (cell_in + shift == wanted))
    lane_group = (iota((group_rows, blocks * LANES), 1) % LANES) // span_h
    everything = slice(0, group_rows)
    for array, (own, far) in enumerate(((own_d, far_d), (own_a, far_a))):
        pieces = [
            jnp.concatenate(
                [side_by_side(own, group, everything), side_by_side(far, group, everything)], axis=1
            )
            for group in range(groups)
        ]
        ends = jnp.dot(
            jnp.concatenate(pieces, axis=0), halo_m[...], preferred_element_type=jnp.float32
        )
        held = jnp.zeros((group_rows, blocks * LANES), jnp.float32)
        for group in range(groups):
            held = jnp.where(
                lane_group == group, ends[group * group_rows : (group + 1) * group_rows], held
            )
        for step in range(blocks):
            outs[step][array * group_rows : (array + 1) * group_rows, :] = held[
                :, step * LANES : (step + 1) * LANES
            ].astype(jnp.bfloat16)
    fill_main(main_m, sizes, mode)
    for index, fields in enumerate(GROUPS[1:], start=1):
        write_main(
            (own_d, own_a), fields, cells, main_m, outs[index * blocks : (index + 1) * blocks]
        )


def coefficient(distance):
    near = jnp.where(distance == 1, 8.0, jnp.where(distance == -1, -8.0, 0.0))
    return jnp.where(distance == 2, -1.0, jnp.where(distance == -2, 1.0, near))


def triad_kernel(sizes, fields, where, slots_ref, *refs):
    harms, blocks, width, groups, slots, all_fields, cells, harm_devices = sizes
    first = fields == GROUPS[0]
    lead = refs[:blocks]
    mains = lead if first else refs[blocks : 2 * blocks]
    at = blocks if first else 2 * blocks
    halos = refs[at : at + blocks]
    outs = refs[at + blocks : at + blocks + blocks * harm_devices]
    radial_m, axial_m, plain_v, axial_v, radial_v, sums, staged = refs[
        at + blocks + blocks * harm_devices :
    ]
    count = len(fields)
    span_h = harms * HALO
    used = harms * width
    tile = groups * cells
    shape = (LANES, LANES)
    row, col = iota(shape, 0), iota(shape, 1)
    inside = (row // width == col // width) & (row < used) & (col < used)
    within = jnp.where(inside, coefficient(row - col), 0.0).astype(jnp.bfloat16)
    square = (tile, tile)
    row_t, col_t = iota(square, 0), iota(square, 1)
    axial_m[...] = jnp.where(
        row_t // cells == col_t // cells, coefficient(col_t - row_t), 0.0
    ).astype(jnp.bfloat16)

    for group in range(groups):
        part = row - group * span_h
        mine = (part >= 0) & (part < span_h) & (col < used) & (part // HALO == col // width)
        place = halo_offset(part % HALO, width)
        around = jnp.where(mine, coefficient(place - col % width), 0.0).astype(jnp.bfloat16)
        radial_m[group] = jnp.concatenate([within, around], axis=0)
    for group in range(groups):
        pieces = []
        for array in range(2):
            for local, field in enumerate(fields):
                for step in range(blocks):
                    start = ((array * count + local) * groups + group) * cells
                    beside = (array * all_fields + field) * cells
                    pieces.append(
                        jnp.concatenate(
                            [
                                mains[step][start : start + cells, :],
                                halos[step][beside : beside + cells, :],
                            ],
                            axis=1,
                        )
                    )
        slopes = jnp.dot(
            jnp.concatenate(pieces, axis=0), radial_m[group], preferred_element_type=jnp.float32
        )
        index = 0
        for array in range(2):
            for local in range(count):
                for step in range(blocks):
                    radial_v[array * count + local, step * groups + group] = slopes[
                        index * cells : (index + 1) * cells, :
                    ]
                    index += 1
    for step in range(blocks):
        for local in range(count):
            starts = [(array * count + local) * tile for array in range(2)]
            both = jnp.concatenate([mains[step][s : s + tile, :] for s in starts], axis=1)
            slopes = jnp.dot(axial_m[...], both, preferred_element_type=jnp.float32)
            for array in range(2):
                for group in range(groups):
                    axial_v[array * count + local, step * groups + group] = slopes[
                        group * cells : (group + 1) * cells, array * LANES : (array + 1) * LANES
                    ]
        for which in range(4):
            for group in range(groups):
                start = (which * groups + group) * cells
                plain_v[which, step * groups + group] = lead[step][
                    start : start + cells, :
                ].astype(jnp.float32)

    @pl.loop(0, blocks * slots)
    def _(index):
        step = index // slots

        def add_stop(stop, running):
            source = wrapped(step + stop, blocks)
            at_a = step * groups + slots_ref[(index * blocks + stop) * 2] * 2
            at_d = source * groups + slots_ref[(index * blocks + stop) * 2 + 1] * 2
            d1r, d1i, d2r, d2i = (plain_v[w, at_d + c] for w in (0, 1) for c in (0, 1))
            a1r, a1i, a2r, a2i = (plain_v[w, at_a + c] for w in (2, 3) for c in (0, 1))
            result = []
            for local in range(count):
                xar, xai = axial_v[count + local, at_a], axial_v[count + local, at_a + 1]
                rar, rai = radial_v[count + local, at_a], radial_v[count + local, at_a + 1]
                xdr, xdi = axial_v[local, at_d], axial_v[local, at_d + 1]
                rdr, rdi = radial_v[local, at_d], radial_v[local, at_d + 1]
                real = (d1r * xar + d1i * xai) + (d2r * rar + d2i * rai)
                real = real + ((xdr * a1r + xdi * a1i) + (rdr * a2r + rdi * a2i))
                imag = (d1r * xai - d1i * xar) + (d2r * rai - d2i * rar)
                imag = imag + ((xdr * a1i - xdi * a1r) + (rdr * a2i - rdi * a2r))
                old_real, old_imag = running[local]
                result.append((old_real + real, old_imag + imag))
            return tuple(result)

        zero = jnp.zeros((cells, LANES), jnp.float32)
        running = tuple((zero, zero) for _ in range(count))
        if blocks <= 4:
            for stop in range(blocks):
                running = add_stop(stop, running)
        else:
            running = lax.fori_loop(0, blocks, add_stop, running)
        for local in range(count):
            for part in range(2):
                sums[index, part * count + local] = running[local][part]

    scale = 1.0 / (12.0 * math.sqrt(8.0 * blocks * HARMS))
    per_harm = blocks // harm_devices
    own_cells = cells // blocks
    lane_slot = iota((cells, LANES), 1) // width

    @pl.loop(0, blocks)
    def _(step):
        block = wrapped(where[0] - step + blocks, blocks)
        for row in range(2 * count):
            packed = jnp.zeros((cells, LANES), jnp.float32)
            for slot in range(slots):
                value = sums[step * slots + slot, row]
                reach = harms // 2
                while reach:
                    value = value + pltpu.roll(value, reach * width, axis=1)
                    reach //= 2
                if used < LANES and slot:
                    value = pltpu.roll(value, slot * width, axis=1)
                packed = jnp.where(lane_slot == slot, value, packed)
            packed = packed * scale
            for owner in range(blocks):
                staged[owner, block, row * own_cells : (row + 1) * own_cells, :] = packed[
                    owner * own_cells : (owner + 1) * own_cells, :
                ]

    for step in range(blocks):
        owner = wrapped(where[0] + step, blocks)
        for turn in range(harm_devices):
            harm = wrapped(where[1] + turn, harm_devices)
            for local in range(per_harm):
                outs[step * harm_devices + turn][local] = staged[owner, harm * per_harm + local]


def unpack_kernel(sizes, where, *refs):
    blocks, harm_devices, slots, width, per_harm, own_cells, all_fields = sizes
    ins, out_ref = refs[:-1], refs[-1]
    peers = blocks * harm_devices
    for index, fields in enumerate(GROUPS):
        count = len(fields)
        rows = 2 * count * own_cells
        lane_block = iota((rows, LANES), 1) // width
        for local in range(per_harm):
            packed = [jnp.zeros((rows, LANES), jnp.float32) for _ in range(slots)]
            for step in range(blocks):
                source = wrapped(where[0] - step + blocks, blocks)
                total = ins[index * peers + step * harm_devices][local]
                for turn in range(1, harm_devices):
                    total = total + ins[index * peers + step * harm_devices + turn][local]
                for slot in range(slots):
                    amount = lax.rem((source - slot + blocks) * width, LANES)
                    moved = pltpu.roll(total, amount, axis=1)
                    packed[slot] = jnp.where(lane_block == source, moved, packed[slot])
            for slot in range(slots):
                for part in range(2):
                    for at, field in enumerate(fields):
                        start = (part * count + at) * own_cells
                        target = (part * all_fields + field) * own_cells
                        out_ref[local * slots + slot, target : target + own_cells, :] = packed[
                            slot
                        ][start : start + own_cells, :]


def smem(count):
    return [pl.BlockSpec(memory_space=pltpu.SMEM)] * count


def vmem(count):
    return [pl.BlockSpec(memory_space=pltpu.VMEM)] * count


def moved_up(values, axis):
    count = lax.axis_size(axis)
    result = [values[0]]
    for step in range(1, count):
        pairs = [(source, (source + step) % count) for source in range(count)]
        result.append(lax.ppermute(values[step], axis, pairs))
    return result


def to_owners(parts, mode, harm):
    modes, harms = lax.axis_size("mode"), lax.axis_size("harm")
    if modes * harms > 8:
        stacked = jnp.stack(parts).reshape((modes, harms) + parts[0].shape)
        stacked = jnp.roll(stacked, (mode, harm), axis=(0, 1)).reshape((-1,) + parts[0].shape)
        came = lax.all_to_all(stacked, ("mode", "harm"), split_axis=0, concat_axis=0, tiled=True)
        came = came.reshape((modes, harms) + parts[0].shape)
        came = jnp.take(came, (mode - jnp.arange(modes)) % modes, axis=0)
        came = jnp.take(came, (harm - jnp.arange(harms)) % harms, axis=1)
        return [came[step, turn] for step in range(modes) for turn in range(harms)]
    result = [parts[0]]
    for index in range(1, modes * harms):
        step, turn = divmod(index, harms)
        pairs = [
            (z * harms + h, (z + step) % modes * harms + (h + turn) % harms)
            for z in range(modes)
            for h in range(harms)
        ]
        result.append(lax.ppermute(parts[index], ("mode", "harm"), pairs))
    return result


def body(direct_field, adjoint_field, triad_slots):
    blocks, harm_devices = lax.axis_size("mode"), lax.axis_size("harm")
    harms, slots, parts, fields, cells, radial = direct_field.shape
    width = radial // blocks
    groups, group_rows = slots * parts, fields * cells
    tile = groups * cells
    params = pltpu.CompilerParams(vmem_limit_bytes=VMEM_LIMIT)
    mode, harm, rad = (lax.axis_index(axis).astype(jnp.int32) for axis in ("mode", "harm", "rad"))
    where = jnp.stack([mode, harm, rad])

    direct = direct_field.reshape(harms, groups, group_rows, radial)
    adjoint = adjoint_field.reshape(harms, groups, group_rows, radial)
    swap = [(0, 1), (1, 0)]
    far_direct = lax.ppermute(direct, "rad", swap)
    far_adjoint = lax.ppermute(adjoint, "rad", swap)

    def payload(rows):
        return [jax.ShapeDtypeStruct((rows, LANES), jnp.bfloat16)] * blocks

    def one_field(field):
        return pl.BlockSpec((harms, groups, cells, radial), lambda i: (0, 0, field, 0))

    sizes = (harms, blocks, width)
    main_matrix = pltpu.VMEM((harms * LANES, blocks * LANES), jnp.bfloat16)
    lead = pl.pallas_call(
        functools.partial(first_pack_kernel, sizes, cells),
        grid=(1,),
        out_shape=payload(2 * len(GROUPS[0]) * tile),
        in_specs=smem(1) + [one_field(field) for field in GROUPS[0]] * 2,
        out_specs=vmem(blocks),
        scratch_shapes=[main_matrix],
        compiler_params=params,
        name="pack_first",
    )(where, *[direct] * len(GROUPS[0]), *[adjoint] * len(GROUPS[0]))
    lead = moved_up(lead, "mode")

    shapes = payload(2 * group_rows)
    for group in GROUPS[1:]:
        shapes = shapes + payload(2 * len(group) * tile)
    packed = pl.pallas_call(
        functools.partial(second_pack_kernel, sizes, cells),
        out_shape=shapes,
        in_specs=smem(1) + vmem(4),
        out_specs=vmem(len(shapes)),
        scratch_shapes=[
            main_matrix,
            pltpu.VMEM((2 * harms * LANES, blocks * LANES), jnp.bfloat16),
        ],
        compiler_params=params,
        name="pack_rest",
    )(where, direct, adjoint, far_direct, far_adjoint)
    halos = moved_up(packed[:blocks], "mode")
    mains = [lead]
    for index in range(1, len(GROUPS)):
        mains.append(moved_up(packed[index * blocks : (index + 1) * blocks], "mode"))
    own_slots = triad_slots.reshape(-1)
    slot_list = jnp.concatenate(moved_up([own_slots] * blocks, "mode"))

    per_harm, own_cells = blocks // harm_devices, cells // blocks
    sizes = (harms, blocks, width, groups, slots, fields, cells, harm_devices)
    owned = []
    for index, group in enumerate(GROUPS):
        count = len(group)
        operands = mains[0] + (mains[index] if index else []) + halos
        derived = pltpu.VMEM((2 * count, blocks * groups, cells, LANES), jnp.float32)
        chunk = jax.ShapeDtypeStruct((per_harm, 2 * count * own_cells, LANES), jnp.float32)
        sent = pl.pallas_call(
            functools.partial(triad_kernel, sizes, group),
            out_shape=[chunk] * (blocks * harm_devices),
            in_specs=smem(2) + vmem(len(operands)),
            out_specs=vmem(blocks * harm_devices),
            scratch_shapes=[
                pltpu.VMEM((groups, 2 * LANES, LANES), jnp.bfloat16),
                pltpu.VMEM((tile, tile), jnp.bfloat16),
                pltpu.VMEM((4, blocks * groups, cells, LANES), jnp.float32),
                derived,
                derived,
                pltpu.VMEM((blocks * slots, 2 * count, cells, LANES), jnp.float32),
                pltpu.VMEM((blocks, blocks, 2 * count * own_cells, LANES), jnp.float32),
            ],
            compiler_params=params,
            name="triads",
        )(where, slot_list, *operands)
        owned += to_owners(sent, mode, harm)

    sizes = (blocks, harm_devices, slots, width, per_harm, own_cells, fields)
    result = pl.pallas_call(
        functools.partial(unpack_kernel, sizes),
        out_shape=jax.ShapeDtypeStruct(
            (per_harm * slots, 2 * fields * own_cells, LANES), jnp.float32
        ),
        in_specs=smem(1) + vmem(len(owned)),
        out_specs=vmem(1)[0],
        compiler_params=params,
        name="unpack",
    )(where, *owned)
    return result.reshape(per_harm * slots, 2, fields, own_cells, radial)


def solution(mesh):
    return jax.shard_map(
        body,
        mesh=mesh,
        in_specs=(
            P(("case", "harm"), "mode", None, None, None, "rad"),
            P(("case", "harm"), "mode", None, None, None, "rad"),
            P("mode", None, None),
        ),
        out_specs=P(("case", "harm"), None, None, "mode", "rad"),
        check_vma=False,
    )
```

time: 81.4 us -> 99.8 us (1.23)
  blocking collectives: 54 us -> 0 us
  starting transfers between devices: 6.88 us -> 52.1 us
  waiting for transfers between devices: 2.82 us -> 30.6 us
    ppermute x0 -> x36, starting transfers between devices: none -> 51.6 us  [the longest x21 33.3 us: to_owners(): result.append(lax.ppermute(parts[index], ('mode', 'harm'), pairs))]
    all_gather x1 -> x0, blocking collectives: 40.6 us -> none  [body(): lax.all_gather(triad_slots, 'mode', axis=0, tiled=True).reshape(-1)]
    ppermute x0 -> x36, waiting for transfers between devices: none -> 30.6 us  [the longest x21 16.2 us: to_owners(): result.append(lax.ppermute(parts[index], ('mode', 'harm'), pairs))]
    all_to_all x1 -> x0, blocking collectives: 13.4 us -> none  [body(): lax.all_to_all(parts, ('mode', 'harm'), split_axis=0, concat_axis=0, tile...]
    all_to_all x1 -> x0, starting transfers between devices: 6.37 us -> none  [body(): lax.all_to_all(packed, 'mode', split_axis=0, concat_axis=0, tiled=True)]
    ppermute x1, waiting for transfers between devices: 1.88 us -> 0.01 us  [body(): far_direct = lax.ppermute(direct, 'rad', swap)]
    pallas_call x3 -> x6, Pallas kernels: 14.8 us -> 14.2 us  [the longest x3 9.12 us: body(): pl.pallas_call(functools.partial(triad_kernel, sizes, group), out_shape=[...]
    unnamed x6 -> x11, local copies, waits for them, and re-layouts: 2.18 us -> 2.3 us
  transfers between devices with their start and end apart: 3 -> 38, of which waited for: 2 -> 11; matrix products, arithmetic and copies ran while one was open for 0% -> 0% of each run, Pallas kernels for 0% -> 9%
where the time goes in v2:
time: 99.8 us; the launch traced here: 99.6 us
  starting transfers between devices  52.1 us (52%)
  waiting for transfers between devices  30.6 us (31%)
  Pallas kernels  14.2 us (14%)
  local copies, waits for them, and re-layouts  2.39 us (2%)
    ppermute x21, starting transfers between devices, to_owners(): result.append(lax.ppermute(parts[index], ('mode', 'harm'), pairs))  33.3 us
    ppermute x15, starting transfers between devices, moved_up(): result.append(lax.ppermute(values[step], axis, pairs))  18.3 us
    ppermute x21, waiting for transfers between devices, to_owners(): result.append(lax.ppermute(parts[index], ('mode', 'harm'), pairs))  16.2 us
    ppermute x15, waiting for transfers between devices, moved_up(): result.append(lax.ppermute(values[step], axis, pairs))  14.4 us
    pallas_call x3, Pallas kernels, body(): pl.pallas_call(functools.partial(triad_kernel, sizes, group), out_shape=[...  9.12 us
    pallas_call x1, Pallas kernels, body(): pl.pallas_call(functools.partial(second_pack_kernel, sizes, cells), out_s...  2.59 us
    unnamed x11, local copies, waits for them, and re-layouts  2.3 us
  transfers between devices with their start and end apart: 38, of which 11 were waited for; matrix products, arithmetic and copies ran while one was open for 0% of the time, Pallas kernels for 9%

profile of v2, /device:TPU:0, one launch (start us, length us, event | category | flops | bytes accessed | tf_op | source)
XLA Modules:
  0.0 99.6 jit_solution(3162393256933252025)
XLA Ops:
  0.0 0.5 collective-permute-start.6
  0.5 0.1 collective-permute-start.7
  0.5 0.1 pad_add_fusion.where
  0.6 1.1 %copy-done = bf16[4,4,2,5,16,128]{5,4,3,2,1,0:T(8,128)(2,1)S(1)} copy-done((bf16[4,4,2,5,16,128]{5,4,3,2,1,0:T(8,128)(2,1)S(1)}, bf16[4,4,2,5,16,128]{5,4,3,2,1,0:T(8,128)(2,1)}, u32[]{:S(2)}) %copy-start) | copy-done | bytes 655384
  1.7 1.1 %copy-done.2 = bf16[4,4,2,5,16,128]{5,4,3,2,1,0:T(8,128)(2,1)S(1)} copy-done((bf16[4,4,2,5,16,128]{5,4,3,2,1,0:T(8,128)(2,1)S(1)}, bf16[4,4,2,5,16,128]{5,4,3,2,1,0:T(8,128)(2,1)}, u32[]{:S(2)}) %copy-start.2) | copy-done | bytes 655384
  2.8 1.0 %pack_first.1 = (bf16[512,128]{1,0:T(8,128)(2,1)S(1)}, bf16[512,128]{1,0:T(8,128)(2,1)S(1)}, bf16[512,128]{1,0:T(8,128)(2,1)S(1)}, bf16[512,128]{1,0:T(8,128)(2,1)S(1)}) custom-call(s32[3]{0:T(128)S(1)} %pad_add_fusion.where, bf16[4,8,80,128]{3,2,1,0:T(8,128)(2,1)S(1)} %bitcast.7, bf16[4,8,80,128]{3,2,1,0:T(8,128)(2,1)S(1)} %bitcast.8, ...), custom_call_target="tpu_custom_call" | custom-call | tf_op jit(solution)/shard_map/pack_first/pallas_call | solution.py:365
  3.8 0.0 copy-start.4
  3.8 3.1 %collective-permute-start.3 = (bf16[512,128]{1,0:T(8,128)(2,1)S(1)}, bf16[512,128]{1,0:T(8,128)(2,1)S(1)}, u32[]{:S(2)}, u32[]{:S(2)}) collective-permute-start(bf16[512,128]{1,0:T(8,128)(2,1)S(1)} %get-tuple-element.46), channel_id=1, source_target_pairs={{0,4},{4,8},{8,12},{12,0},{1,5},{5,9},{9,13},{13,1},{2,6},{6,10},{... | collective-permute-start | bytes 393224 | tf_op jit(solution)/shard_map/ppermute | solution.py:315
  6.9 2.6 %collective-permute-start.4 = (bf16[512,128]{1,0:T(8,128)(2,1)S(1)}, bf16[512,128]{1,0:T(8,128)(2,1)S(1)}, u32[]{:S(2)}, u32[]{:S(2)}) collective-permute-start(bf16[512,128]{1,0:T(8,128)(2,1)S(1)} %get-tuple-element.47), channel_id=1, source_target_pairs={{0,8},{4,12},{8,0},{12,4},{1,9},{5,13},{9,1},{13,5},{2,10},{6,14},... | collective-permute-start | bytes 393224 | tf_op jit(solution)/shard_map/ppermute | solution.py:315
  9.5 1.3 %collective-permute-start.5 = (bf16[512,128]{1,0:T(8,128)(2,1)S(1)}, bf16[512,128]{1,0:T(8,128)(2,1)S(1)}, u32[]{:S(2)}, u32[]{:S(2)}) collective-permute-start(bf16[512,128]{1,0:T(8,128)(2,1)S(1)} %get-tuple-element.48), channel_id=1, source_target_pairs={{0,12},{4,0},{8,4},{12,8},{1,13},{5,1},{9,5},{13,9},{2,14},{6,2},{... | collective-permute-start | bytes 393224 | tf_op jit(solution)/shard_map/ppermute | solution.py:315
  10.8 0.1 copy.5
  10.9 0.1 reshape.12
  11.0 0.0 collective-permute-done.6.far_d
  11.1 0.7 collective-permute-start
  11.8 0.0 collective-permute-done.7.far_a
  11.8 0.3 collective-permute-start.1
  12.1 2.6 %pack_rest.1 = (bf16[160,128]{1,0:T(8,128)(2,1)S(1)}, bf16[160,128]{1,0:T(8,128)(2,1)S(1)}, bf16[160,128]{1,0:T(8,128)(2,1)S(1)}, bf16[160,128]{1,0:T(8,128)(2,1...) custom-call(s32[3]{0:T(128)S(1)} %pad_add_fusion.where, ...), custom_call_target="tpu_custom_call" | custom-call | tf_op jit(solution)/shard_map/pack_rest/pallas_call | solution.py:380
  14.7 3.5 %collective-permute-done = s32[32]{0:T(128)S(1)} collective-permute-done((s32[32]{0:T(128)S(1)}, s32[32]{0:T(128)S(1)}, u32[]{:S(2)}, u32[]{:S(2)}) %collective-permute-start) | collective-permute-done | bytes 160 | tf_op jit(solution)/shard_map/ppermute | solution.py:315
  18.2 0.0 collective-permute-start.2
  18.2 2.8 %collective-permute-done.1 = s32[32]{0:T(128)S(1)} collective-permute-done((s32[32]{0:T(128)S(1)}, s32[32]{0:T(128)S(1)}, u32[]{:S(2)}, u32[]{:S(2)}) %collective-permute-start.1) | collective-permute-done | bytes 160 | tf_op jit(solution)/shard_map/ppermute | solution.py:315
  21.0 2.2 %collective-permute-start.10 = (bf16[160,128]{1,0:T(8,128)(2,1)S(1)}, bf16[160,128]{1,0:T(8,128)(2,1)S(1)}, u32[]{:S(2)}, u32[]{:S(2)}) collective-permute-start(bf16[160,128]{1,0:T(8,128)(2,1)S(1)} %get-tuple-element.52), channel_id=1, source_target_pairs={{0,12},{4,0},{8,4},{12,8},{1,13},{5,1},{9,5},{13,9},{2,14},{6,2},{... | collective-permute-start | bytes 122888 | tf_op jit(solution)/shard_map/ppermute | solution.py:315
  23.2 0.0 collective-permute-done.2
  23.2 0.6 collective-permute-start.8
  23.8 1.5 %collective-permute-start.9 = (bf16[160,128]{1,0:T(8,128)(2,1)S(1)}, bf16[160,128]{1,0:T(8,128)(2,1)S(1)}, u32[]{:S(2)}, u32[]{:S(2)}) collective-permute-start(bf16[160,128]{1,0:T(8,128)(2,1)S(1)} %get-tuple-element.51), channel_id=1, source_target_pairs={{0,8},{4,12},{8,0},{12,4},{1,9},{5,13},{9,1},{13,5},{2,10},{6,14},... | collective-permute-start | bytes 122888 | tf_op jit(solution)/shard_map/ppermute | solution.py:315
  25.3 0.1 pad_add_fusion.1.slots_ref
  25.4 3.7 %collective-permute-done.8.refs_5_.refs_9_ = bf16[160,128]{1,0:T(8,128)(2,1)S(1)} collective-permute-done((bf16[160,128]{1,0:T(8,128)(2,1)S(1)}, bf16[160,128]{1,0:T(8,128)(2,1)S(1)}, u32[]{:S(2)}, u32[]{:S(2)}) %collective-permute-start.8) | collective-permute-done | bytes 40992 | tf_op jit(solution)/shard_map/ppermute | solution.py:315
  29.1 0.1 collective-permute-done.9.refs_6_.refs_10_
  29.2 3.4 %triads.3 = (f32[2,16,128]{2,1,0:T(8,128)S(1)}, f32[2,16,128]{2,1,0:T(8,128)S(1)}, f32[2,16,128]{2,1,0:T(8,128)S(1)}, f32[2,16,128]{2,1,0:T(8,128)S(1)}, f32[2,1...) custom-call(s32[3]{0:T(128)S(1)} %pad_add_fusion.where, ...), custom_call_target="tpu_custom_call" | custom-call | tf_op jit(solution)/shard_map/triads/pallas_call | solution.py:407
  32.5 1.6 %collective-permute-start.11 = (f32[2,16,128]{2,1,0:T(8,128)S(1)}, f32[2,16,128]{2,1,0:T(8,128)S(1)}, u32[]{:S(2)}, u32[]{:S(2)}) collective-permute-start(f32[2,16,128]{2,1,0:T(8,128)S(1)} %get-tuple-element.54), channel_id=1, source_target_pairs={{0,2},{2,0},{4,6},{6,4},{8,10},{10,8},{12,14},{14,12},{1,3},{3,1},... | collective-permute-start | bytes 49160 | tf_op jit(solution)/shard_map/ppermute | solution.py:337
  34.1 1.6 %collective-permute-start.12 = (f32[2,16,128]{2,1,0:T(8,128)S(1)}, f32[2,16,128]{2,1,0:T(8,128)S(1)}, u32[]{:S(2)}, u32[]{:S(2)}) collective-permute-start(f32[2,16,128]{2,1,0:T(8,128)S(1)} %get-tuple-element.55), channel_id=1, source_target_pairs={{0,4},{2,6},{4,8},{6,10},{8,12},{10,14},{12,0},{14,2},{1,5},{3,7},... | collective-permute-start | bytes 49160 | tf_op jit(solution)/shard_map/ppermute | solution.py:337
  35.7 0.0 collective-permute-start.28
  35.7 2.3 %collective-permute-start.13 = (f32[2,16,128]{2,1,0:T(8,128)S(1)}, f32[2,16,128]{2,1,0:T(8,128)S(1)}, u32[]{:S(2)}, u32[]{:S(2)}) collective-permute-start(f32[2,16,128]{2,1,0:T(8,128)S(1)} %get-tuple-element.56), channel_id=1, source_target_pairs={{0,6},{2,4},{4,10},{6,8},{8,14},{10,12},{12,2},{14,0},{1,7},{3,5},... | collective-permute-start | bytes 49160 | tf_op jit(solution)/shard_map/ppermute | solution.py:337
  38.0 1.0 %collective-permute-start.18 = (bf16[512,128]{1,0:T(8,128)(2,1)S(1)}, bf16[512,128]{1,0:T(8,128)(2,1)S(1)}, u32[]{:S(2)}, u32[]{:S(2)}) collective-permute-start(bf16[512,128]{1,0:T(8,128)(2,1)S(1)} %get-tuple-element.62), channel_id=1, source_target_pairs={{0,4},{4,8},{8,12},{12,0},{1,5},{5,9},{9,13},{13,1},{2,6},{6,10},{... | collective-permute-start | bytes 393224 | tf_op jit(solution)/shard_map/ppermute | solution.py:315
  39.0 1.1 %collective-permute-start.19 = (bf16[512,128]{1,0:T(8,128)(2,1)S(1)}, bf16[512,128]{1,0:T(8,128)(2,1)S(1)}, u32[]{:S(2)}, u32[]{:S(2)}) collective-permute-start(bf16[512,128]{1,0:T(8,128)(2,1)S(1)} %get-tuple-element.63), channel_id=1, source_target_pairs={{0,8},{4,12},{8,0},{12,4},{1,9},{5,13},{9,1},{13,5},{2,10},{6,14},... | collective-permute-start | bytes 393224 | tf_op jit(solution)/shard_map/ppermute | solution.py:315
  40.1 2.9 %collective-permute-start.20 = (bf16[512,128]{1,0:T(8,128)(2,1)S(1)}, bf16[512,128]{1,0:T(8,128)(2,1)S(1)}, u32[]{:S(2)}, u32[]{:S(2)}) collective-permute-start(bf16[512,128]{1,0:T(8,128)(2,1)S(1)} %get-tuple-element.64), channel_id=1, source_target_pairs={{0,12},{4,0},{8,4},{12,8},{1,13},{5,1},{9,5},{13,9},{2,14},{6,2},{... | collective-permute-start | bytes 393224 | tf_op jit(solution)/shard_map/ppermute | solution.py:315
  43.0 2.1 %collective-permute-start.14 = (f32[2,16,128]{2,1,0:T(8,128)S(1)}, f32[2,16,128]{2,1,0:T(8,128)S(1)}, u32[]{:S(2)}, u32[]{:S(2)}) collective-permute-start(f32[2,16,128]{2,1,0:T(8,128)S(1)} %get-tuple-element.57), channel_id=1, source_target_pairs={{0,8},{2,10},{4,12},{6,14},{8,0},{10,2},{12,4},{14,6},{1,9},{3,11}... | collective-permute-start | bytes 49160 | tf_op jit(solution)/shard_map/ppermute | solution.py:337
  45.1 6.8 %collective-permute-done.14.refs_4_ = f32[2,16,128]{2,1,0:T(8,128)S(1)} collective-permute-done((f32[2,16,128]{2,1,0:T(8,128)S(1)}, f32[2,16,128]{2,1,0:T(8,128)S(1)}, u32[]{:S(2)}, u32[]{:S(2)}) %collective-permute-start.14) | collective-permute-done | bytes 16416 | tf_op jit(solution)/shard_map/ppermute | solution.py:337
  51.8 0.3 collective-permute-start.15
  52.1 5.2 %collective-permute-done.15.refs_5_ = f32[2,16,128]{2,1,0:T(8,128)S(1)} collective-permute-done((f32[2,16,128]{2,1,0:T(8,128)S(1)}, f32[2,16,128]{2,1,0:T(8,128)S(1)}, u32[]{:S(2)}, u32[]{:S(2)}) %collective-permute-start.15) | collective-permute-done | bytes 16416 | tf_op jit(solution)/shard_map/ppermute | solution.py:337
  57.4 0.9 collective-permute-start.30
  58.3 4.3 %collective-permute-done.29.refs_6_ = bf16[256,128]{1,0:T(8,128)(2,1)S(1)} collective-permute-done((bf16[256,128]{1,0:T(8,128)(2,1)S(1)}, bf16[256,128]{1,0:T(8,128)(2,1)S(1)}, u32[]{:S(2)}, u32[]{:S(2)}) %collective-permute-start.29) | collective-permute-done | bytes 65568 | tf_op jit(solution)/shard_map/ppermute | solution.py:315
  62.6 2.4 %collective-permute-start.16 = (f32[2,16,128]{2,1,0:T(8,128)S(1)}, f32[2,16,128]{2,1,0:T(8,128)S(1)}, u32[]{:S(2)}, u32[]{:S(2)}) collective-permute-start(f32[2,16,128]{2,1,0:T(8,128)S(1)} %get-tuple-element.59), channel_id=1, source_target_pairs={{0,12},{2,14},{4,0},{6,2},{8,4},{10,6},{12,8},{14,10},{1,13},{3,15... | collective-permute-start | bytes 49160 | tf_op jit(solution)/shard_map/ppermute | solution.py:337
  65.0 0.7 collective-permute-start.17
  65.7 2.4 %triads.5 = (f32[2,8,128]{2,1,0:T(8,128)S(1)}, f32[2,8,128]{2,1,0:T(8,128)S(1)}, f32[2,8,128]{2,1,0:T(8,128)S(1)}, f32[2,8,128]{2,1,0:T(8,128)S(1)}, f32[2,8,128...) custom-call(s32[3]{0:T(128)S(1)} %pad_add_fusion.where, ...), custom_call_target="tpu_custom_call" | custom-call | tf_op jit(solution)/shard_map/triads/pallas_call | solution.py:407
  68.2 0.8 collective-permute-start.31
  69.0 2.0 %collective-permute-start.32 = (f32[2,8,128]{2,1,0:T(8,128)S(1)}, f32[2,8,128]{2,1,0:T(8,128)S(1)}, u32[]{:S(2)}, u32[]{:S(2)}) collective-permute-start(f32[2,8,128]{2,1,0:T(8,128)S(1)} %get-tuple-element.79), channel_id=1, source_target_pairs={{0,4},{2,6},{4,8},{6,10},{8,12},{10,14},{12,0},{14,2},{1,5},{3,7},... | collective-permute-start | bytes 24584 | tf_op jit(solution)/shard_map/ppermute | solution.py:337
  71.0 0.8 collective-permute-start.33
  71.8 2.3 %collective-permute-start.34 = (f32[2,8,128]{2,1,0:T(8,128)S(1)}, f32[2,8,128]{2,1,0:T(8,128)S(1)}, u32[]{:S(2)}, u32[]{:S(2)}) collective-permute-start(f32[2,8,128]{2,1,0:T(8,128)S(1)} %get-tuple-element.81), channel_id=1, source_target_pairs={{0,8},{2,10},{4,12},{6,14},{8,0},{10,2},{12,4},{14,6},{1,9},{3,11}... | collective-permute-start | bytes 24584 | tf_op jit(solution)/shard_map/ppermute | solution.py:337
  74.1 3.4 %triads.4 = (f32[2,16,128]{2,1,0:T(8,128)S(1)}, f32[2,16,128]{2,1,0:T(8,128)S(1)}, f32[2,16,128]{2,1,0:T(8,128)S(1)}, f32[2,16,128]{2,1,0:T(8,128)S(1)}, f32[2,1...) custom-call(s32[3]{0:T(128)S(1)} %pad_add_fusion.where, ...), custom_call_target="tpu_custom_call" | custom-call | tf_op jit(solution)/shard_map/triads/pallas_call | solution.py:407
  77.5 0.8 collective-permute-start.21
  78.3 2.0 %collective-permute-start.22 = (f32[2,16,128]{2,1,0:T(8,128)S(1)}, f32[2,16,128]{2,1,0:T(8,128)S(1)}, u32[]{:S(2)}, u32[]{:S(2)}) collective-permute-start(f32[2,16,128]{2,1,0:T(8,128)S(1)} %get-tuple-element.67), channel_id=1, source_target_pairs={{0,4},{2,6},{4,8},{6,10},{8,12},{10,14},{12,0},{14,2},{1,5},{3,7},... | collective-permute-start | bytes 49160 | tf_op jit(solution)/shard_map/ppermute | solution.py:337
  80.3 0.7 collective-permute-start.35
  81.0 2.4 %collective-permute-start.36 = (f32[2,8,128]{2,1,0:T(8,128)S(1)}, f32[2,8,128]{2,1,0:T(8,128)S(1)}, u32[]{:S(2)}, u32[]{:S(2)}) collective-permute-start(f32[2,8,128]{2,1,0:T(8,128)S(1)} %get-tuple-element.83), channel_id=1, source_target_pairs={{0,12},{2,14},{4,0},{6,2},{8,4},{10,6},{12,8},{14,10},{1,13},{3,15... | collective-permute-start | bytes 24584 | tf_op jit(solution)/shard_map/ppermute | solution.py:337
  83.5 2.1 %collective-permute-start.37 = (f32[2,8,128]{2,1,0:T(8,128)S(1)}, f32[2,8,128]{2,1,0:T(8,128)S(1)}, u32[]{:S(2)}, u32[]{:S(2)}) collective-permute-start(f32[2,8,128]{2,1,0:T(8,128)S(1)} %get-tuple-element.84), channel_id=1, source_target_pairs={{0,14},{2,12},{4,2},{6,0},{8,6},{10,4},{12,10},{14,8},{1,15},{3,13... | collective-permute-start | bytes 24584 | tf_op jit(solution)/shard_map/ppermute | solution.py:337
  85.6 0.2 collective-permute-done.35.refs_21_
  85.9 0.8 collective-permute-start.23
  86.6 2.2 %collective-permute-start.24 = (f32[2,16,128]{2,1,0:T(8,128)S(1)}, f32[2,16,128]{2,1,0:T(8,128)S(1)}, u32[]{:S(2)}, u32[]{:S(2)}) collective-permute-start(f32[2,16,128]{2,1,0:T(8,128)S(1)} %get-tuple-element.69), channel_id=1, source_target_pairs={{0,8},{2,10},{4,12},{6,14},{8,0},{10,2},{12,4},{14,6},{1,9},{3,11}... | collective-permute-start | bytes 49160 | tf_op jit(solution)/shard_map/ppermute | solution.py:337
  88.9 0.9 collective-permute-start.25
  89.8 3.7 %collective-permute-start.26 = (f32[2,16,128]{2,1,0:T(8,128)S(1)}, f32[2,16,128]{2,1,0:T(8,128)S(1)}, u32[]{:S(2)}, u32[]{:S(2)}) collective-permute-start(f32[2,16,128]{2,1,0:T(8,128)S(1)} %get-tuple-element.71), channel_id=1, source_target_pairs={{0,12},{2,14},{4,0},{6,2},{8,4},{10,6},{12,8},{14,10},{1,13},{3,15... | collective-permute-start | bytes 49160 | tf_op jit(solution)/shard_map/ppermute | solution.py:337
  93.5 0.7 collective-permute-start.27
  94.2 0.2 collective-permute-done.25.refs_13_
  94.4 0.6 collective-permute-done.26.refs_14_
  95.0 3.2 %collective-permute-done.27.refs_15_ = f32[2,16,128]{2,1,0:T(8,128)S(1)} collective-permute-done((f32[2,16,128]{2,1,0:T(8,128)S(1)}, f32[2,16,128]{2,1,0:T(8,128)S(1)}, u32[]{:S(2)}, u32[]{:S(2)}) %collective-permute-start.27) | collective-permute-done | bytes 16416 | tf_op jit(solution)/shard_map/ppermute | solution.py:337
  98.2 1.5 %unpack.1 = f32[8,40,128]{2,1,0:T(8,128)} custom-call(s32[3]{0:T(128)S(1)} %pad_add_fusion.where, f32[2,16,128]{2,1,0:T(8,128)S(1)} %get-tuple-element.53.refs_0_, f32[2,16,128]{2,1,0:T(8,128)S(1)} %collective-permute-done.11.refs_1_, f32[2,16,128]{2,1,0:T(8,128)S(1)} %collective-permute-done.12.refs_2_, f32[2,16,128]{2,1,0:T(8,128)S(1)} %collective-permute-done.13.refs_3_, ...), custom_call_target="tpu_custom_call" | custom-call | tf_op jit(solution)/shard_map/unpack/pallas_call | solution.py:427
  (32 shorter events, 0.1 us)
Async XLA Ops:
  0.0 11.0 %collective-permute-start.6 = (bf16[4,8,80,128]{3,2,1,0:T(8,128)(2,1)}, bf16[4,8,80,128]{3,2,1,0:T(8,128)(2,1)S(1)}, u32[]{:S(2)}, u32[]{:S(2)}) collective-permute-start(bf16[4,8,80,128]{3,2,1,0:T(8,128)(2,1)} %bitcast.6), channel_id=1, source_target_pairs={{0,1},{1,0},{2,3},{3,2},{4,5},{5,4},{6,7},{7,6},{8,9},{9,8},{10,11... | collective-permute-start | bytes 1966088 | tf_op jit(solution)/shard_map/ppermute | solution.py:354
  0.5 11.3 %collective-permute-start.7 = (bf16[4,8,80,128]{3,2,1,0:T(8,128)(2,1)}, bf16[4,8,80,128]{3,2,1,0:T(8,128)(2,1)S(1)}, u32[]{:S(2)}, u32[]{:S(2)}) collective-permute-start(bf16[4,8,80,128]{3,2,1,0:T(8,128)(2,1)} %bitcast.10), channel_id=1, source_target_pairs={{0,1},{1,0},{2,3},{3,2},{4,5},{5,4},{6,7},{7,6},{8,9},{9,8},{10,11... | collective-permute-start | bytes 1966088 | tf_op jit(solution)/shard_map/ppermute | solution.py:355
  0.6 1.1 %copy-start = (bf16[4,4,2,5,16,128]{5,4,3,2,1,0:T(8,128)(2,1)S(1)}, bf16[4,4,2,5,16,128]{5,4,3,2,1,0:T(8,128)(2,1)}, u32[]{:S(2)}) copy-start(bf16[4,4,2,5,16,128]{5,4,3,2,1,0:T(8,128)(2,1)} %param.3) | copy-start | bytes 1966084
  1.7 1.1 %copy-start.2 = (bf16[4,4,2,5,16,128]{5,4,3,2,1,0:T(8,128)(2,1)S(1)}, bf16[4,4,2,5,16,128]{5,4,3,2,1,0:T(8,128)(2,1)}, u32[]{:S(2)}) copy-start(bf16[4,4,2,5,16,128]{5,4,3,2,1,0:T(8,128)(2,1)} %param.4) | copy-start | bytes 1966084
  2.8 9.4 %copy-start.1 = (bf16[4,4,2,5,16,128]{5,4,3,2,1,0:T(8,128)(2,1)S(1)}, bf16[4,4,2,5,16,128]{5,4,3,2,1,0:T(8,128)(2,1)}, u32[]{:S(2)}) copy-start(bf16[4,4,2,5,16,128]{5,4,3,2,1,0:T(8,128)(2,1)} %param.3) | copy-start | bytes 1966084
  2.8 9.4 %copy-start.3 = (bf16[4,4,2,5,16,128]{5,4,3,2,1,0:T(8,128)(2,1)S(1)}, bf16[4,4,2,5,16,128]{5,4,3,2,1,0:T(8,128)(2,1)}, u32[]{:S(2)}) copy-start(bf16[4,4,2,5,16,128]{5,4,3,2,1,0:T(8,128)(2,1)} %param.4) | copy-start | bytes 1966084
  3.8 7.0 %copy-start.4 = (s32[4,4,2]{1,2,0:T(2,128)S(1)}, s32[4,4,2]{1,2,0:T(2,128)}, u32[]{:S(2)}) copy-start(s32[4,4,2]{1,2,0:T(2,128)} %param.5) | copy-start | bytes 388
  3.8 20.0 %collective-permute-start.3 = (bf16[512,128]{1,0:T(8,128)(2,1)S(1)}, bf16[512,128]{1,0:T(8,128)(2,1)S(1)}, u32[]{:S(2)}, u32[]{:S(2)}) collective-permute-start(bf16[512,128]{1,0:T(8,128)(2,1)S(1)} %get-tuple-element.46), channel_id=1, source_target_pairs={{0,4},{4,8},{8,12},{12,0},{1,5},{5,9},{9,13},{13,1},{2,6},{6,10},{... | collective-permute-start | bytes 393224 | tf_op jit(solution)/shard_map/ppermute | solution.py:315
  6.9 18.5 %collective-permute-start.4 = (bf16[512,128]{1,0:T(8,128)(2,1)S(1)}, bf16[512,128]{1,0:T(8,128)(2,1)S(1)}, u32[]{:S(2)}, u32[]{:S(2)}) collective-permute-start(bf16[512,128]{1,0:T(8,128)(2,1)S(1)} %get-tuple-element.47), channel_id=1, source_target_pairs={{0,8},{4,12},{8,0},{12,4},{1,9},{5,13},{9,1},{13,5},{2,10},{6,14},... | collective-permute-start | bytes 393224 | tf_op jit(solution)/shard_map/ppermute | solution.py:315
  9.5 15.9 %collective-permute-start.5 = (bf16[512,128]{1,0:T(8,128)(2,1)S(1)}, bf16[512,128]{1,0:T(8,128)(2,1)S(1)}, u32[]{:S(2)}, u32[]{:S(2)}) collective-permute-start(bf16[512,128]{1,0:T(8,128)(2,1)S(1)} %get-tuple-element.48), channel_id=1, source_target_pairs={{0,12},{4,0},{8,4},{12,8},{1,13},{5,1},{9,5},{13,9},{2,14},{6,2},{... | collective-permute-start | bytes 393224 | tf_op jit(solution)/shard_map/ppermute | solution.py:315
  11.1 7.2 %collective-permute-start = (s32[32]{0:T(128)S(1)}, s32[32]{0:T(128)S(1)}, u32[]{:S(2)}, u32[]{:S(2)}) collective-permute-start(s32[32]{0:T(128)S(1)} %reshape.12), channel_id=1, source_target_pairs={{0,4},{4,8},{8,12},{12,0},{1,5},{5,9},{9,13},{13,1},{2,6},{6,10},{... | collective-permute-start | bytes 392 | tf_op jit(solution)/shard_map/ppermute | solution.py:315
  11.8 9.2 %collective-permute-start.1 = (s32[32]{0:T(128)S(1)}, s32[32]{0:T(128)S(1)}, u32[]{:S(2)}, u32[]{:S(2)}) collective-permute-start(s32[32]{0:T(128)S(1)} %reshape.12), channel_id=1, source_target_pairs={{0,8},{4,12},{8,0},{12,4},{1,9},{5,13},{9,1},{13,5},{2,10},{6,14},... | collective-permute-start | bytes 392 | tf_op jit(solution)/shard_map/ppermute | solution.py:315
  18.2 5.0 %collective-permute-start.2 = (s32[32]{0:T(128)S(1)}, s32[32]{0:T(128)S(1)}, u32[]{:S(2)}, u32[]{:S(2)}) collective-permute-start(s32[32]{0:T(128)S(1)} %reshape.12), channel_id=1, source_target_pairs={{0,12},{4,0},{8,4},{12,8},{1,13},{5,1},{9,5},{13,9},{2,14},{6,2},{... | collective-permute-start | bytes 392 | tf_op jit(solution)/shard_map/ppermute | solution.py:315
  21.0 4.4 %collective-permute-start.10 = (bf16[160,128]{1,0:T(8,128)(2,1)S(1)}, bf16[160,128]{1,0:T(8,128)(2,1)S(1)}, u32[]{:S(2)}, u32[]{:S(2)}) collective-permute-start(bf16[160,128]{1,0:T(8,128)(2,1)S(1)} %get-tuple-element.52), channel_id=1, source_target_pairs={{0,12},{4,0},{8,4},{12,8},{1,13},{5,1},{9,5},{13,9},{2,14},{6,2},{... | collective-permute-start | bytes 122888 | tf_op jit(solution)/shard_map/ppermute | solution.py:315
  23.2 5.9 %collective-permute-start.8 = (bf16[160,128]{1,0:T(8,128)(2,1)S(1)}, bf16[160,128]{1,0:T(8,128)(2,1)S(1)}, u32[]{:S(2)}, u32[]{:S(2)}) collective-permute-start(bf16[160,128]{1,0:T(8,128)(2,1)S(1)} %get-tuple-element.50), channel_id=1, source_target_pairs={{0,4},{4,8},{8,12},{12,0},{1,5},{5,9},{9,13},{13,1},{2,6},{6,10},{... | collective-permute-start | bytes 122888 | tf_op jit(solution)/shard_map/ppermute | solution.py:315
  23.8 5.3 %collective-permute-start.9 = (bf16[160,128]{1,0:T(8,128)(2,1)S(1)}, bf16[160,128]{1,0:T(8,128)(2,1)S(1)}, u32[]{:S(2)}, u32[]{:S(2)}) collective-permute-start(bf16[160,128]{1,0:T(8,128)(2,1)S(1)} %get-tuple-element.51), channel_id=1, source_target_pairs={{0,8},{4,12},{8,0},{12,4},{1,9},{5,13},{9,1},{13,5},{2,10},{6,14},... | collective-permute-start | bytes 122888 | tf_op jit(solution)/shard_map/ppermute | solution.py:315
  32.5 6.5 %collective-permute-start.11 = (f32[2,16,128]{2,1,0:T(8,128)S(1)}, f32[2,16,128]{2,1,0:T(8,128)S(1)}, u32[]{:S(2)}, u32[]{:S(2)}) collective-permute-start(f32[2,16,128]{2,1,0:T(8,128)S(1)} %get-tuple-element.54), channel_id=1, source_target_pairs={{0,2},{2,0},{4,6},{6,4},{8,10},{10,8},{12,14},{14,12},{1,3},{3,1},... | collective-permute-start | bytes 49160 | tf_op jit(solution)/shard_map/ppermute | solution.py:337
  34.1 6.0 %collective-permute-start.12 = (f32[2,16,128]{2,1,0:T(8,128)S(1)}, f32[2,16,128]{2,1,0:T(8,128)S(1)}, u32[]{:S(2)}, u32[]{:S(2)}) collective-permute-start(f32[2,16,128]{2,1,0:T(8,128)S(1)} %get-tuple-element.55), channel_id=1, source_target_pairs={{0,4},{2,6},{4,8},{6,10},{8,12},{10,14},{12,0},{14,2},{1,5},{3,7},... | collective-permute-start | bytes 49160 | tf_op jit(solution)/shard_map/ppermute | solution.py:337
  35.7 21.7 %collective-permute-start.28 = (bf16[256,128]{1,0:T(8,128)(2,1)S(1)}, bf16[256,128]{1,0:T(8,128)(2,1)S(1)}, u32[]{:S(2)}, u32[]{:S(2)}) collective-permute-start(bf16[256,128]{1,0:T(8,128)(2,1)S(1)} %get-tuple-element.74), channel_id=1, source_target_pairs={{0,4},{4,8},{8,12},{12,0},{1,5},{5,9},{9,13},{13,1},{2,6},{6,10},{... | collective-permute-start | bytes 196616 | tf_op jit(solution)/shard_map/ppermute | solution.py:315
  35.7 7.3 %collective-permute-start.13 = (f32[2,16,128]{2,1,0:T(8,128)S(1)}, f32[2,16,128]{2,1,0:T(8,128)S(1)}, u32[]{:S(2)}, u32[]{:S(2)}) collective-permute-start(f32[2,16,128]{2,1,0:T(8,128)S(1)} %get-tuple-element.56), channel_id=1, source_target_pairs={{0,6},{2,4},{4,10},{6,8},{8,14},{10,12},{12,2},{14,0},{1,7},{3,5},... | collective-permute-start | bytes 49160 | tf_op jit(solution)/shard_map/ppermute | solution.py:337
  38.0 31.0 %collective-permute-start.18 = (bf16[512,128]{1,0:T(8,128)(2,1)S(1)}, bf16[512,128]{1,0:T(8,128)(2,1)S(1)}, u32[]{:S(2)}, u32[]{:S(2)}) collective-permute-start(bf16[512,128]{1,0:T(8,128)(2,1)S(1)} %get-tuple-element.62), channel_id=1, source_target_pairs={{0,4},{4,8},{8,12},{12,0},{1,5},{5,9},{9,13},{13,1},{2,6},{6,10},{... | collective-permute-start | bytes 393224 | tf_op jit(solution)/shard_map/ppermute | solution.py:315
  39.0 32.0 %collective-permute-start.19 = (bf16[512,128]{1,0:T(8,128)(2,1)S(1)}, bf16[512,128]{1,0:T(8,128)(2,1)S(1)}, u32[]{:S(2)}, u32[]{:S(2)}) collective-permute-start(bf16[512,128]{1,0:T(8,128)(2,1)S(1)} %get-tuple-element.63), channel_id=1, source_target_pairs={{0,8},{4,12},{8,0},{12,4},{1,9},{5,13},{9,1},{13,5},{2,10},{6,14},... | collective-permute-start | bytes 393224 | tf_op jit(solution)/shard_map/ppermute | solution.py:315
  40.1 31.7 %collective-permute-start.20 = (bf16[512,128]{1,0:T(8,128)(2,1)S(1)}, bf16[512,128]{1,0:T(8,128)(2,1)S(1)}, u32[]{:S(2)}, u32[]{:S(2)}) collective-permute-start(bf16[512,128]{1,0:T(8,128)(2,1)S(1)} %get-tuple-element.64), channel_id=1, source_target_pairs={{0,12},{4,0},{8,4},{12,8},{1,13},{5,1},{9,5},{13,9},{2,14},{6,2},{... | collective-permute-start | bytes 393224 | tf_op jit(solution)/shard_map/ppermute | solution.py:315
  43.0 8.9 %collective-permute-start.14 = (f32[2,16,128]{2,1,0:T(8,128)S(1)}, f32[2,16,128]{2,1,0:T(8,128)S(1)}, u32[]{:S(2)}, u32[]{:S(2)}) collective-permute-start(f32[2,16,128]{2,1,0:T(8,128)S(1)} %get-tuple-element.57), channel_id=1, source_target_pairs={{0,8},{2,10},{4,12},{6,14},{8,0},{10,2},{12,4},{14,6},{1,9},{3,11}... | collective-permute-start | bytes 49160 | tf_op jit(solution)/shard_map/ppermute | solution.py:337
  51.8 5.5 %collective-permute-start.15 = (f32[2,16,128]{2,1,0:T(8,128)S(1)}, f32[2,16,128]{2,1,0:T(8,128)S(1)}, u32[]{:S(2)}, u32[]{:S(2)}) collective-permute-start(f32[2,16,128]{2,1,0:T(8,128)S(1)} %get-tuple-element.58), channel_id=1, source_target_pairs={{0,10},{2,8},{4,14},{6,12},{8,2},{10,0},{12,6},{14,4},{1,11},{3,9}... | collective-permute-start | bytes 49160 | tf_op jit(solution)/shard_map/ppermute | solution.py:337
  57.4 5.2 %collective-permute-start.29 = (bf16[256,128]{1,0:T(8,128)(2,1)S(1)}, bf16[256,128]{1,0:T(8,128)(2,1)S(1)}, u32[]{:S(2)}, u32[]{:S(2)}) collective-permute-start(bf16[256,128]{1,0:T(8,128)(2,1)S(1)} %get-tuple-element.75), channel_id=1, source_target_pairs={{0,8},{4,12},{8,0},{12,4},{1,9},{5,13},{9,1},{13,5},{2,10},{6,14},... | collective-permute-start | bytes 196616 | tf_op jit(solution)/shard_map/ppermute | solution.py:315
  57.4 7.6 %collective-permute-start.30 = (bf16[256,128]{1,0:T(8,128)(2,1)S(1)}, bf16[256,128]{1,0:T(8,128)(2,1)S(1)}, u32[]{:S(2)}, u32[]{:S(2)}) collective-permute-start(bf16[256,128]{1,0:T(8,128)(2,1)S(1)} %get-tuple-element.76), channel_id=1, source_target_pairs={{0,12},{4,0},{8,4},{12,8},{1,13},{5,1},{9,5},{13,9},{2,14},{6,2},{... | collective-permute-start | bytes 196616 | tf_op jit(solution)/shard_map/ppermute | solution.py:315
  62.6 5.6 %collective-permute-start.16 = (f32[2,16,128]{2,1,0:T(8,128)S(1)}, f32[2,16,128]{2,1,0:T(8,128)S(1)}, u32[]{:S(2)}, u32[]{:S(2)}) collective-permute-start(f32[2,16,128]{2,1,0:T(8,128)S(1)} %get-tuple-element.59), channel_id=1, source_target_pairs={{0,12},{2,14},{4,0},{6,2},{8,4},{10,6},{12,8},{14,10},{1,13},{3,15... | collective-permute-start | bytes 49160 | tf_op jit(solution)/shard_map/ppermute | solution.py:337
  65.0 12.4 %collective-permute-start.17 = (f32[2,16,128]{2,1,0:T(8,128)S(1)}, f32[2,16,128]{2,1,0:T(8,128)S(1)}, u32[]{:S(2)}, u32[]{:S(2)}) collective-permute-start(f32[2,16,128]{2,1,0:T(8,128)S(1)} %get-tuple-element.60), channel_id=1, source_target_pairs={{0,14},{2,12},{4,2},{6,0},{8,6},{10,4},{12,10},{14,8},{1,15},{3,13... | collective-permute-start | bytes 49160 | tf_op jit(solution)/shard_map/ppermute | solution.py:337
  68.2 10.1 %collective-permute-start.31 = (f32[2,8,128]{2,1,0:T(8,128)S(1)}, f32[2,8,128]{2,1,0:T(8,128)S(1)}, u32[]{:S(2)}, u32[]{:S(2)}) collective-permute-start(f32[2,8,128]{2,1,0:T(8,128)S(1)} %get-tuple-element.78), channel_id=1, source_target_pairs={{0,2},{2,0},{4,6},{6,4},{8,10},{10,8},{12,14},{14,12},{1,3},{3,1},... | collective-permute-start | bytes 24584 | tf_op jit(solution)/shard_map/ppermute | solution.py:337
  69.0 11.3 %collective-permute-start.32 = (f32[2,8,128]{2,1,0:T(8,128)S(1)}, f32[2,8,128]{2,1,0:T(8,128)S(1)}, u32[]{:S(2)}, u32[]{:S(2)}) collective-permute-start(f32[2,8,128]{2,1,0:T(8,128)S(1)} %get-tuple-element.79), channel_id=1, source_target_pairs={{0,4},{2,6},{4,8},{6,10},{8,12},{10,14},{12,0},{14,2},{1,5},{3,7},... | collective-permute-start | bytes 24584 | tf_op jit(solution)/shard_map/ppermute | solution.py:337
  71.0 10.0 %collective-permute-start.33 = (f32[2,8,128]{2,1,0:T(8,128)S(1)}, f32[2,8,128]{2,1,0:T(8,128)S(1)}, u32[]{:S(2)}, u32[]{:S(2)}) collective-permute-start(f32[2,8,128]{2,1,0:T(8,128)S(1)} %get-tuple-element.80), channel_id=1, source_target_pairs={{0,6},{2,4},{4,10},{6,8},{8,14},{10,12},{12,2},{14,0},{1,7},{3,5},... | collective-permute-start | bytes 24584 | tf_op jit(solution)/shard_map/ppermute | solution.py:337
  71.8 11.7 %collective-permute-start.34 = (f32[2,8,128]{2,1,0:T(8,128)S(1)}, f32[2,8,128]{2,1,0:T(8,128)S(1)}, u32[]{:S(2)}, u32[]{:S(2)}) collective-permute-start(f32[2,8,128]{2,1,0:T(8,128)S(1)} %get-tuple-element.81), channel_id=1, source_target_pairs={{0,8},{2,10},{4,12},{6,14},{8,0},{10,2},{12,4},{14,6},{1,9},{3,11}... | collective-permute-start | bytes 24584 | tf_op jit(solution)/shard_map/ppermute | solution.py:337
  77.5 12.3 %collective-permute-start.21 = (f32[2,16,128]{2,1,0:T(8,128)S(1)}, f32[2,16,128]{2,1,0:T(8,128)S(1)}, u32[]{:S(2)}, u32[]{:S(2)}) collective-permute-start(f32[2,16,128]{2,1,0:T(8,128)S(1)} %get-tuple-element.66), channel_id=1, source_target_pairs={{0,2},{2,0},{4,6},{6,4},{8,10},{10,8},{12,14},{14,12},{1,3},{3,1},... | collective-permute-start | bytes 49160 | tf_op jit(solution)/shard_map/ppermute | solution.py:337
  78.3 15.2 %collective-permute-start.22 = (f32[2,16,128]{2,1,0:T(8,128)S(1)}, f32[2,16,128]{2,1,0:T(8,128)S(1)}, u32[]{:S(2)}, u32[]{:S(2)}) collective-permute-start(f32[2,16,128]{2,1,0:T(8,128)S(1)} %get-tuple-element.67), channel_id=1, source_target_pairs={{0,4},{2,6},{4,8},{6,10},{8,12},{10,14},{12,0},{14,2},{1,5},{3,7},... | collective-permute-start | bytes 49160 | tf_op jit(solution)/shard_map/ppermute | solution.py:337
  80.3 5.5 %collective-permute-start.35 = (f32[2,8,128]{2,1,0:T(8,128)S(1)}, f32[2,8,128]{2,1,0:T(8,128)S(1)}, u32[]{:S(2)}, u32[]{:S(2)}) collective-permute-start(f32[2,8,128]{2,1,0:T(8,128)S(1)} %get-tuple-element.82), channel_id=1, source_target_pairs={{0,10},{2,8},{4,14},{6,12},{8,2},{10,0},{12,6},{14,4},{1,11},{3,9}... | collective-permute-start | bytes 24584 | tf_op jit(solution)/shard_map/ppermute | solution.py:337
  81.0 5.6 %collective-permute-start.36 = (f32[2,8,128]{2,1,0:T(8,128)S(1)}, f32[2,8,128]{2,1,0:T(8,128)S(1)}, u32[]{:S(2)}, u32[]{:S(2)}) collective-permute-start(f32[2,8,128]{2,1,0:T(8,128)S(1)} %get-tuple-element.83), channel_id=1, source_target_pairs={{0,12},{2,14},{4,0},{6,2},{8,4},{10,6},{12,8},{14,10},{1,13},{3,15... | collective-permute-start | bytes 24584 | tf_op jit(solution)/shard_map/ppermute | solution.py:337
  83.5 5.4 %collective-permute-start.37 = (f32[2,8,128]{2,1,0:T(8,128)S(1)}, f32[2,8,128]{2,1,0:T(8,128)S(1)}, u32[]{:S(2)}, u32[]{:S(2)}) collective-permute-start(f32[2,8,128]{2,1,0:T(8,128)S(1)} %get-tuple-element.84), channel_id=1, source_target_pairs={{0,14},{2,12},{4,2},{6,0},{8,6},{10,4},{12,10},{14,8},{1,15},{3,13... | collective-permute-start | bytes 24584 | tf_op jit(solution)/shard_map/ppermute | solution.py:337
  85.9 8.4 %collective-permute-start.23 = (f32[2,16,128]{2,1,0:T(8,128)S(1)}, f32[2,16,128]{2,1,0:T(8,128)S(1)}, u32[]{:S(2)}, u32[]{:S(2)}) collective-permute-start(f32[2,16,128]{2,1,0:T(8,128)S(1)} %get-tuple-element.68), channel_id=1, source_target_pairs={{0,6},{2,4},{4,10},{6,8},{8,14},{10,12},{12,2},{14,0},{1,7},{3,5},... | collective-permute-start | bytes 49160 | tf_op jit(solution)/shard_map/ppermute | solution.py:337
  86.6 7.6 %collective-permute-start.24 = (f32[2,16,128]{2,1,0:T(8,128)S(1)}, f32[2,16,128]{2,1,0:T(8,128)S(1)}, u32[]{:S(2)}, u32[]{:S(2)}) collective-permute-start(f32[2,16,128]{2,1,0:T(8,128)S(1)} %get-tuple-element.69), channel_id=1, source_target_pairs={{0,8},{2,10},{4,12},{6,14},{8,0},{10,2},{12,4},{14,6},{1,9},{3,11}... | collective-permute-start | bytes 49160 | tf_op jit(solution)/shard_map/ppermute | solution.py:337
  88.9 5.5 %collective-permute-start.25 = (f32[2,16,128]{2,1,0:T(8,128)S(1)}, f32[2,16,128]{2,1,0:T(8,128)S(1)}, u32[]{:S(2)}, u32[]{:S(2)}) collective-permute-start(f32[2,16,128]{2,1,0:T(8,128)S(1)} %get-tuple-element.70), channel_id=1, source_target_pairs={{0,10},{2,8},{4,14},{6,12},{8,2},{10,0},{12,6},{14,4},{1,11},{3,9}... | collective-permute-start | bytes 49160 | tf_op jit(solution)/shard_map/ppermute | solution.py:337
  89.8 5.2 %collective-permute-start.26 = (f32[2,16,128]{2,1,0:T(8,128)S(1)}, f32[2,16,128]{2,1,0:T(8,128)S(1)}, u32[]{:S(2)}, u32[]{:S(2)}) collective-permute-start(f32[2,16,128]{2,1,0:T(8,128)S(1)} %get-tuple-element.71), channel_id=1, source_target_pairs={{0,12},{2,14},{4,0},{6,2},{8,4},{10,6},{12,8},{14,10},{1,13},{3,15... | collective-permute-start | bytes 49160 | tf_op jit(solution)/shard_map/ppermute | solution.py:337
  93.5 4.6 %collective-permute-start.27 = (f32[2,16,128]{2,1,0:T(8,128)S(1)}, f32[2,16,128]{2,1,0:T(8,128)S(1)}, u32[]{:S(2)}, u32[]{:S(2)}) collective-permute-start(f32[2,16,128]{2,1,0:T(8,128)S(1)} %get-tuple-element.72), channel_id=1, source_target_pairs={{0,14},{2,12},{4,2},{6,0},{8,6},{10,4},{12,10},{14,8},{1,15},{3,13... | collective-permute-start | bytes 49160 | tf_op jit(solution)/shard_map/ppermute | solution.py:337

commit v3 on v2

v3 whole, which is shorter than its diff:
```python
import functools
import math

import jax
import jax.numpy as jnp
from jax import lax
from jax.experimental import pallas as pl
from jax.experimental.pallas import tpu as pltpu
from jax.sharding import PartitionSpec as P

HARMS = 8
LANES = 128
HALO = 4
SLOT_ROWS = 16
GROUPS = ((1, 2, 0, 3, 4),)
VMEM_LIMIT = 40 * 1024 * 1024


def iota(shape, axis):
    return lax.broadcasted_iota(jnp.int32, shape, axis)


def one_hot(mask):
    return jnp.where(mask, 1.0, 0.0).astype(jnp.bfloat16)


def halo_offset(index, width):
    return jnp.where(index < 2, index - 2, index - 2 + width)


def wrapped(index, count):
    return jnp.where(index >= count, index - count, index)


def columns(harms, blocks):
    shape = (harms * LANES, blocks * LANES)
    row, col = iota(shape, 0), iota(shape, 1)
    return row // LANES, row % LANES, col // LANES, col % LANES


def side_by_side(ref, group, rows):
    return jnp.concatenate([ref[k, group, rows, :] for k in range(ref.shape[0])], axis=1)


def fill_main(matrix, sizes):
    harms, blocks, width = sizes
    harm_in, cell_in, owner, lane = columns(harms, blocks)
    matrix[...] = one_hot(
        (lane // width == harm_in) & (cell_in == owner * width + lane % width)
    )


def write_main(arrays, fields, cells, matrix, out):
    groups = arrays[0].shape[1]
    pieces = []
    for array in arrays:
        for field in fields:
            rows = slice(field * cells, (field + 1) * cells)
            pieces += [side_by_side(array, group, rows) for group in range(groups)]
    main = jnp.dot(
        jnp.concatenate(pieces, axis=0), matrix[...], preferred_element_type=jnp.float32
    )
    for owner in range(out.shape[0]):
        out[owner, 0 : main.shape[0], :] = main[:, owner * LANES : (owner + 1) * LANES].astype(
            jnp.bfloat16
        )


def first_pack_kernel(sizes, cells, rad, slots, own_d, own_a, far_d, far_a, out, main_m, halo_m):
    harms, blocks, width = sizes
    groups, group_rows = own_d.shape[1], own_d.shape[2]
    fill_main(main_m, sizes)
    write_main((own_d, own_a), GROUPS[0], cells, main_m, out)
    base = 2 * len(GROUPS[0]) * groups * cells
    shift = jnp.where(rad[0] == 0, LANES, -LANES)
    depth = harms * LANES
    span_h = harms * HALO
    harm_in, cell_in, owner, lane = columns(harms, blocks)
    part = lane % span_h
    wanted = owner * width + halo_offset(part % HALO, width)
    same = (part // HALO == harm_in) & (lane < groups * span_h)
    halo_m[0:depth, :] = one_hot(same & (cell_in == wanted))
    halo_m[depth:, :] = one_hot(same & (cell_in + shift == wanted))
    lane_group = (iota((group_rows, blocks * LANES), 1) % LANES) // span_h
    everything = slice(0, group_rows)
    for array, (own, far) in enumerate(((own_d, far_d), (own_a, far_a))):
        pieces = [
            jnp.concatenate(
                [side_by_side(own, group, everything), side_by_side(far, group, everything)], axis=1
            )
            for group in range(groups)
        ]
        ends = jnp.dot(
            jnp.concatenate(pieces, axis=0), halo_m[...], preferred_element_type=jnp.float32
        )
        held = jnp.zeros((group_rows, blocks * LANES), jnp.float32)
        for group in range(groups):
            held = jnp.where(
                lane_group == group, ends[group * group_rows : (group + 1) * group_rows], held
            )
        start = base + array * group_rows
        for block in range(blocks):
            out[block, start : start + group_rows, :] = held[
                :, block * LANES : (block + 1) * LANES
            ].astype(jnp.bfloat16)
    lane = iota((SLOT_ROWS, LANES), 1)
    listed = jnp.zeros((SLOT_ROWS, LANES), jnp.int32)
    for index in range(slots.shape[0]):
        listed = jnp.where(lane == index, slots[index], listed)
    start = base + 2 * group_rows
    for block in range(blocks):
        out[block, start : start + SLOT_ROWS, :] = listed.astype(jnp.float32).astype(jnp.bfloat16)


def rest_pack_kernel(sizes, cells, own_d, own_a, *refs):
    outs, matrix = refs[:-1], refs[-1]
    fill_main(matrix, sizes)
    for fields, out in zip(GROUPS[1:], outs):
        write_main((own_d, own_a), fields, cells, matrix, out)


def coefficient(distance):
    near = jnp.where(distance == 1, 8.0, jnp.where(distance == -1, -8.0, 0.0))
    return jnp.where(distance == 2, -1.0, jnp.where(distance == -2, 1.0, near))


def triad_kernel(sizes, fields, *refs):
    harms, blocks, width, groups, slots, all_fields, cells, harm_devices = sizes
    first = fields == GROUPS[0]
    lead, main = refs[0], refs[0 if first else 1]
    at = 1 if first else 2
    out, radial_m, axial_m, plain_v, axial_v, radial_v, sums, slots_v, slots_s, slots_sem = refs[at:]
    halo_row = 2 * len(GROUPS[0]) * groups * cells
    slot_row = halo_row + 2 * all_fields * cells
    for block in range(blocks):
        slots_v[block : block + 1, :] = (
            lead[block, slot_row : slot_row + SLOT_ROWS, :].astype(jnp.float32)[0:1, :]
        ).astype(jnp.int32)
    listing = pltpu.make_async_copy(slots_v, slots_s, slots_sem)
    listing.start()
    count = len(fields)
    span_h = harms * HALO
    used = harms * width
    tile = groups * cells
    shape = (LANES, LANES)
    row, col = iota(shape, 0), iota(shape, 1)
    inside = (row // width == col // width) & (row < used) & (col < used)
    within = jnp.where(inside, coefficient(row - col), 0.0).astype(jnp.bfloat16)
    square = (tile, tile)
    row_t, col_t = iota(square, 0), iota(square, 1)
    axial_m[...] = jnp.where(
        row_t // cells == col_t // cells, coefficient(col_t - row_t), 0.0
    ).astype(jnp.bfloat16)

    for group in range(groups):
        part = row - group * span_h
        mine = (part >= 0) & (part < span_h) & (col < used) & (part // HALO == col // width)
        place = halo_offset(part % HALO, width)
        around = jnp.where(mine, coefficient(place - col % width), 0.0).astype(jnp.bfloat16)
        radial_m[group] = jnp.concatenate([within, around], axis=0)
    for group in range(groups):
        pieces = []
        for array in range(2):
            for local, field in enumerate(fields):
                for step in range(blocks):
                    start = ((array * count + local) * groups + group) * cells
                    beside = halo_row + (array * all_fields + field) * cells
                    pieces.append(
                        jnp.concatenate(
                            [
                                main[step, start : start + cells, :],
                                lead[step, beside : beside + cells, :],
                            ],
                            axis=1,
                        )
                    )
        slopes = jnp.dot(
            jnp.concatenate(pieces, axis=0), radial_m[group], preferred_element_type=jnp.float32
        )
        index = 0
        for array in range(2):
            for local in range(count):
                for step in range(blocks):
                    radial_v[array * count + local, step * groups + group] = slopes[
                        index * cells : (index + 1) * cells, :
                    ]
                    index += 1
    for step in range(blocks):
        for local in range(count):
            starts = [(array * count + local) * tile for array in range(2)]
            both = jnp.concatenate([main[step, s : s + tile, :] for s in starts], axis=1)
            slopes = jnp.dot(axial_m[...], both, preferred_element_type=jnp.float32)
            for array in range(2):
                for group in range(groups):
                    axial_v[array * count + local, step * groups + group] = slopes[
                        group * cells : (group + 1) * cells, array * LANES : (array + 1) * LANES
                    ]
        for which in range(4):
            for group in range(groups):
                held = which // 2 * len(GROUPS[0]) + which % 2
                start = (held * groups + group) * cells
                plain_v[which, step * groups + group] = lead[
                    step, start : start + cells, :
                ].astype(jnp.float32)

    listing.wait()

    @pl.loop(0, blocks * slots)
    def _(index):
        step = index // slots
        entry = lax.rem(index, slots) * blocks

        def add_stop(stop, running):
            source = wrapped(step - stop + blocks, blocks)
            at_a = step * groups + slots_s[step, (entry + stop) * 2] * 2
            at_d = source * groups + slots_s[step, (entry + stop) * 2 + 1] * 2
            d1r, d1i, d2r, d2i = (plain_v[w, at_d + c] for w in (0, 1) for c in (0, 1))
            a1r, a1i, a2r, a2i = (plain_v[w, at_a + c] for w in (2, 3) for c in (0, 1))
            result = []
            for local in range(count):
                xar, xai = axial_v[count + local, at_a], axial_v[count + local, at_a + 1]
                rar, rai = radial_v[count + local, at_a], radial_v[count + local, at_a + 1]
                xdr, xdi = axial_v[local, at_d], axial_v[local, at_d + 1]
                rdr, rdi = radial_v[local, at_d], radial_v[local, at_d + 1]
                real = (d1r * xar + d1i * xai) + (d2r * rar + d2i * rai)
                real = real + ((xdr * a1r + xdi * a1i) + (rdr * a2r + rdi * a2i))
                imag = (d1r * xai - d1i * xar) + (d2r * rai - d2i * rar)
                imag = imag + ((xdr * a1i - xdi * a1r) + (rdr * a2i - rdi * a2r))
                old_real, old_imag = running[local]
                result.append((old_real + real, old_imag + imag))
            return tuple(result)

        zero = jnp.zeros((cells, LANES), jnp.float32)
        running = tuple((zero, zero) for _ in range(count))
        if blocks <= 4:
            for stop in range(blocks):
                running = add_stop(stop, running)
        else:
            running = lax.fori_loop(0, blocks, add_stop, running)
        for local in range(count):
            for part in range(2):
                sums[index, part * count + local] = running[local][part]

    scale = 1.0 / (12.0 * math.sqrt(8.0 * blocks * HARMS))
    per_harm = blocks // harm_devices
    own_cells = cells // blocks
    lane_slot = iota((cells, LANES), 1) // width

    @pl.loop(0, blocks)
    def _(step):
        for row in range(2 * count):
            packed = jnp.zeros((cells, LANES), jnp.float32)
            for slot in range(slots):
                value = sums[step * slots + slot, row]
                reach = harms // 2
                while reach:
                    value = value + pltpu.roll(value, reach * width, axis=1)
                    reach //= 2
                if used < LANES and slot:
                    value = pltpu.roll(value, slot * width, axis=1)
                packed = jnp.where(lane_slot == slot, value, packed)
            packed = packed * scale
            for owner in range(blocks):
                out[
                    owner * harm_devices + step // per_harm,
                    lax.rem(step, per_harm),
                    row * own_cells : (row + 1) * own_cells,
                    :,
                ] = packed[owner * own_cells : (owner + 1) * own_cells, :]


def unpack_kernel(sizes, *refs):
    blocks, harm_devices, slots, width, per_harm, own_cells, all_fields = sizes
    ins, out_ref = refs[:-1], refs[-1]
    for came, fields in zip(ins, GROUPS):
        count = len(fields)
        rows = 2 * count * own_cells
        lane_block = iota((rows, LANES), 1) // width
        for local in range(per_harm):
            packed = [jnp.zeros((rows, LANES), jnp.float32) for _ in range(slots)]
            for source in range(blocks):
                total = came[source * harm_devices, local]
                for harm in range(1, harm_devices):
                    total = total + came[source * harm_devices + harm, local]
                for slot in range(slots):
                    amount = (source - slot) * width % LANES
                    moved = pltpu.roll(total, amount, axis=1) if amount else total
                    packed[slot] = jnp.where(lane_block == source, moved, packed[slot])
            for slot in range(slots):
                for part in range(2):
                    for at, field in enumerate(fields):
                        start = (part * count + at) * own_cells
                        target = (part * all_fields + field) * own_cells
                        out_ref[local * slots + slot, target : target + own_cells, :] = packed[
                            slot
                        ][start : start + own_cells, :]


def smem(count):
    return [pl.BlockSpec(memory_space=pltpu.SMEM)] * count


def vmem(count):
    return [pl.BlockSpec(memory_space=pltpu.VMEM)] * count


def exchanged(value, axes):
    return lax.all_to_all(value, axes, split_axis=0, concat_axis=0, tiled=True)


def body(direct_field, adjoint_field, triad_slots):
    blocks, harm_devices = lax.axis_size("mode"), lax.axis_size("harm")
    harms, slots, parts, fields, cells, radial = direct_field.shape
    width = radial // blocks
    groups, group_rows = slots * parts, fields * cells
    tile = groups * cells
    params = pltpu.CompilerParams(vmem_limit_bytes=VMEM_LIMIT)
    rad = lax.axis_index("rad").astype(jnp.int32).reshape(1)

    direct = direct_field.reshape(harms, groups, group_rows, radial)
    adjoint = adjoint_field.reshape(harms, groups, group_rows, radial)
    swap = [(0, 1), (1, 0)]
    far_direct = lax.ppermute(direct, "rad", swap)
    far_adjoint = lax.ppermute(adjoint, "rad", swap)

    def payload(rows):
        return jax.ShapeDtypeStruct((blocks, rows, LANES), jnp.bfloat16)

    sizes = (harms, blocks, width)
    main_matrix = pltpu.VMEM((harms * LANES, blocks * LANES), jnp.bfloat16)
    lead = pl.pallas_call(
        functools.partial(first_pack_kernel, sizes, cells),
        out_shape=payload(2 * len(GROUPS[0]) * tile + 2 * group_rows + SLOT_ROWS),
        in_specs=smem(2) + vmem(4),
        out_specs=vmem(1)[0],
        scratch_shapes=[
            main_matrix,
            pltpu.VMEM((2 * harms * LANES, blocks * LANES), jnp.bfloat16),
        ],
        compiler_params=params,
        name="pack_first",
    )(rad, triad_slots.reshape(-1), direct, adjoint, far_direct, far_adjoint)
    came = [exchanged(lead, "mode")]
    if len(GROUPS) > 1:
        shapes = [payload(2 * len(group) * tile) for group in GROUPS[1:]]
        rest = pl.pallas_call(
            functools.partial(rest_pack_kernel, sizes, cells),
            out_shape=shapes,
            in_specs=vmem(2),
            out_specs=vmem(len(shapes)),
            scratch_shapes=[main_matrix],
            compiler_params=params,
            name="pack_rest",
        )(direct, adjoint)
        came += [exchanged(value, "mode") for value in rest]

    per_harm, own_cells = blocks // harm_devices, cells // blocks
    sizes = (harms, blocks, width, groups, slots, fields, cells, harm_devices)
    listed = (max(blocks, 8), LANES)
    owned = []
    for index, group in enumerate(GROUPS):
        count = len(group)
        operands = [came[0]] + ([came[index]] if index else [])
        derived = pltpu.VMEM((2 * count, blocks * groups, cells, LANES), jnp.float32)
        sent = pl.pallas_call(
            functools.partial(triad_kernel, sizes, group),
            out_shape=jax.ShapeDtypeStruct(
                (blocks * harm_devices, per_harm, 2 * count * own_cells, LANES), jnp.float32
            ),
            in_specs=vmem(len(operands)),
            out_specs=vmem(1)[0],
            scratch_shapes=[
                pltpu.VMEM((groups, 2 * LANES, LANES), jnp.bfloat16),
                pltpu.VMEM((tile, tile), jnp.bfloat16),
                pltpu.VMEM((4, blocks * groups, cells, LANES), jnp.float32),
                derived,
                derived,
                pltpu.VMEM((blocks * slots, 2 * count, cells, LANES), jnp.float32),
                pltpu.VMEM(listed, jnp.int32),
                pltpu.SMEM(listed, jnp.int32),
                pltpu.SemaphoreType.DMA,
            ],
            compiler_params=params,
            name="triads",
        )(*operands)
        owned.append(exchanged(sent, ("mode", "harm")))

    sizes = (blocks, harm_devices, slots, width, per_harm, own_cells, fields)
    result = pl.pallas_call(
        functools.partial(unpack_kernel, sizes),
        out_shape=jax.ShapeDtypeStruct(
            (per_harm * slots, 2 * fields * own_cells, LANES), jnp.float32
        ),
        in_specs=vmem(len(owned)),
        out_specs=vmem(1)[0],
        compiler_params=params,
        name="unpack",
    )(*owned)
    return result.reshape(per_harm * slots, 2, fields, own_cells, radial)


def solution(mesh):
    return jax.shard_map(
        body,
        mesh=mesh,
        in_specs=(
            P(("case", "harm"), "mode", None, None, None, "rad"),
            P(("case", "harm"), "mode", None, None, None, "rad"),
            P("mode", None, None),
        ),
        out_specs=P(("case", "harm"), None, None, "mode", "rad"),
        check_vma=False,
    )
```

time: 99.8 us -> 72.9 us (0.73)
  blocking collectives: 0 us -> 55.8 us
  starting transfers between devices: 52.1 us -> 0.51 us
  waiting for transfers between devices: 30.6 us -> 1.93 us
  Pallas kernels: 14.2 us -> 11.3 us
    all_to_all x0 -> x2, blocking collectives: none -> 55.8 us  [exchanged(): return lax.all_to_all(value, axes, split_axis=0, concat_axis=0, tiled=True)]
    ppermute x36 -> x0, starting transfers between devices: 51.6 us -> none  [the longest x21 33.3 us: to_owners(): result.append(lax.ppermute(parts[index], ('mode', 'harm'), pairs))]
    ppermute x36 -> x0, waiting for transfers between devices: 30.6 us -> none  [the longest x21 16.2 us: to_owners(): result.append(lax.ppermute(parts[index], ('mode', 'harm'), pairs))]
    pallas_call x5 -> x2, Pallas kernels: 12.7 us -> 10.4 us  [the longest x1 7.6 us: body(): pl.pallas_call(functools.partial(triad_kernel, sizes, group), out_shape=j...]
    unnamed x11 -> x5, local copies, waits for them, and re-layouts: 2.3 us -> 2.96 us
  transfers between devices with their start and end apart: 38 -> 2, of which waited for: 11 -> 2; matrix products, arithmetic and copies ran while one was open for 0% -> 1% of each run, Pallas kernels for 9% -> 0%
where the time goes in v3:
time: 72.9 us; the launch traced here: 72.6 us
  blocking collectives  55.8 us (77%)
  Pallas kernels  11.3 us (16%)
  local copies, waits for them, and re-layouts  3.06 us (4%)
  waiting for transfers between devices  1.93 us (3%)
    all_to_all x2, blocking collectives, exchanged(): return lax.all_to_all(value, axes, split_axis=0, concat_axis=0, tiled=True)  55.8 us
    pallas_call x1, Pallas kernels, body(): pl.pallas_call(functools.partial(triad_kernel, sizes, group), out_shape=j...  7.6 us
    unnamed x5, local copies, waits for them, and re-layouts  2.96 us
    pallas_call x1, Pallas kernels, body(): pl.pallas_call(functools.partial(first_pack_kernel, sizes, cells), out_sh...  2.83 us
  transfers between devices with their start and end apart: 2, of which 2 were waited for; matrix products, arithmetic and copies ran while one was open for 1% of the time, Pallas kernels for 0%

profile of v3, /device:TPU:0, one launch (start us, length us, event | category | flops | bytes accessed | tf_op | source)
XLA Modules:
  0.0 72.6 jit_solution(5568332219298235343)
XLA Ops:
  0.0 0.5 collective-permute-start
  0.5 0.1 collective-permute-start.1
  0.5 0.8 %copy.5 = s32[4,4,2]{2,1,0:T(4,128)S(1)} copy(s32[4,4,2]{1,2,0:T(2,128)} %param.5) | data formatting | bytes 256 | tf_op args[2]
  1.3 0.1 reshape.16.slots
  1.4 1.0 %collective-permute-done.far_d = bf16[4,8,80,128]{3,2,1,0:T(8,128)(2,1)S(1)} collective-permute-done((bf16[4,8,80,128]{3,2,1,0:T(8,128)(2,1)}, bf16[4,8,80,128]{3,2,1,0:T(8,128)(2,1)S(1)}, u32[]{:S(2)}, u32[]{:S(2)}) %collective-permute-start) | collective-permute-done | bytes 655392 | tf_op jit(solution)/shard_map/ppermute | solution.py:323
  2.4 0.9 %collective-permute-done.1.far_a = bf16[4,8,80,128]{3,2,1,0:T(8,128)(2,1)S(1)} collective-permute-done((bf16[4,8,80,128]{3,2,1,0:T(8,128)(2,1)}, bf16[4,8,80,128]{3,2,1,0:T(8,128)(2,1)S(1)}, u32[]{:S(2)}, u32[]{:S(2)}) %collective-permute-start.1) | collective-permute-done | bytes 655392 | tf_op jit(solution)/shard_map/ppermute | solution.py:324
  3.3 0.0 copy-start
  3.3 1.1 %copy-done = bf16[4,4,2,5,16,128]{5,4,3,2,1,0:T(8,128)(2,1)S(1)} copy-done((bf16[4,4,2,5,16,128]{5,4,3,2,1,0:T(8,128)(2,1)S(1)}, bf16[4,4,2,5,16,128]{5,4,3,2,1,0:T(8,128)(2,1)}, u32[]{:S(2)}) %copy-start) | copy-done | bytes 655384
  4.4 0.0 copy-start.1
  4.4 1.1 %copy-done.1 = bf16[4,4,2,5,16,128]{5,4,3,2,1,0:T(8,128)(2,1)S(1)} copy-done((bf16[4,4,2,5,16,128]{5,4,3,2,1,0:T(8,128)(2,1)S(1)}, bf16[4,4,2,5,16,128]{5,4,3,2,1,0:T(8,128)(2,1)}, u32[]{:S(2)}) %copy-start.1) | copy-done | bytes 655384
  5.5 2.8 %pack_first.1 = bf16[4,1456,128]{2,1,0:T(8,128)(2,1)S(1)} custom-call(s32[1]{0:T(128)} %bitcast.rad, s32[32]{0:T(128)S(1)} %reshape.16.slots, bf16[4,8,80,128]{3,2,1,0:T(8,128)(2,1)S(1)} %bitcast.5, bf16[4,8,80,128]{3,2,1,0:T(8,128)(2,1)S(1)} %bitcast.7, bf16[4,8,80,128]{3,2,1,0:T(8,128)(2,1)S(1)} %collective-permute-done.far_d, ...), custom_call_target="tpu_custom_call" | custom-call | tf_op jit(solution)/shard_map/pack_first/pallas_call | solution.py:331
  8.3 41.5 %all_to_all.10.refs_0_ = bf16[4,1456,128]{2,1,0:T(8,128)(2,1)S(1)} all-to-all(bf16[4,1456,128]{2,1,0:T(8,128)(2,1)S(1)} %pack_first.1), channel_id=1, replica_groups=mesh['case'=2,'mode'=4,'harm'=2,'rad'=2] {'mode'}, dimensions={0} | all-to-all | bytes 2981888 | tf_op jit(solution)/shard_map/all_to_all | solution.py:308
  49.9 7.6 %triads.1 = f32[8,2,40,128]{3,2,1,0:T(8,128)S(1)} custom-call(bf16[4,1456,128]{2,1,0:T(8,128)(2,1)S(1)} %all_to_all.10.refs_0_), custom_call_target="tpu_custom_call" | custom-call | tf_op jit(solution)/shard_map/triads/pallas_call | solution.py:365
  57.5 14.3 %all_to_all.11.refs_0_ = f32[8,2,40,128]{3,2,1,0:T(8,128)S(1)} all-to-all(f32[8,2,40,128]{3,2,1,0:T(8,128)S(1)} %triads.1), channel_id=1, replica_groups=mesh['case'=2,'mode'=4,'harm'=2,'rad'=2] {'mode','harm'}, dimensions={0} | all-to-all | bytes 655360 | tf_op jit(solution)/shard_map/all_to_all | solution.py:308
  71.8 0.9 %unpack.1 = f32[8,40,128]{2,1,0:T(8,128)} custom-call(f32[8,2,40,128]{3,2,1,0:T(8,128)S(1)} %all_to_all.11.refs_0_), custom_call_target="tpu_custom_call" | custom-call | tf_op jit(solution)/shard_map/unpack/pallas_call | solution.py:389
Async XLA Ops:
  0.0 2.4 %collective-permute-start = (bf16[4,8,80,128]{3,2,1,0:T(8,128)(2,1)}, bf16[4,8,80,128]{3,2,1,0:T(8,128)(2,1)S(1)}, u32[]{:S(2)}, u32[]{:S(2)}) collective-permute-start(bf16[4,8,80,128]{3,2,1,0:T(8,128)(2,1)} %bitcast.4), channel_id=1, source_target_pairs={{0,1},{1,0},{2,3},{3,2},{4,5},{5,4},{6,7},{7,6},{8,9},{9,8},{10,11... | collective-permute-start | bytes 1966088 | tf_op jit(solution)/shard_map/ppermute | solution.py:323
  0.5 2.9 %collective-permute-start.1 = (bf16[4,8,80,128]{3,2,1,0:T(8,128)(2,1)}, bf16[4,8,80,128]{3,2,1,0:T(8,128)(2,1)S(1)}, u32[]{:S(2)}, u32[]{:S(2)}) collective-permute-start(bf16[4,8,80,128]{3,2,1,0:T(8,128)(2,1)} %bitcast.6), channel_id=1, source_target_pairs={{0,1},{1,0},{2,3},{3,2},{4,5},{5,4},{6,7},{7,6},{8,9},{9,8},{10,11... | collective-permute-start | bytes 1966088 | tf_op jit(solution)/shard_map/ppermute | solution.py:324
  3.3 1.1 %copy-start = (bf16[4,4,2,5,16,128]{5,4,3,2,1,0:T(8,128)(2,1)S(1)}, bf16[4,4,2,5,16,128]{5,4,3,2,1,0:T(8,128)(2,1)}, u32[]{:S(2)}) copy-start(bf16[4,4,2,5,16,128]{5,4,3,2,1,0:T(8,128)(2,1)} %param.3) | copy-start | bytes 1966084
  4.4 1.1 %copy-start.1 = (bf16[4,4,2,5,16,128]{5,4,3,2,1,0:T(8,128)(2,1)S(1)}, bf16[4,4,2,5,16,128]{5,4,3,2,1,0:T(8,128)(2,1)}, u32[]{:S(2)}) copy-start(bf16[4,4,2,5,16,128]{5,4,3,2,1,0:T(8,128)(2,1)} %param.4) | copy-start | bytes 1966084

commit v4 on v3

--- a/solution.py
+++ b/solution.py
@@ -12,7 +12,7 @@
 LANES = 128
 HALO = 4
 SLOT_ROWS = 16
-GROUPS = ((1, 2, 0, 3, 4),)
+GROUPS = ((1, 2), (0, 3, 4))
 VMEM_LIMIT = 40 * 1024 * 1024
 
 
@@ -50,28 +50,29 @@
     )
 
 
-def write_main(arrays, fields, cells, matrix, out):
-    groups = arrays[0].shape[1]
-    pieces = []
-    for array in arrays:
-        for field in fields:
-            rows = slice(field * cells, (field + 1) * cells)
-            pieces += [side_by_side(array, group, rows) for group in range(groups)]
-    main = jnp.dot(
-        jnp.concatenate(pieces, axis=0), matrix[...], preferred_element_type=jnp.float32
-    )
+def main_pack_kernel(sizes, pieces, *refs):
+    ins, out, matrix = refs[:pieces], refs[-2], refs[-1]
+    fill_main(matrix, sizes)
+    groups, cells = ins[0].shape[1], ins[0].shape[2]
+    rows = [side_by_side(ref, group, slice(0, cells)) for ref in ins for group in range(groups)]
+    main = jnp.dot(jnp.concatenate(rows, axis=0), matrix[...], preferred_element_type=jnp.float32)
     for owner in range(out.shape[0]):
         out[owner, 0 : main.shape[0], :] = main[:, owner * LANES : (owner + 1) * LANES].astype(
             jnp.bfloat16
         )
 
 
-def first_pack_kernel(sizes, cells, rad, slots, own_d, own_a, far_d, far_a, out, main_m, halo_m):
+def halo_pack_kernel(
+    sizes, base, rad, slots, d_hbm, a_hbm, far_d, far_a, _, out, own_d, own_a, halo_m, ends_v, sems
+):
     harms, blocks, width = sizes
     groups, group_rows = own_d.shape[1], own_d.shape[2]
-    fill_main(main_m, sizes)
-    write_main((own_d, own_a), GROUPS[0], cells, main_m, out)
-    base = 2 * len(GROUPS[0]) * groups * cells
+    loads = []
+    for array, (source, target) in enumerate(((d_hbm, own_d), (a_hbm, own_a))):
+        for k in range(harms):
+            loads.append(pltpu.make_async_copy(source.at[k], target.at[k], sems.at[array, k]))
+    for load in loads:
+        load.start()
     shift = jnp.where(rad[0] == 0, LANES, -LANES)
     depth = harms * LANES
     span_h = harms * HALO
@@ -83,6 +84,8 @@
     halo_m[depth:, :] = one_hot(same & (cell_in + shift == wanted))
     lane_group = (iota((group_rows, blocks * LANES), 1) % LANES) // span_h
     everything = slice(0, group_rows)
+    for load in loads:
+        load.wait()
     for array, (own, far) in enumerate(((own_d, far_d), (own_a, far_a))):
         pieces = [
             jnp.concatenate(
@@ -98,25 +101,23 @@
             held = jnp.where(
                 lane_group == group, ends[group * group_rows : (group + 1) * group_rows], held
             )
-        start = base + array * group_rows
+        start = array * group_rows
         for block in range(blocks):
-            out[block, start : start + group_rows, :] = held[
+            ends_v[block, start : start + group_rows, :] = held[
                 :, block * LANES : (block + 1) * LANES
             ].astype(jnp.bfloat16)
     lane = iota((SLOT_ROWS, LANES), 1)
     listed = jnp.zeros((SLOT_ROWS, LANES), jnp.int32)
     for index in range(slots.shape[0]):
         listed = jnp.where(lane == index, slots[index], listed)
-    start = base + 2 * group_rows
+    start = 2 * group_rows
     for block in range(blocks):
-        out[block, start : start + SLOT_ROWS, :] = listed.astype(jnp.float32).astype(jnp.bfloat16)
-
-
-def rest_pack_kernel(sizes, cells, own_d, own_a, *refs):
-    outs, matrix = refs[:-1], refs[-1]
-    fill_main(matrix, sizes)
-    for fields, out in zip(GROUPS[1:], outs):
-        write_main((own_d, own_a), fields, cells, matrix, out)
+        ends_v[block, start:, :] = listed.astype(jnp.float32).astype(jnp.bfloat16)
+    store = pltpu.make_async_copy(
+        ends_v, out.at[:, base : base + start + SLOT_ROWS, :], sems.at[0, harms]
+    )
+    store.start()
+    store.wait()
 
 
 def coefficient(distance):
@@ -304,6 +305,10 @@
     return [pl.BlockSpec(memory_space=pltpu.VMEM)] * count
 
 
+def anywhere(count):
+    return [pl.BlockSpec(memory_space=pl.ANY)] * count
+
+
 def exchanged(value, axes):
     return lax.all_to_all(value, axes, split_axis=0, concat_axis=0, tiled=True)
 
@@ -327,32 +332,47 @@
         return jax.ShapeDtypeStruct((blocks, rows, LANES), jnp.bfloat16)
 
     sizes = (harms, blocks, width)
-    main_matrix = pltpu.VMEM((harms * LANES, blocks * LANES), jnp.bfloat16)
+    tail = 2 * group_rows + SLOT_ROWS
+
+    def packed(group, extra, after):
+        ins = [direct] * len(group) + [adjoint] * len(group)
+        return pl.pallas_call(
+            functools.partial(main_pack_kernel, sizes, len(ins)),
+            grid=(1,),
+            out_shape=payload(len(ins) * tile + extra),
+            in_specs=[
+                pl.BlockSpec((harms, groups, cells, radial), lambda i, f=field: (0, 0, f, 0))
+                for field in group + group
+            ]
+            + anywhere(len(after)),
+            out_specs=vmem(1)[0],
+            scratch_shapes=[pltpu.VMEM((harms * LANES, blocks * LANES), jnp.bfloat16)],
+            compiler_params=params,
+            name="pack_main",
+        )(*ins, *after)
+
+    lead = packed(GROUPS[0], tail, [])
     lead = pl.pallas_call(
-        functools.partial(first_pack_kernel, sizes, cells),
-        out_shape=payload(2 * len(GROUPS[0]) * tile + 2 * group_rows + SLOT_ROWS),
-        in_specs=smem(2) + vmem(4),
-        out_specs=vmem(1)[0],
+        functools.partial(halo_pack_kernel, sizes, 2 * len(GROUPS[0]) * tile),
+        out_shape=jax.ShapeDtypeStruct(lead.shape, lead.dtype),
+        in_specs=smem(2) + anywhere(2) + vmem(2) + anywhere(1),
+        out_specs=anywhere(1)[0],
         scratch_shapes=[
-            main_matrix,
+            pltpu.VMEM(direct.shape, jnp.bfloat16),
+            pltpu.VMEM(adjoint.shape, jnp.bfloat16),
             pltpu.VMEM((2 * harms * LANES, blocks * LANES), jnp.bfloat16),
+            pltpu.VMEM((blocks, tail, LANES), jnp.bfloat16),
+            pltpu.SemaphoreType.DMA((2, harms + 1)),
         ],
+        input_output_aliases={6: 0},
         compiler_params=params,
-        name="pack_first",
-    )(rad, triad_slots.reshape(-1), direct, adjoint, far_direct, far_adjoint)
+        name="pack_halos",
+    )(rad, triad_slots.reshape(-1), direct, adjoint, far_direct, far_adjoint, lead)
     came = [exchanged(lead, "mode")]
-    if len(GROUPS) > 1:
-        shapes = [payload(2 * len(group) * tile) for group in GROUPS[1:]]
-        rest = pl.pallas_call(
-            functools.partial(rest_pack_kernel, sizes, cells),
-            out_shape=shapes,
-            in_specs=vmem(2),
-            out_specs=vmem(len(shapes)),
-            scratch_shapes=[main_matrix],
-            compiler_params=params,
-            name="pack_rest",
-        )(direct, adjoint)
-        came += [exchanged(value, "mode") for value in rest]
+    last = lead
+    for group in GROUPS[1:]:
+        last = packed(group, 0, [last])
+        came.append(exchanged(last, "mode"))
 
     per_harm, own_cells = blocks // harm_devices, cells // blocks
     sizes = (harms, blocks, width, groups, slots, fields, cells, harm_devices)

time: 72.9 us -> 80 us (1.097)
  blocking collectives: 55.8 us -> 10.6 us
  waiting for transfers between devices: 1.93 us -> 35.5 us
  starting transfers between devices: 0.51 us -> 14 us
  Pallas kernels: 11.3 us -> 16.9 us
    all_to_all x2 -> x1, blocking collectives: 55.8 us -> 10.6 us  [exchanged(): return lax.all_to_all(value, axes, split_axis=0, concat_axis=0, tiled=True)]
    all_to_all x0 -> x3, waiting for transfers between devices: none -> 35.5 us  [exchanged(): return lax.all_to_all(value, axes, split_axis=0, concat_axis=0, tiled=True)]
    all_to_all x0 -> x3, starting transfers between devices: none -> 13.5 us  [exchanged(): return lax.all_to_all(value, axes, split_axis=0, concat_axis=0, tiled=True)]
    pallas_call x1 -> x3, Pallas kernels: 2.83 us -> 7.63 us  [the longest x1 4.74 us: body(): pl.pallas_call(functools.partial(halo_pack_kernel, sizes, 2 * len(GROUPS[...]
    ppermute x1, waiting for transfers between devices: 0.99 us -> 0.01 us  [body(): far_direct = lax.ppermute(direct, 'rad', swap)]
    ppermute x1, waiting for transfers between devices: 0.94 us -> 0.01 us  [body(): far_adjoint = lax.ppermute(adjoint, 'rad', swap)]
    pallas_call x1 -> x2, Pallas kernels: 7.6 us -> 8.41 us  [body(): pl.pallas_call(functools.partial(triad_kernel, sizes, group), out_shape=j...]
    unnamed x5 -> x11, local copies, waits for them, and re-layouts: 2.96 us -> 2.29 us
  transfers between devices with their start and end apart: 2 -> 5, of which waited for: 2 -> 3; matrix products, arithmetic and copies ran while one was open for 1% -> 0% of each run, Pallas kernels for 0% -> 14%
where the time goes in v4:
time: 80 us; the launch traced here: 79.5 us
  waiting for transfers between devices  35.5 us (44%)
  Pallas kernels  16.9 us (21%)
  starting transfers between devices  14 us (18%)
  blocking collectives  10.6 us (13%)
  local copies, waits for them, and re-layouts  2.39 us (3%)
    all_to_all x3, waiting for transfers between devices, exchanged(): return lax.all_to_all(value, axes, split_axis=0, concat_axis=0, tiled=True)  35.5 us
    all_to_all x3, starting transfers between devices, exchanged(): return lax.all_to_all(value, axes, split_axis=0, concat_axis=0, tiled=True)  13.5 us
    all_to_all x1, blocking collectives, exchanged(): return lax.all_to_all(value, axes, split_axis=0, concat_axis=0, tiled=True)  10.6 us
    pallas_call x2, Pallas kernels, body(): pl.pallas_call(functools.partial(triad_kernel, sizes, group), out_shape=j...  8.41 us
    pallas_call x1, Pallas kernels, body(): pl.pallas_call(functools.partial(halo_pack_kernel, sizes, 2 * len(GROUPS[...  4.74 us
    pallas_call x2, Pallas kernels, packed(): pl.pallas_call(functools.partial(main_pack_kernel, sizes, len(ins)), grid...  2.88 us
    unnamed x11, local copies, waits for them, and re-layouts  2.29 us
  transfers between devices with their start and end apart: 5, of which 3 were waited for; matrix products, arithmetic and copies ran while one was open for 0% of the time, Pallas kernels for 14%

profile of v4, /device:TPU:0, one launch (start us, length us, event | category | flops | bytes accessed | tf_op | source)
XLA Modules:
  0.0 79.5 jit_solution(10806678450660854870)
XLA Ops:
  0.0 0.5 collective-permute-start
  0.5 0.1 collective-permute-start.1
  0.5 0.0 copy-start
  0.5 1.1 %copy-done = bf16[4,4,2,5,16,128]{5,4,3,2,1,0:T(8,128)(2,1)S(1)} copy-done((bf16[4,4,2,5,16,128]{5,4,3,2,1,0:T(8,128)(2,1)S(1)}, bf16[4,4,2,5,16,128]{5,4,3,2,1,0:T(8,128)(2,1)}, u32[]{:S(2)}) %copy-start) | copy-done | bytes 655384
  1.6 0.0 copy-start.2
  1.6 1.1 %copy-done.2 = bf16[4,4,2,5,16,128]{5,4,3,2,1,0:T(8,128)(2,1)S(1)} copy-done((bf16[4,4,2,5,16,128]{5,4,3,2,1,0:T(8,128)(2,1)S(1)}, bf16[4,4,2,5,16,128]{5,4,3,2,1,0:T(8,128)(2,1)}, u32[]{:S(2)}) %copy-start.2) | copy-done | bytes 655384
  2.7 0.0 copy-start.4
  2.7 0.0 copy-start.1
  2.7 0.0 copy-start.3
  2.7 1.4 %pack_main.2._ = bf16[4,688,128]{2,1,0:T(8,128)(2,1)} custom-call(bf16[4,8,80,128]{3,2,1,0:T(8,128)(2,1)S(1)} %bitcast.5, bf16[4,8,80,128]{3,2,1,0:T(8,128)(2,1)S(1)} %bitcast.6, bf16[4,8,80,128]{3,2,1,0:T(8,128)(2,1)S(1)} %bitcast.12, bf16[4,8,80,128]{3,2,1,0:T(8,128)(2,1)S(1)} %bitcast.13), custom_call_target="tpu_custom_call" | custom-call | tf_op jit(solution)/shard_map/pack_main/pallas_call | solution.py:339
  4.1 0.0 copy-done.4
  4.1 0.1 copy.6
  4.2 0.1 reshape.16.slots
  4.3 0.0 collective-permute-done.far_d
  4.3 0.0 collective-permute-done.1.far_a
  4.3 0.0 copy-done.1
  4.3 0.0 copy-done.3
  4.3 4.7 %pack_halos.1.refs_6_ = bf16[4,688,128]{2,1,0:T(8,128)(2,1)} custom-call(s32[1]{0:T(128)} %bitcast.rad, s32[32]{0:T(128)S(1)} %reshape.16.slots, bf16[4,8,80,128]{3,2,1,0:T(8,128)(2,1)S(1)} %bitcast.7, bf16[4,8,80,128]{3,2,1,0:T(8,128)(2,1)S(1)} %bitcast.14, bf16[4,8,80,128]{3,2,1,0:T(8,128)(2,1)S(1)} %collective-permute-done.far_d, ...), custom_call_target="tpu_custom_call", output_to_operand_aliasing={{}: (6, {})} | custom-call | tf_op jit(solution)/shard_map/pack_halos/pallas_call | solution.py:355
  9.1 6.3 %all-to-all-start = ((bf16[4,688,128]{2,1,0:T(8,128)(2,1)}), bf16[4,688,128]{2,1,0:T(8,128)(2,1)S(1)}, u32[]{:S(2)}, u32[]{:S(2)}) async-start(bf16[4,688,128]{2,1,0:T(8,128)(2,1)} %pack_halos.1.refs_6_), calls=%async_computation | async-start | bytes 1409024 | tf_op jit(solution)/shard_map/all_to_all | solution.py:313
  15.4 1.5 %pack_main.3 = bf16[4,768,128]{2,1,0:T(8,128)(2,1)} custom-call(bf16[4,8,80,128]{3,2,1,0:T(8,128)(2,1)S(1)} %bitcast.8, bf16[4,8,80,128]{3,2,1,0:T(8,128)(2,1)S(1)} %bitcast.9, bf16[4,8,80,128]{3,2,1,0:T(8,128)(2,1)S(1)} %bitcast.10, bf16[4,8,80,128]{3,2,1,0:T(8,128)(2,1)S(1)} %bitcast.15, bf16[4,8,80,128]{3,2,1,0:T(8,128)(2,1)S(1)} %bitcast.16, ...), custom_call_target="tpu_custom_call" | custom-call | tf_op jit(solution)/shard_map/pack_main/pallas_call | solution.py:339
  16.9 17.0 %all-to-all-done.refs_0_ = bf16[4,688,128]{2,1,0:T(8,128)(2,1)S(1)} async-done(((bf16[4,688,128]{2,1,0:T(8,128)(2,1)}), bf16[4,688,128]{2,1,0:T(8,128)(2,1)S(1)}, u32[]{:S(2)}, u32[]{:S(2)}) %all-to-all-start) | async-done | bytes 704544 | tf_op jit(solution)/shard_map/all_to_all | solution.py:313
  33.9 3.5 %all-to-all-start.2 = ((bf16[4,768,128]{2,1,0:T(8,128)(2,1)}), bf16[4,768,128]{2,1,0:T(8,128)(2,1)S(1)}, u32[]{:S(2)}, u32[]{:S(2)}) async-start(bf16[4,768,128]{2,1,0:T(8,128)(2,1)} %pack_main.3), calls=%async_computation.2 | async-start | bytes 1572864 | tf_op jit(solution)/shard_map/all_to_all | solution.py:313
  37.4 4.0 %triads.2 = f32[8,2,16,128]{3,2,1,0:T(8,128)} custom-call(bf16[4,688,128]{2,1,0:T(8,128)(2,1)S(1)} %all-to-all-done.refs_0_), custom_call_target="tpu_custom_call" | custom-call | tf_op jit(solution)/shard_map/triads/pallas_call | solution.py:385
  41.4 15.6 %all-to-all-done.2.refs_1_ = bf16[4,768,128]{2,1,0:T(8,128)(2,1)S(1)} async-done(((bf16[4,768,128]{2,1,0:T(8,128)(2,1)}), bf16[4,768,128]{2,1,0:T(8,128)(2,1)S(1)}, u32[]{:S(2)}, u32[]{:S(2)}) %all-to-all-start.2) | async-done | bytes 786464 | tf_op jit(solution)/shard_map/all_to_all | solution.py:313
  57.0 3.7 %all-to-all-start.1 = ((f32[8,2,16,128]{3,2,1,0:T(8,128)}), f32[8,2,16,128]{3,2,1,0:T(8,128)S(1)}, u32[]{:S(2)}, u32[]{:S(2)}) async-start(f32[8,2,16,128]{3,2,1,0:T(8,128)} %triads.2), calls=%async_computation.1 | async-start | bytes 262144 | tf_op jit(solution)/shard_map/all_to_all | solution.py:313
  60.7 4.4 %triads.3 = f32[8,2,24,128]{3,2,1,0:T(8,128)S(1)} custom-call(bf16[4,688,128]{2,1,0:T(8,128)(2,1)S(1)} %all-to-all-done.refs_0_, bf16[4,768,128]{2,1,0:T(8,128)(2,1)S(1)} %all-to-all-done.2.refs_1_), custom_call_target="tpu_custom_call" | custom-call | tf_op jit(solution)/shard_map/triads/pallas_call | solution.py:385
  65.1 2.9 %all-to-all-done.1.refs_0_ = f32[8,2,16,128]{3,2,1,0:T(8,128)S(1)} async-done(((f32[8,2,16,128]{3,2,1,0:T(8,128)}), f32[8,2,16,128]{3,2,1,0:T(8,128)S(1)}, u32[]{:S(2)}, u32[]{:S(2)}) %all-to-all-start.1) | async-done | bytes 131104 | tf_op jit(solution)/shard_map/all_to_all | solution.py:313
  68.0 10.6 %all_to_all.20.refs_1_ = f32[8,2,24,128]{3,2,1,0:T(8,128)S(1)} all-to-all(f32[8,2,24,128]{3,2,1,0:T(8,128)S(1)} %triads.3), channel_id=1, replica_groups=mesh['case'=2,'mode'=4,'harm'=2,'rad'=2] {'mode','harm'}, dimensions={0} | all-to-all | bytes 393216 | tf_op jit(solution)/shard_map/all_to_all | solution.py:313
  78.7 0.9 %unpack.1 = f32[8,40,128]{2,1,0:T(8,128)} custom-call(f32[8,2,16,128]{3,2,1,0:T(8,128)S(1)} %all-to-all-done.1.refs_0_, f32[8,2,24,128]{3,2,1,0:T(8,128)S(1)} %all_to_all.20.refs_1_), custom_call_target="tpu_custom_call" | custom-call | tf_op jit(solution)/shard_map/unpack/pallas_call | solution.py:409
Async XLA Ops:
  0.0 4.3 %collective-permute-start = (bf16[4,8,80,128]{3,2,1,0:T(8,128)(2,1)}, bf16[4,8,80,128]{3,2,1,0:T(8,128)(2,1)S(1)}, u32[]{:S(2)}, u32[]{:S(2)}) collective-permute-start(bf16[4,8,80,128]{3,2,1,0:T(8,128)(2,1)} %bitcast.4), channel_id=1, source_target_pairs={{0,1},{1,0},{2,3},{3,2},{4,5},{5,4},{6,7},{7,6},{8,9},{9,8},{10,11... | collective-permute-start | bytes 1966088 | tf_op jit(solution)/shard_map/ppermute | solution.py:328
  0.5 3.8 %collective-permute-start.1 = (bf16[4,8,80,128]{3,2,1,0:T(8,128)(2,1)}, bf16[4,8,80,128]{3,2,1,0:T(8,128)(2,1)S(1)}, u32[]{:S(2)}, u32[]{:S(2)}) collective-permute-start(bf16[4,8,80,128]{3,2,1,0:T(8,128)(2,1)} %bitcast.11), channel_id=1, source_target_pairs={{0,1},{1,0},{2,3},{3,2},{4,5},{5,4},{6,7},{7,6},{8,9},{9,8},{10,11... | collective-permute-start | bytes 1966088 | tf_op jit(solution)/shard_map/ppermute | solution.py:329
  0.5 1.1 %copy-start = (bf16[4,4,2,5,16,128]{5,4,3,2,1,0:T(8,128)(2,1)S(1)}, bf16[4,4,2,5,16,128]{5,4,3,2,1,0:T(8,128)(2,1)}, u32[]{:S(2)}) copy-start(bf16[4,4,2,5,16,128]{5,4,3,2,1,0:T(8,128)(2,1)} %param.3) | copy-start | bytes 1966084
  1.6 1.1 %copy-start.2 = (bf16[4,4,2,5,16,128]{5,4,3,2,1,0:T(8,128)(2,1)S(1)}, bf16[4,4,2,5,16,128]{5,4,3,2,1,0:T(8,128)(2,1)}, u32[]{:S(2)}) copy-start(bf16[4,4,2,5,16,128]{5,4,3,2,1,0:T(8,128)(2,1)} %param.4) | copy-start | bytes 1966084
  2.7 1.4 %copy-start.4 = (s32[4,4,2]{1,2,0:T(2,128)S(1)}, s32[4,4,2]{1,2,0:T(2,128)}, u32[]{:S(2)}) copy-start(s32[4,4,2]{1,2,0:T(2,128)} %param.5) | copy-start | bytes 388
  2.7 1.6 %copy-start.1 = (bf16[4,4,2,5,16,128]{5,4,3,2,1,0:T(8,128)(2,1)S(1)}, bf16[4,4,2,5,16,128]{5,4,3,2,1,0:T(8,128)(2,1)}, u32[]{:S(2)}) copy-start(bf16[4,4,2,5,16,128]{5,4,3,2,1,0:T(8,128)(2,1)} %param.3) | copy-start | bytes 1966084
  2.7 1.6 %copy-start.3 = (bf16[4,4,2,5,16,128]{5,4,3,2,1,0:T(8,128)(2,1)S(1)}, bf16[4,4,2,5,16,128]{5,4,3,2,1,0:T(8,128)(2,1)}, u32[]{:S(2)}) copy-start(bf16[4,4,2,5,16,128]{5,4,3,2,1,0:T(8,128)(2,1)} %param.4) | copy-start | bytes 1966084
  9.1 24.9 %all-to-all-start = ((bf16[4,688,128]{2,1,0:T(8,128)(2,1)}), bf16[4,688,128]{2,1,0:T(8,128)(2,1)S(1)}, u32[]{:S(2)}, u32[]{:S(2)}) async-start(bf16[4,688,128]{2,1,0:T(8,128)(2,1)} %pack_halos.1.refs_6_), calls=%async_computation | async-start | bytes 1409024 | tf_op jit(solution)/shard_map/all_to_all | solution.py:313
  33.9 23.1 %all-to-all-start.2 = ((bf16[4,768,128]{2,1,0:T(8,128)(2,1)}), bf16[4,768,128]{2,1,0:T(8,128)(2,1)S(1)}, u32[]{:S(2)}, u32[]{:S(2)}) async-start(bf16[4,768,128]{2,1,0:T(8,128)(2,1)} %pack_main.3), calls=%async_computation.2 | async-start | bytes 1572864 | tf_op jit(solution)/shard_map/all_to_all | solution.py:313
  57.0 11.0 %all-to-all-start.1 = ((f32[8,2,16,128]{3,2,1,0:T(8,128)}), f32[8,2,16,128]{3,2,1,0:T(8,128)S(1)}, u32[]{:S(2)}, u32[]{:S(2)}) async-start(f32[8,2,16,128]{3,2,1,0:T(8,128)} %triads.2), calls=%async_computation.1 | async-start | bytes 262144 | tf_op jit(solution)/shard_map/all_to_all | solution.py:313

commit v5 on v3

--- a/solution.py
+++ b/solution.py
@@ -12,7 +12,7 @@
 LANES = 128
 HALO = 4
 SLOT_ROWS = 16
-GROUPS = ((1, 2, 0, 3, 4),)
+GROUPS = ((1, 2), (0, 3, 4))
 VMEM_LIMIT = 40 * 1024 * 1024
 
 
@@ -32,50 +32,57 @@
     return jnp.where(index >= count, index - count, index)
 
 
-def columns(harms, blocks):
+def columns(harms, blocks, first):
     shape = (harms * LANES, blocks * LANES)
     row, col = iota(shape, 0), iota(shape, 1)
-    return row // LANES, row % LANES, col // LANES, col % LANES
+    owner = wrapped(col // LANES + first, blocks)
+    return row // LANES, row % LANES, owner, col % LANES
 
 
 def side_by_side(ref, group, rows):
     return jnp.concatenate([ref[k, group, rows, :] for k in range(ref.shape[0])], axis=1)
 
 
-def fill_main(matrix, sizes):
+def fill_main(matrix, sizes, first):
     harms, blocks, width = sizes
-    harm_in, cell_in, owner, lane = columns(harms, blocks)
+    harm_in, cell_in, owner, lane = columns(harms, blocks, first)
     matrix[...] = one_hot(
         (lane // width == harm_in) & (cell_in == owner * width + lane % width)
     )
 
 
-def write_main(arrays, fields, cells, matrix, out):
-    groups = arrays[0].shape[1]
-    pieces = []
-    for array in arrays:
+def main_slabs(sizes, fields, first, own_d, own_a, matrix, cells):
+    fill_main(matrix, sizes, first)
+    rows = []
+    for ref in (own_d, own_a):
         for field in fields:
-            rows = slice(field * cells, (field + 1) * cells)
-            pieces += [side_by_side(array, group, rows) for group in range(groups)]
-    main = jnp.dot(
-        jnp.concatenate(pieces, axis=0), matrix[...], preferred_element_type=jnp.float32
-    )
-    for owner in range(out.shape[0]):
-        out[owner, 0 : main.shape[0], :] = main[:, owner * LANES : (owner + 1) * LANES].astype(
-            jnp.bfloat16
-        )
-
-
-def first_pack_kernel(sizes, cells, rad, slots, own_d, own_a, far_d, far_a, out, main_m, halo_m):
+            piece = slice(field * cells, (field + 1) * cells)
+            rows += [side_by_side(ref, group, piece) for group in range(ref.shape[1])]
+    main = jnp.dot(jnp.concatenate(rows, axis=0), matrix[...], preferred_element_type=jnp.float32)
+    main = main.astype(jnp.bfloat16)
+    return [main[:, owner * LANES : (owner + 1) * LANES] for owner in range(sizes[1])]
+
+
+def lead_pack_kernel(sizes, cells, own_d, own_a, out, matrix):
+    slabs = main_slabs(sizes, GROUPS[0], 0, own_d, own_a, matrix, cells)
+    for owner, slab in enumerate(slabs):
+        out[owner] = slab
+
+
+def group_pack_kernel(sizes, cells, fields, mode, own_d, own_a, _, *refs):
+    slabs = main_slabs(sizes, fields, mode[0], own_d, own_a, refs[-1], cells)
+    for out, slab in zip(refs[:-1], slabs):
+        out[...] = slab
+
+
+def halo_pack_kernel(sizes, base, rad, slots, own_d, own_a, far_d, far_a, lead, out, halo_m):
     harms, blocks, width = sizes
     groups, group_rows = own_d.shape[1], own_d.shape[2]
-    fill_main(main_m, sizes)
-    write_main((own_d, own_a), GROUPS[0], cells, main_m, out)
-    base = 2 * len(GROUPS[0]) * groups * cells
+    out[:, 0:base, :] = lead[...]
     shift = jnp.where(rad[0] == 0, LANES, -LANES)
     depth = harms * LANES
     span_h = harms * HALO
-    harm_in, cell_in, owner, lane = columns(harms, blocks)
+    harm_in, cell_in, owner, lane = columns(harms, blocks, 0)
     part = lane % span_h
     wanted = owner * width + halo_offset(part % HALO, width)
     same = (part // HALO == harm_in) & (lane < groups * span_h)
@@ -112,13 +119,6 @@
         out[block, start : start + SLOT_ROWS, :] = listed.astype(jnp.float32).astype(jnp.bfloat16)
 
 
-def rest_pack_kernel(sizes, cells, own_d, own_a, *refs):
-    outs, matrix = refs[:-1], refs[-1]
-    fill_main(matrix, sizes)
-    for fields, out in zip(GROUPS[1:], outs):
-        write_main((own_d, own_a), fields, cells, matrix, out)
-
-
 def coefficient(distance):
     near = jnp.where(distance == 1, 8.0, jnp.where(distance == -1, -8.0, 0.0))
     return jnp.where(distance == 2, -1.0, jnp.where(distance == -2, 1.0, near))
@@ -127,8 +127,10 @@
 def triad_kernel(sizes, fields, *refs):
     harms, blocks, width, groups, slots, all_fields, cells, harm_devices = sizes
     first = fields == GROUPS[0]
-    lead, main = refs[0], refs[0 if first else 1]
-    at = 1 if first else 2
+    mode, lead = refs[:2]
+    mains = [lead.at[block] for block in range(blocks)] if first else refs[2 : 2 + blocks]
+    origins = [step if first else wrapped(mode[0] - step + blocks, blocks) for step in range(blocks)]
+    at = 2 if first else 2 + blocks
     out, radial_m, axial_m, plain_v, axial_v, radial_v, sums, slots_v, slots_s, slots_sem = refs[at:]
     halo_row = 2 * len(GROUPS[0]) * groups * cells
     slot_row = halo_row + 2 * all_fields * cells
@@ -168,8 +170,8 @@
                     pieces.append(
                         jnp.concatenate(
                             [
-                                main[step, start : start + cells, :],
-                                lead[step, beside : beside + cells, :],
+                                mains[step][start : start + cells, :],
+                                lead[origins[step], beside : beside + cells, :],
                             ],
                             axis=1,
                         )
@@ -181,18 +183,18 @@
         for array in range(2):
             for local in range(count):
                 for step in range(blocks):
-                    radial_v[array * count + local, step * groups + group] = slopes[
+                    radial_v[array * count + local, origins[step] * groups + group] = slopes[
                         index * cells : (index + 1) * cells, :
                     ]
                     index += 1
     for step in range(blocks):
         for local in range(count):
             starts = [(array * count + local) * tile for array in range(2)]
-            both = jnp.concatenate([main[step, s : s + tile, :] for s in starts], axis=1)
+            both = jnp.concatenate([mains[step][s : s + tile, :] for s in starts], axis=1)
             slopes = jnp.dot(axial_m[...], both, preferred_element_type=jnp.float32)
             for array in range(2):
                 for group in range(groups):
-                    axial_v[array * count + local, step * groups + group] = slopes[
+                    axial_v[array * count + local, origins[step] * groups + group] = slopes[
                         group * cells : (group + 1) * cells, array * LANES : (array + 1) * LANES
                     ]
         for which in range(4):
@@ -304,6 +306,19 @@
     return [pl.BlockSpec(memory_space=pltpu.VMEM)] * count
 
 
+def anywhere(count):
+    return [pl.BlockSpec(memory_space=pl.ANY)] * count
+
+
+def moved_up(values, axis):
+    count = lax.axis_size(axis)
+    result = [values[0]]
+    for step in range(1, count):
+        pairs = [(source, (source + step) % count) for source in range(count)]
+        result.append(lax.ppermute(values[step], axis, pairs))
+    return result
+
+
 def exchanged(value, axes):
     return lax.all_to_all(value, axes, split_axis=0, concat_axis=0, tiled=True)
 
@@ -315,7 +330,7 @@
     groups, group_rows = slots * parts, fields * cells
     tile = groups * cells
     params = pltpu.CompilerParams(vmem_limit_bytes=VMEM_LIMIT)
-    rad = lax.axis_index("rad").astype(jnp.int32).reshape(1)
+    mode, rad = (lax.axis_index(axis).astype(jnp.int32).reshape(1) for axis in ("mode", "rad"))
 
     direct = direct_field.reshape(harms, groups, group_rows, radial)
     adjoint = adjoint_field.reshape(harms, groups, group_rows, radial)
@@ -323,36 +338,42 @@
     far_direct = lax.ppermute(direct, "rad", swap)
     far_adjoint = lax.ppermute(adjoint, "rad", swap)
 
-    def payload(rows):
-        return jax.ShapeDtypeStruct((blocks, rows, LANES), jnp.bfloat16)
-
     sizes = (harms, blocks, width)
-    main_matrix = pltpu.VMEM((harms * LANES, blocks * LANES), jnp.bfloat16)
+    tail = 2 * group_rows + SLOT_ROWS
+
+    matrix = pltpu.VMEM((harms * LANES, blocks * LANES), jnp.bfloat16)
+    base = 2 * len(GROUPS[0]) * tile
     lead = pl.pallas_call(
-        functools.partial(first_pack_kernel, sizes, cells),
-        out_shape=payload(2 * len(GROUPS[0]) * tile + 2 * group_rows + SLOT_ROWS),
-        in_specs=smem(2) + vmem(4),
+        functools.partial(lead_pack_kernel, sizes, cells),
+        out_shape=jax.ShapeDtypeStruct((blocks, base, LANES), jnp.bfloat16),
+        in_specs=vmem(2),
         out_specs=vmem(1)[0],
-        scratch_shapes=[
-            main_matrix,
-            pltpu.VMEM((2 * harms * LANES, blocks * LANES), jnp.bfloat16),
-        ],
+        scratch_shapes=[matrix],
         compiler_params=params,
-        name="pack_first",
-    )(rad, triad_slots.reshape(-1), direct, adjoint, far_direct, far_adjoint)
-    came = [exchanged(lead, "mode")]
-    if len(GROUPS) > 1:
-        shapes = [payload(2 * len(group) * tile) for group in GROUPS[1:]]
-        rest = pl.pallas_call(
-            functools.partial(rest_pack_kernel, sizes, cells),
-            out_shape=shapes,
-            in_specs=vmem(2),
-            out_specs=vmem(len(shapes)),
-            scratch_shapes=[main_matrix],
+        name="pack_lead",
+    )(direct, adjoint)
+    lead = pl.pallas_call(
+        functools.partial(halo_pack_kernel, sizes, base),
+        out_shape=jax.ShapeDtypeStruct((blocks, base + tail, LANES), jnp.bfloat16),
+        in_specs=smem(2) + vmem(4) + vmem(1),
+        out_specs=vmem(1)[0],
+        scratch_shapes=[pltpu.VMEM((2 * harms * LANES, blocks * LANES), jnp.bfloat16)],
+        compiler_params=params,
+        name="pack_halos",
+    )(rad, triad_slots.reshape(-1), direct, adjoint, far_direct, far_adjoint, lead)
+    came = [[exchanged(lead, "mode")]]
+    for group in GROUPS[1:]:
+        slab = jax.ShapeDtypeStruct((2 * len(group) * tile, LANES), jnp.bfloat16)
+        slabs = pl.pallas_call(
+            functools.partial(group_pack_kernel, sizes, cells, group),
+            out_shape=[slab] * blocks,
+            in_specs=smem(1) + vmem(2) + anywhere(1),
+            out_specs=vmem(blocks),
+            scratch_shapes=[matrix],
             compiler_params=params,
-            name="pack_rest",
-        )(direct, adjoint)
-        came += [exchanged(value, "mode") for value in rest]
+            name="pack_group",
+        )(mode, direct, adjoint, lead)
+        came.append(moved_up(slabs, "mode"))
 
     per_harm, own_cells = blocks // harm_devices, cells // blocks
     sizes = (harms, blocks, width, groups, slots, fields, cells, harm_devices)
@@ -360,14 +381,14 @@
     owned = []
     for index, group in enumerate(GROUPS):
         count = len(group)
-        operands = [came[0]] + ([came[index]] if index else [])
+        operands = came[0] + (came[index] if index else [])
         derived = pltpu.VMEM((2 * count, blocks * groups, cells, LANES), jnp.float32)
         sent = pl.pallas_call(
             functools.partial(triad_kernel, sizes, group),
             out_shape=jax.ShapeDtypeStruct(
                 (blocks * harm_devices, per_harm, 2 * count * own_cells, LANES), jnp.float32
             ),
-            in_specs=vmem(len(operands)),
+            in_specs=smem(1) + vmem(len(operands)),
             out_specs=vmem(1)[0],
             scratch_shapes=[
                 pltpu.VMEM((groups, 2 * LANES, LANES), jnp.bfloat16),
@@ -382,7 +403,7 @@
             ],
             compiler_params=params,
             name="triads",
-        )(*operands)
+        )(mode, *operands)
         owned.append(exchanged(sent, ("mode", "harm")))
 
     sizes = (blocks, harm_devices, slots, width, per_harm, own_cells, fields)

time: 72.9 us -> 78.8 us (1.081)
  blocking collectives: 55.8 us -> 14.4 us
  waiting for transfers between devices: 1.93 us -> 31.2 us
  starting transfers between devices: 0.51 us -> 16.4 us
  Pallas kernels: 11.3 us -> 13.4 us
    all_to_all x2 -> x1, blocking collectives: 55.8 us -> 14.4 us  [exchanged(): return lax.all_to_all(value, axes, split_axis=0, concat_axis=0, tiled=True)]
    all_to_all x0 -> x2, waiting for transfers between devices: none -> 18.5 us  [exchanged(): return lax.all_to_all(value, axes, split_axis=0, concat_axis=0, tiled=True)]
    ppermute x0 -> x3, waiting for transfers between devices: none -> 12.6 us  [moved_up(): result.append(lax.ppermute(values[step], axis, pairs))]
    all_to_all x0 -> x2, starting transfers between devices: none -> 9.98 us  [exchanged(): return lax.all_to_all(value, axes, split_axis=0, concat_axis=0, tiled=True)]
    ppermute x0 -> x3, starting transfers between devices: none -> 5.9 us  [moved_up(): result.append(lax.ppermute(values[step], axis, pairs))]
    pallas_call x1 -> x3, Pallas kernels: 2.83 us -> 4.13 us  [the longest x1 3.01 us: body(): pl.pallas_call(functools.partial(halo_pack_kernel, sizes, base), out_shap...]
    ppermute x1, waiting for transfers between devices: 0.99 us -> 0.01 us  [body(): far_direct = lax.ppermute(direct, 'rad', swap)]
    ppermute x1, waiting for transfers between devices: 0.94 us -> 0.01 us  [body(): far_adjoint = lax.ppermute(adjoint, 'rad', swap)]
  transfers between devices with their start and end apart: 2 -> 7, of which waited for: 2 -> 3; matrix products, arithmetic and copies ran while one was open for 1% -> 0% of each run, Pallas kernels for 0% -> 7%
where the time goes in v5:
time: 78.8 us; the launch traced here: 78.4 us
  waiting for transfers between devices  31.2 us (40%)
  starting transfers between devices  16.4 us (21%)
  blocking collectives  14.4 us (18%)
  Pallas kernels  13.4 us (17%)
  local copies, waits for them, and re-layouts  2.94 us (4%)
    all_to_all x2, waiting for transfers between devices, exchanged(): return lax.all_to_all(value, axes, split_axis=0, concat_axis=0, tiled=True)  18.5 us
    all_to_all x1, blocking collectives, exchanged(): return lax.all_to_all(value, axes, split_axis=0, concat_axis=0, tiled=True)  14.4 us
    ppermute x3, waiting for transfers between devices, moved_up(): result.append(lax.ppermute(values[step], axis, pairs))  12.6 us
    all_to_all x2, starting transfers between devices, exchanged(): return lax.all_to_all(value, axes, split_axis=0, concat_axis=0, tiled=True)  9.98 us
    pallas_call x2, Pallas kernels, body(): pl.pallas_call(functools.partial(triad_kernel, sizes, group), out_shape=j...  8.43 us
    ppermute x3, starting transfers between devices, moved_up(): result.append(lax.ppermute(values[step], axis, pairs))  5.9 us
    pallas_call x1, Pallas kernels, body(): pl.pallas_call(functools.partial(halo_pack_kernel, sizes, base), out_shap...  3.01 us
    unnamed x11, local copies, waits for them, and re-layouts  2.85 us
  transfers between devices with their start and end apart: 7, of which 3 were waited for; matrix products, arithmetic and copies ran while one was open for 0% of the time, Pallas kernels for 7%

profile of v5, /device:TPU:0, one launch (start us, length us, event | category | flops | bytes accessed | tf_op | source)
XLA Modules:
  0.0 78.4 jit_solution(18001149659121032323)
XLA Ops:
  0.0 0.5 collective-permute-start
  0.5 0.1 collective-permute-start.1
  0.5 0.0 copy-start
  0.5 1.1 %copy-done = bf16[4,4,2,5,16,128]{5,4,3,2,1,0:T(8,128)(2,1)S(1)} copy-done((bf16[4,4,2,5,16,128]{5,4,3,2,1,0:T(8,128)(2,1)S(1)}, bf16[4,4,2,5,16,128]{5,4,3,2,1,0:T(8,128)(2,1)}, u32[]{:S(2)}) %copy-start) | copy-done | bytes 655384
  1.6 0.0 copy-start.2
  1.6 1.1 %copy-done.2 = bf16[4,4,2,5,16,128]{5,4,3,2,1,0:T(8,128)(2,1)S(1)} copy-done((bf16[4,4,2,5,16,128]{5,4,3,2,1,0:T(8,128)(2,1)S(1)}, bf16[4,4,2,5,16,128]{5,4,3,2,1,0:T(8,128)(2,1)}, u32[]{:S(2)}) %copy-start.2) | copy-done | bytes 655384
  2.7 0.0 copy-start.4
  2.7 0.0 copy-start.1
  2.7 0.0 copy-start.3
  2.7 0.5 pack_lead.1.lead
  3.2 0.2 copy-done.4
  3.4 0.1 copy.5
  3.5 0.1 reshape.20.slots
  3.6 0.0 collective-permute-done.far_d
  3.6 0.0 collective-permute-done.1.far_a
  3.6 0.2 copy-done.1
  3.8 0.2 copy-done.3
  4.0 3.0 %pack_halos.1._ = bf16[4,688,128]{2,1,0:T(8,128)(2,1)} custom-call(s32[1]{0:T(128)} %bitcast.1.rad, s32[32]{0:T(128)S(1)} %reshape.20.slots, bf16[4,8,80,128]{3,2,1,0:T(8,128)(2,1)S(1)} %bitcast.7, bf16[4,8,80,128]{3,2,1,0:T(8,128)(2,1)S(1)} %bitcast.11, bf16[4,8,80,128]{3,2,1,0:T(8,128)(2,1)S(1)} %collective-permute-done.far_d, ...), custom_call_target="tpu_custom_call" | custom-call | tf_op jit(solution)/shard_map/pack_halos/pallas_call | solution.py:355
  7.0 6.3 %all-to-all-start = ((bf16[4,688,128]{2,1,0:T(8,128)(2,1)}), bf16[4,688,128]{2,1,0:T(8,128)(2,1)S(1)}, u32[]{:S(2)}, u32[]{:S(2)}) async-start(bf16[4,688,128]{2,1,0:T(8,128)(2,1)} %pack_halos.1._), calls=%async_computation | async-start | bytes 1409024 | tf_op jit(solution)/shard_map/all_to_all | solution.py:323
  13.3 18.5 %all-to-all-done.refs_1_ = bf16[4,688,128]{2,1,0:T(8,128)(2,1)S(1)} async-done(((bf16[4,688,128]{2,1,0:T(8,128)(2,1)}), bf16[4,688,128]{2,1,0:T(8,128)(2,1)S(1)}, u32[]{:S(2)}, u32[]{:S(2)}) %all-to-all-start) | async-done | bytes 704544 | tf_op jit(solution)/shard_map/all_to_all | solution.py:323
  31.8 4.0 %triads.2 = f32[8,2,16,128]{3,2,1,0:T(8,128)} custom-call(s32[1]{0:T(128)} %bitcast.refs_0_.mode, bf16[4,688,128]{2,1,0:T(8,128)(2,1)S(1)} %all-to-all-done.refs_1_), custom_call_target="tpu_custom_call" | custom-call | tf_op jit(solution)/shard_map/triads/pallas_call | solution.py:386
  35.9 3.7 %all-to-all-start.1 = ((f32[8,2,16,128]{3,2,1,0:T(8,128)}), f32[8,2,16,128]{3,2,1,0:T(8,128)S(1)}, u32[]{:S(2)}, u32[]{:S(2)}) async-start(f32[8,2,16,128]{3,2,1,0:T(8,128)} %triads.2), calls=%async_computation.1 | async-start | bytes 262144 | tf_op jit(solution)/shard_map/all_to_all | solution.py:323
  39.5 0.6 pack_group.1
  40.2 2.1 %collective-permute-start.2 = (bf16[768,128]{1,0:T(8,128)(2,1)S(1)}, bf16[768,128]{1,0:T(8,128)(2,1)S(1)}, u32[]{:S(2)}, u32[]{:S(2)}) collective-permute-start(bf16[768,128]{1,0:T(8,128)(2,1)S(1)} %get-tuple-element.10), channel_id=1, source_target_pairs={{0,4},{4,8},{8,12},{12,0},{1,5},{5,9},{9,13},{13,1},{2,6},{6,10},{... | collective-permute-start | bytes 589832 | tf_op jit(solution)/shard_map/ppermute | solution.py:318
  42.2 2.4 %collective-permute-start.3 = (bf16[768,128]{1,0:T(8,128)(2,1)S(1)}, bf16[768,128]{1,0:T(8,128)(2,1)S(1)}, u32[]{:S(2)}, u32[]{:S(2)}) collective-permute-start(bf16[768,128]{1,0:T(8,128)(2,1)S(1)} %get-tuple-element.11), channel_id=1, source_target_pairs={{0,8},{4,12},{8,0},{12,4},{1,9},{5,13},{9,1},{13,5},{2,10},{6,14},... | collective-permute-start | bytes 589832 | tf_op jit(solution)/shard_map/ppermute | solution.py:318
  44.6 1.5 %collective-permute-start.4 = (bf16[768,128]{1,0:T(8,128)(2,1)S(1)}, bf16[768,128]{1,0:T(8,128)(2,1)S(1)}, u32[]{:S(2)}, u32[]{:S(2)}) collective-permute-start(bf16[768,128]{1,0:T(8,128)(2,1)S(1)} %get-tuple-element.12), channel_id=1, source_target_pairs={{0,12},{4,0},{8,4},{12,8},{1,13},{5,1},{9,5},{13,9},{2,14},{6,2},{... | collective-permute-start | bytes 589832 | tf_op jit(solution)/shard_map/ppermute | solution.py:318
  46.1 5.4 %collective-permute-done.2.refs_3_ = bf16[768,128]{1,0:T(8,128)(2,1)S(1)} collective-permute-done((bf16[768,128]{1,0:T(8,128)(2,1)S(1)}, bf16[768,128]{1,0:T(8,128)(2,1)S(1)}, u32[]{:S(2)}, u32[]{:S(2)}) %collective-permute-start.2) | collective-permute-done | bytes 196640 | tf_op jit(solution)/shard_map/ppermute | solution.py:318
  51.5 7.2 %collective-permute-done.3.refs_4_ = bf16[768,128]{1,0:T(8,128)(2,1)S(1)} collective-permute-done((bf16[768,128]{1,0:T(8,128)(2,1)S(1)}, bf16[768,128]{1,0:T(8,128)(2,1)S(1)}, u32[]{:S(2)}, u32[]{:S(2)}) %collective-permute-start.3) | collective-permute-done | bytes 196640 | tf_op jit(solution)/shard_map/ppermute | solution.py:318
  58.7 0.0 collective-permute-done.4.refs_5_
  58.7 4.4 %triads.3 = f32[8,2,24,128]{3,2,1,0:T(8,128)S(1)} custom-call(s32[1]{0:T(128)} %bitcast.refs_0_.mode, bf16[4,688,128]{2,1,0:T(8,128)(2,1)S(1)} %all-to-all-done.refs_1_, bf16[768,128]{1,0:T(8,128)(2,1)S(1)} %get-tuple-element.9.refs_2_, bf16[768,128]{1,0:T(8,128)(2,1)S(1)} %collective-permute-done.2.refs_3_, ...), custom_call_target="tpu_custom_call" | custom-call | tf_op jit(solution)/shard_map/triads/pallas_call | solution.py:386
  63.1 0.0 all-to-all-done.1.refs_0_
  63.1 14.4 %all_to_all.15.refs_1_ = f32[8,2,24,128]{3,2,1,0:T(8,128)S(1)} all-to-all(f32[8,2,24,128]{3,2,1,0:T(8,128)S(1)} %triads.3), channel_id=1, replica_groups=mesh['case'=2,'mode'=4,'harm'=2,'rad'=2] {'mode','harm'}, dimensions={0} | all-to-all | bytes 393216 | tf_op jit(solution)/shard_map/all_to_all | solution.py:323
  77.5 0.9 %unpack.1 = f32[8,40,128]{2,1,0:T(8,128)} custom-call(f32[8,2,16,128]{3,2,1,0:T(8,128)S(1)} %all-to-all-done.1.refs_0_, f32[8,2,24,128]{3,2,1,0:T(8,128)S(1)} %all_to_all.15.refs_1_), custom_call_target="tpu_custom_call" | custom-call | tf_op jit(solution)/shard_map/unpack/pallas_call | solution.py:410
Async XLA Ops:
  0.0 3.6 %collective-permute-start = (bf16[4,8,80,128]{3,2,1,0:T(8,128)(2,1)}, bf16[4,8,80,128]{3,2,1,0:T(8,128)(2,1)S(1)}, u32[]{:S(2)}, u32[]{:S(2)}) collective-permute-start(bf16[4,8,80,128]{3,2,1,0:T(8,128)(2,1)} %bitcast.5), channel_id=1, source_target_pairs={{0,1},{1,0},{2,3},{3,2},{4,5},{5,4},{6,7},{7,6},{8,9},{9,8},{10,11... | collective-permute-start | bytes 1966088 | tf_op jit(solution)/shard_map/ppermute | solution.py:338
  0.5 3.1 %collective-permute-start.1 = (bf16[4,8,80,128]{3,2,1,0:T(8,128)(2,1)}, bf16[4,8,80,128]{3,2,1,0:T(8,128)(2,1)S(1)}, u32[]{:S(2)}, u32[]{:S(2)}) collective-permute-start(bf16[4,8,80,128]{3,2,1,0:T(8,128)(2,1)} %bitcast.9), channel_id=1, source_target_pairs={{0,1},{1,0},{2,3},{3,2},{4,5},{5,4},{6,7},{7,6},{8,9},{9,8},{10,11... | collective-permute-start | bytes 1966088 | tf_op jit(solution)/shard_map/ppermute | solution.py:339
  0.5 1.1 %copy-start = (bf16[4,4,2,5,16,128]{5,4,3,2,1,0:T(8,128)(2,1)S(1)}, bf16[4,4,2,5,16,128]{5,4,3,2,1,0:T(8,128)(2,1)}, u32[]{:S(2)}) copy-start(bf16[4,4,2,5,16,128]{5,4,3,2,1,0:T(8,128)(2,1)} %param.3) | copy-start | bytes 1966084
  1.6 1.1 %copy-start.2 = (bf16[4,4,2,5,16,128]{5,4,3,2,1,0:T(8,128)(2,1)S(1)}, bf16[4,4,2,5,16,128]{5,4,3,2,1,0:T(8,128)(2,1)}, u32[]{:S(2)}) copy-start(bf16[4,4,2,5,16,128]{5,4,3,2,1,0:T(8,128)(2,1)} %param.4) | copy-start | bytes 1966084
  2.7 0.7 copy-start.4
  2.7 1.1 %copy-start.1 = (bf16[4,4,2,5,16,128]{5,4,3,2,1,0:T(8,128)(2,1)S(1)}, bf16[4,4,2,5,16,128]{5,4,3,2,1,0:T(8,128)(2,1)}, u32[]{:S(2)}) copy-start(bf16[4,4,2,5,16,128]{5,4,3,2,1,0:T(8,128)(2,1)} %param.3) | copy-start | bytes 1966084
  2.7 1.3 %copy-start.3 = (bf16[4,4,2,5,16,128]{5,4,3,2,1,0:T(8,128)(2,1)S(1)}, bf16[4,4,2,5,16,128]{5,4,3,2,1,0:T(8,128)(2,1)}, u32[]{:S(2)}) copy-start(bf16[4,4,2,5,16,128]{5,4,3,2,1,0:T(8,128)(2,1)} %param.4) | copy-start | bytes 1966084
  7.0 24.8 %all-to-all-start = ((bf16[4,688,128]{2,1,0:T(8,128)(2,1)}), bf16[4,688,128]{2,1,0:T(8,128)(2,1)S(1)}, u32[]{:S(2)}, u32[]{:S(2)}) async-start(bf16[4,688,128]{2,1,0:T(8,128)(2,1)} %pack_halos.1._), calls=%async_computation | async-start | bytes 1409024 | tf_op jit(solution)/shard_map/all_to_all | solution.py:323
  35.9 27.3 %all-to-all-start.1 = ((f32[8,2,16,128]{3,2,1,0:T(8,128)}), f32[8,2,16,128]{3,2,1,0:T(8,128)S(1)}, u32[]{:S(2)}, u32[]{:S(2)}) async-start(f32[8,2,16,128]{3,2,1,0:T(8,128)} %triads.2), calls=%async_computation.1 | async-start | bytes 262144 | tf_op jit(solution)/shard_map/all_to_all | solution.py:323
  40.2 11.3 %collective-permute-start.2 = (bf16[768,128]{1,0:T(8,128)(2,1)S(1)}, bf16[768,128]{1,0:T(8,128)(2,1)S(1)}, u32[]{:S(2)}, u32[]{:S(2)}) collective-permute-start(bf16[768,128]{1,0:T(8,128)(2,1)S(1)} %get-tuple-element.10), channel_id=1, source_target_pairs={{0,4},{4,8},{8,12},{12,0},{1,5},{5,9},{9,13},{13,1},{2,6},{6,10},{... | collective-permute-start | bytes 589832 | tf_op jit(solution)/shard_map/ppermute | solution.py:318
  42.2 16.4 %collective-permute-start.3 = (bf16[768,128]{1,0:T(8,128)(2,1)S(1)}, bf16[768,128]{1,0:T(8,128)(2,1)S(1)}, u32[]{:S(2)}, u32[]{:S(2)}) collective-permute-start(bf16[768,128]{1,0:T(8,128)(2,1)S(1)} %get-tuple-element.11), channel_id=1, source_target_pairs={{0,8},{4,12},{8,0},{12,4},{1,9},{5,13},{9,1},{13,5},{2,10},{6,14},... | collective-permute-start | bytes 589832 | tf_op jit(solution)/shard_map/ppermute | solution.py:318
  44.6 14.1 %collective-permute-start.4 = (bf16[768,128]{1,0:T(8,128)(2,1)S(1)}, bf16[768,128]{1,0:T(8,128)(2,1)S(1)}, u32[]{:S(2)}, u32[]{:S(2)}) collective-permute-start(bf16[768,128]{1,0:T(8,128)(2,1)S(1)} %get-tuple-element.12), channel_id=1, source_target_pairs={{0,12},{4,0},{8,4},{12,8},{1,13},{5,1},{9,5},{13,9},{2,14},{6,2},{... | collective-permute-start | bytes 589832 | tf_op jit(solution)/shard_map/ppermute | solution.py:318

commit v6 on v5

v6 whole, which is shorter than its diff:
```python
import functools
import math

import jax
import jax.numpy as jnp
from jax import lax
from jax.experimental import pallas as pl
from jax.experimental.pallas import tpu as pltpu
from jax.sharding import PartitionSpec as P

HARMS = 8
LANES = 128
HALO = 4
SLOT_ROWS = 16
VMEM_LIMIT = 40 * 1024 * 1024


def iota(shape, axis):
    return lax.broadcasted_iota(jnp.int32, shape, axis)


def one_hot(mask):
    return jnp.where(mask, 1.0, 0.0).astype(jnp.bfloat16)


def halo_offset(index, width):
    return jnp.where(index < 2, index - 2, index - 2 + width)


def wrapped(index, count):
    return jnp.where(index >= count, index - count, index)


def columns(harms, blocks, first):
    shape = (harms * LANES, blocks * LANES)
    row, col = iota(shape, 0), iota(shape, 1)
    owner = wrapped(col // LANES + first, blocks)
    return row // LANES, row % LANES, owner, col % LANES


def side_by_side(ref, group, rows):
    return jnp.concatenate([ref[k, group, rows, :] for k in range(ref.shape[0])], axis=1)


def matrix_kernel(sizes, groups, mode, rad, direct, adjoint, main_m, halo_m, own_d, own_a, sems):
    harms, blocks, width = sizes
    loads = [
        pltpu.make_async_copy(source.at[k], target.at[k], sems.at[array, k])
        for array, (source, target) in enumerate(((direct, own_d), (adjoint, own_a)))
        for k in range(harms)
    ]
    for load in loads:
        load.start()
    harm_in, cell_in, owner, lane = columns(harms, blocks, mode[0])
    main_m[...] = one_hot(
        (lane // width == harm_in) & (cell_in == owner * width + lane % width)
    )
    shift = jnp.where(rad[0] == 0, LANES, -LANES)
    depth = harms * LANES
    span_h = harms * HALO
    part = lane % span_h
    wanted = owner * width + halo_offset(part % HALO, width)
    same = (part // HALO == harm_in) & (lane < groups * span_h)
    halo_m[0:depth, :] = one_hot(same & (cell_in == wanted))
    halo_m[depth:, :] = one_hot(same & (cell_in + shift == wanted))
    for load in loads:
        load.wait()


def pack_kernel(sizes, cells, slots, own_d, own_a, far_d, far_a, main_m, halo_m, *outs):
    harms, blocks, width = sizes
    groups, group_rows = own_d.shape[1], own_d.shape[2]
    fields = group_rows // cells
    tile = groups * cells
    lane_group = (iota((group_rows, blocks * LANES), 1) % LANES) // (harms * HALO)
    everything = slice(0, group_rows)
    base = 2 * fields * tile
    for array, (own, far) in enumerate(((own_d, far_d), (own_a, far_a))):
        near = [side_by_side(own, group, everything) for group in range(groups)]
        rows = [
            near[group][field * cells : (field + 1) * cells, :]
            for field in range(fields)
            for group in range(groups)
        ]
        main = jnp.dot(
            jnp.concatenate(rows, axis=0), main_m[...], preferred_element_type=jnp.float32
        )
        pieces = [
            jnp.concatenate([near[group], side_by_side(far, group, everything)], axis=1)
            for group in range(groups)
        ]
        ends = jnp.dot(
            jnp.concatenate(pieces, axis=0), halo_m[...], preferred_element_type=jnp.float32
        )
        held = jnp.zeros((group_rows, blocks * LANES), jnp.float32)
        for group in range(groups):
            held = jnp.where(
                lane_group == group, ends[group * group_rows : (group + 1) * group_rows], held
            )
        for step, out in enumerate(outs):
            lanes = slice(step * LANES, (step + 1) * LANES)
            start = array * fields * tile
            out[start : start + fields * tile, :] = main[:, lanes].astype(jnp.bfloat16)
            start = base + array * group_rows
            out[start : start + group_rows, :] = held[:, lanes].astype(jnp.bfloat16)
    lane = iota((SLOT_ROWS, LANES), 1)
    listed = jnp.zeros((SLOT_ROWS, LANES), jnp.int32)
    for index in range(slots.shape[0]):
        listed = jnp.where(lane == index, slots[index], listed)
    for out in outs:
        out[base + 2 * group_rows :, :] = listed.astype(jnp.float32).astype(jnp.bfloat16)


def coefficient(distance):
    near = jnp.where(distance == 1, 8.0, jnp.where(distance == -1, -8.0, 0.0))
    return jnp.where(distance == 2, -1.0, jnp.where(distance == -2, 1.0, near))


def triad_kernel(sizes, mode, *refs):
    harms, blocks, width, groups, slots, count, cells, harm_devices = sizes
    mains = refs[:blocks]
    origins = [wrapped(mode[0] - step + blocks, blocks) for step in range(blocks)]
    out, radial_m, axial_m, plain_v, axial_v, radial_v, sums, slots_v, slots_s, slots_sem = refs[
        blocks:
    ]
    halo_row = 2 * count * groups * cells
    slot_row = halo_row + 2 * count * cells
    for step in range(blocks):
        slots_v[step : step + 1, :] = (
            mains[step][slot_row : slot_row + SLOT_ROWS, :].astype(jnp.float32)[0:1, :]
        ).astype(jnp.int32)
    listing = pltpu.make_async_copy(slots_v, slots_s, slots_sem)
    listing.start()
    span_h = harms * HALO
    used = harms * width
    tile = groups * cells
    shape = (LANES, LANES)
    row, col = iota(shape, 0), iota(shape, 1)
    inside = (row // width == col // width) & (row < used) & (col < used)
    within = jnp.where(inside, coefficient(row - col), 0.0).astype(jnp.bfloat16)
    square = (tile, tile)
    row_t, col_t = iota(square, 0), iota(square, 1)
    axial_m[...] = jnp.where(
        row_t // cells == col_t // cells, coefficient(col_t - row_t), 0.0
    ).astype(jnp.bfloat16)

    for group in range(groups):
        part = row - group * span_h
        mine = (part >= 0) & (part < span_h) & (col < used) & (part // HALO == col // width)
        place = halo_offset(part % HALO, width)
        around = jnp.where(mine, coefficient(place - col % width), 0.0).astype(jnp.bfloat16)
        radial_m[group] = jnp.concatenate([within, around], axis=0)
    for group in range(groups):
        pieces = []
        for array in range(2):
            for local in range(count):
                for step in range(blocks):
                    start = ((array * count + local) * groups + group) * cells
                    beside = halo_row + (array * count + local) * cells
                    pieces.append(
                        jnp.concatenate(
                            [
                                mains[step][start : start + cells, :],
                                mains[step][beside : beside + cells, :],
                            ],
                            axis=1,
                        )
                    )
        slopes = jnp.dot(
            jnp.concatenate(pieces, axis=0), radial_m[group], preferred_element_type=jnp.float32
        )
        index = 0
        for array in range(2):
            for local in range(count):
                for step in range(blocks):
                    radial_v[array * count + local, origins[step] * groups + group] = slopes[
                        index * cells : (index + 1) * cells, :
                    ]
                    index += 1
    for step in range(blocks):
        for local in range(count):
            starts = [(array * count + local) * tile for array in range(2)]
            both = jnp.concatenate([mains[step][s : s + tile, :] for s in starts], axis=1)
            slopes = jnp.dot(axial_m[...], both, preferred_element_type=jnp.float32)
            for array in range(2):
                for group in range(groups):
                    axial_v[array * count + local, origins[step] * groups + group] = slopes[
                        group * cells : (group + 1) * cells, array * LANES : (array + 1) * LANES
                    ]
        for which in range(4):
            for group in range(groups):
                held = which // 2 * count + 1 + which % 2
                start = (held * groups + group) * cells
                plain_v[which, origins[step] * groups + group] = mains[step][
                    start : start + cells, :
                ].astype(jnp.float32)

    listing.wait()

    @pl.loop(0, blocks * slots)
    def _(index):
        step = index // slots
        listed = wrapped(mode[0] - step + blocks, blocks)
        entry = lax.rem(index, slots) * blocks

        def add_stop(stop, running):
            source = wrapped(step - stop + blocks, blocks)
            at_a = step * groups + slots_s[listed, (entry + stop) * 2] * 2
            at_d = source * groups + slots_s[listed, (entry + stop) * 2 + 1] * 2
            d1r, d1i, d2r, d2i = (plain_v[w, at_d + c] for w in (0, 1) for c in (0, 1))
            a1r, a1i, a2r, a2i = (plain_v[w, at_a + c] for w in (2, 3) for c in (0, 1))
            result = []
            for local in range(count):
                xar, xai = axial_v[count + local, at_a], axial_v[count + local, at_a + 1]
                rar, rai = radial_v[count + local, at_a], radial_v[count + local, at_a + 1]
                xdr, xdi = axial_v[local, at_d], axial_v[local, at_d + 1]
                rdr, rdi = radial_v[local, at_d], radial_v[local, at_d + 1]
                real = (d1r * xar + d1i * xai) + (d2r * rar + d2i * rai)
                real = real + ((xdr * a1r + xdi * a1i) + (rdr * a2r + rdi * a2i))
                imag = (d1r * xai - d1i * xar) + (d2r * rai - d2i * rar)
                imag = imag + ((xdr * a1i - xdi * a1r) + (rdr * a2i - rdi * a2r))
                old_real, old_imag = running[local]
                result.append((old_real + real, old_imag + imag))
            return tuple(result)

        zero = jnp.zeros((cells, LANES), jnp.float32)
        running = tuple((zero, zero) for _ in range(count))
        if blocks <= 4:
            for stop in range(blocks):
                running = add_stop(stop, running)
        else:
            running = lax.fori_loop(0, blocks, add_stop, running)
        for local in range(count):
            for part in range(2):
                sums[index, part * count + local] = running[local][part]

    scale = 1.0 / (12.0 * math.sqrt(8.0 * blocks * HARMS))
    per_harm = blocks // harm_devices
    own_cells = cells // blocks
    lane_slot = iota((cells, LANES), 1) // width

    @pl.loop(0, blocks)
    def _(step):
        for row in range(2 * count):
            packed = jnp.zeros((cells, LANES), jnp.float32)
            for slot in range(slots):
                value = sums[step * slots + slot, row]
                reach = harms // 2
                while reach:
                    value = value + pltpu.roll(value, reach * width, axis=1)
                    reach //= 2
                if used < LANES and slot:
                    value = pltpu.roll(value, slot * width, axis=1)
                packed = jnp.where(lane_slot == slot, value, packed)
            packed = packed * scale
            for owner in range(blocks):
                out[
                    owner * harm_devices + step // per_harm,
                    lax.rem(step, per_harm),
                    row * own_cells : (row + 1) * own_cells,
                    :,
                ] = packed[owner * own_cells : (owner + 1) * own_cells, :]


def unpack_kernel(sizes, came, out_ref):
    blocks, harm_devices, slots, width, per_harm = sizes
    rows = came.shape[2]
    lane_block = iota((rows, LANES), 1) // width
    for local in range(per_harm):
        packed = [jnp.zeros((rows, LANES), jnp.float32) for _ in range(slots)]
        for source in range(blocks):
            total = came[source * harm_devices, local]
            for harm in range(1, harm_devices):
                total = total + came[source * harm_devices + harm, local]
            for slot in range(slots):
                amount = (source - slot) * width % LANES
                moved = pltpu.roll(total, amount, axis=1) if amount else total
                packed[slot] = jnp.where(lane_block == source, moved, packed[slot])
        for slot in range(slots):
            out_ref[local * slots + slot] = packed[slot]


def smem(count):
    return [pl.BlockSpec(memory_space=pltpu.SMEM)] * count


def vmem(count):
    return [pl.BlockSpec(memory_space=pltpu.VMEM)] * count


def moved_up(values, axis):
    count = lax.axis_size(axis)
    result = [values[0]]
    for step in range(1, count):
        pairs = [(source, (source + step) % count) for source in range(count)]
        result.append(lax.ppermute(values[step], axis, pairs))
    return result


def body(direct_field, adjoint_field, triad_slots):
    blocks, harm_devices = lax.axis_size("mode"), lax.axis_size("harm")
    harms, slots, parts, fields, cells, radial = direct_field.shape
    width = radial // blocks
    groups, group_rows = slots * parts, fields * cells
    tile = groups * cells
    params = pltpu.CompilerParams(vmem_limit_bytes=VMEM_LIMIT)
    mode, rad = (lax.axis_index(axis).astype(jnp.int32).reshape(1) for axis in ("mode", "rad"))

    direct = direct_field.reshape(harms, groups, group_rows, radial)
    adjoint = adjoint_field.reshape(harms, groups, group_rows, radial)
    swap = [(0, 1), (1, 0)]
    far_direct = lax.ppermute(direct, "rad", swap)
    far_adjoint = lax.ppermute(adjoint, "rad", swap)

    sizes = (harms, blocks, width)
    depth, span = harms * LANES, blocks * LANES
    main_m, halo_m, own_direct, own_adjoint = pl.pallas_call(
        functools.partial(matrix_kernel, sizes, groups),
        out_shape=[
            jax.ShapeDtypeStruct((depth, span), jnp.bfloat16),
            jax.ShapeDtypeStruct((2 * depth, span), jnp.bfloat16),
            jax.ShapeDtypeStruct(direct.shape, jnp.bfloat16),
            jax.ShapeDtypeStruct(direct.shape, jnp.bfloat16),
        ],
        in_specs=smem(2) + [pl.BlockSpec(memory_space=pl.ANY)] * 2,
        out_specs=vmem(4),
        scratch_shapes=[pltpu.SemaphoreType.DMA((2, harms))],
        compiler_params=params,
        name="matrices",
    )(mode, rad, direct, adjoint)
    payload_rows = 2 * fields * tile + 2 * group_rows + SLOT_ROWS
    slabs = pl.pallas_call(
        functools.partial(pack_kernel, sizes, cells),
        out_shape=[jax.ShapeDtypeStruct((payload_rows, LANES), jnp.bfloat16)] * blocks,
        in_specs=smem(1) + vmem(6),
        out_specs=vmem(blocks),
        compiler_params=params,
        name="pack",
    )(triad_slots.reshape(-1), own_direct, own_adjoint, far_direct, far_adjoint, main_m, halo_m)
    came = moved_up(slabs, "mode")

    per_harm, own_cells = blocks // harm_devices, cells // blocks
    sizes = (harms, blocks, width, groups, slots, fields, cells, harm_devices)
    listed = (max(blocks, 8), LANES)
    derived = pltpu.VMEM((2 * fields, blocks * groups, cells, LANES), jnp.float32)
    out_rows = 2 * fields * own_cells
    sent = pl.pallas_call(
        functools.partial(triad_kernel, sizes),
        out_shape=jax.ShapeDtypeStruct(
            (blocks * harm_devices, per_harm, out_rows, LANES), jnp.float32
        ),
        in_specs=smem(1) + vmem(blocks),
        out_specs=vmem(1)[0],
        scratch_shapes=[
            pltpu.VMEM((groups, 2 * LANES, LANES), jnp.bfloat16),
            pltpu.VMEM((tile, tile), jnp.bfloat16),
            pltpu.VMEM((4, blocks * groups, cells, LANES), jnp.float32),
            derived,
            derived,
            pltpu.VMEM((blocks * slots, 2 * fields, cells, LANES), jnp.float32),
            pltpu.VMEM(listed, jnp.int32),
            pltpu.SMEM(listed, jnp.int32),
            pltpu.SemaphoreType.DMA,
        ],
        compiler_params=params,
        name="triads",
    )(mode, *came)
    owned = lax.all_to_all(sent, ("mode", "harm"), split_axis=0, concat_axis=0, tiled=True)

    result = pl.pallas_call(
        functools.partial(unpack_kernel, (blocks, harm_devices, slots, width, per_harm)),
        out_shape=jax.ShapeDtypeStruct((per_harm * slots, out_rows, LANES), jnp.float32),
        in_specs=vmem(1),
        out_specs=vmem(1)[0],
        compiler_params=params,
        name="unpack",
    )(owned)
    return result.reshape(per_harm * slots, 2, fields, own_cells, radial)


def solution(mesh):
    return jax.shard_map(
        body,
        mesh=mesh,
        in_specs=(
            P(("case", "harm"), "mode", None, None, None, "rad"),
            P(("case", "harm"), "mode", None, None, None, "rad"),
            P("mode", None, None),
        ),
        out_specs=P(("case", "harm"), None, None, "mode", "rad"),
        check_vma=False,
    )
```

time: 78.8 us -> 69.2 us (0.88)
  starting transfers between devices: 16.4 us -> 7.52 us
  waiting for transfers between devices: 31.2 us -> 23 us
  blocking collectives: 14.4 us -> 21.7 us
    all_to_all x2 -> x0, waiting for transfers between devices: 18.5 us -> none  [exchanged(): return lax.all_to_all(value, axes, split_axis=0, concat_axis=0, tiled=True)]
    ppermute x3, waiting for transfers between devices: 12.6 us -> 23 us  [moved_up(): result.append(lax.ppermute(values[step], axis, pairs))]
    all_to_all x2 -> x0, starting transfers between devices: 9.98 us -> none  [exchanged(): return lax.all_to_all(value, axes, split_axis=0, concat_axis=0, tiled=True)]
    all_to_all x1, blocking collectives: 14.4 us -> 21.7 us  [body(): lax.all_to_all(sent, ('mode', 'harm'), split_axis=0, concat_axis=0, tiled...]
    ppermute x3, starting transfers between devices: 5.9 us -> 7.01 us  [moved_up(): result.append(lax.ppermute(values[step], axis, pairs))]
    pallas_call x6 -> x4, Pallas kernels: 13.4 us -> 13.6 us  [the longest x1 7.72 us: body(): pl.pallas_call(functools.partial(triad_kernel, sizes), out_shape=jax.Shap...]
    unnamed x11 -> x7, local copies, waits for them, and re-layouts: 2.85 us -> 2.97 us
  transfers between devices with their start and end apart: 7 -> 5, of which waited for: 3 -> 2; matrix products, arithmetic and copies ran while one was open for 0% -> 0% of each run, Pallas kernels for 7% -> 3%
where the time goes in v6:
time: 69.2 us; the launch traced here: 69 us
  waiting for transfers between devices  23 us (33%)
  blocking collectives  21.7 us (31%)
  Pallas kernels  13.6 us (20%)
  starting transfers between devices  7.52 us (11%)
  local copies, waits for them, and re-layouts  3.06 us (4%)
    ppermute x3, waiting for transfers between devices, moved_up(): result.append(lax.ppermute(values[step], axis, pairs))  23 us
    all_to_all x1, blocking collectives, body(): lax.all_to_all(sent, ('mode', 'harm'), split_axis=0, concat_axis=0, tiled...  21.7 us
    pallas_call x1, Pallas kernels, body(): pl.pallas_call(functools.partial(triad_kernel, sizes), out_shape=jax.Shap...  7.72 us
    ppermute x3, starting transfers between devices, moved_up(): result.append(lax.ppermute(values[step], axis, pairs))  7.01 us
    unnamed x7, local copies, waits for them, and re-layouts  2.97 us
    pallas_call x1, Pallas kernels, body(): pl.pallas_call(functools.partial(pack_kernel, sizes, cells), out_shape=[j...  2.75 us
    pallas_call x1, Pallas kernels, body(): pl.pallas_call(functools.partial(matrix_kernel, sizes, groups), out_shape...  2.25 us
  transfers between devices with their start and end apart: 5, of which 2 were waited for; matrix products, arithmetic and copies ran while one was open for 0% of the time, Pallas kernels for 3%

profile of v6, /device:TPU:0, one launch (start us, length us, event | category | flops | bytes accessed | tf_op | source)
XLA Modules:
  0.0 69.0 jit_solution(17984649367244527832)
XLA Ops:
  0.0 0.5 collective-permute-start
  0.5 0.1 collective-permute-start.1
  0.5 0.0 copy-start.2
  0.5 0.7 copy-done.2
  1.2 0.1 copy.5
  1.3 0.1 reshape.19.slots
  1.4 0.0 copy-start
  1.4 1.1 %copy-done = bf16[4,4,2,5,16,128]{5,4,3,2,1,0:T(8,128)(2,1)S(1)} copy-done((bf16[4,4,2,5,16,128]{5,4,3,2,1,0:T(8,128)(2,1)S(1)}, bf16[4,4,2,5,16,128]{5,4,3,2,1,0:T(8,128)(2,1)}, u32[]{:S(2)}) %copy-start) | copy-done | bytes 655384
  2.5 0.0 copy-start.1
  2.5 1.1 %copy-done.1 = bf16[4,4,2,5,16,128]{5,4,3,2,1,0:T(8,128)(2,1)S(1)} copy-done((bf16[4,4,2,5,16,128]{5,4,3,2,1,0:T(8,128)(2,1)S(1)}, bf16[4,4,2,5,16,128]{5,4,3,2,1,0:T(8,128)(2,1)}, u32[]{:S(2)}) %copy-start.1) | copy-done | bytes 655384
  3.6 2.2 %matrices.1 = (bf16[512,512]{1,0:T(8,128)(2,1)S(1)}, bf16[1024,512]{1,0:T(8,128)(2,1)S(1)}, bf16[4,8,80,128]{3,2,1,0:T(8,128)(2,1)S(1)}, bf16[4,8,80,128]{3,2,1,0:T(8,128)(2,1)S(1)}) custom-call(s32[1]{0:T(128)} %bitcast.mode, s32[1]{0:T(128)} %bitcast.1.rad, bf16[4,8,80,128]{3,2,1,0:T(8,128)(2,1)S(1)} %bitcast.6, bf16[4,8,80,128]{3,2,1,0:T(8,128)(2,1)S(1)} %bitcast.8), custom_call_target="tpu_custom_call" | custom-call | tf_op jit(solution)/shard_map/matrices/pallas_call | solution.py:317
  5.8 0.0 collective-permute-done.far_d
  5.9 0.0 collective-permute-done.1.far_a
  5.9 2.7 %pack.1 = (bf16[1456,128]{1,0:T(8,128)(2,1)S(1)}, bf16[1456,128]{1,0:T(8,128)(2,1)S(1)}, bf16[1456,128]{1,0:T(8,128)(2,1)S(1)}, bf16[1456,128]{1,0:T(8,128)(2,1)S(1)}) custom-call(s32[32]{0:T(128)S(1)} %reshape.19.slots, bf16[4,8,80,128]{3,2,1,0:T(8,128)(2,1)S(1)} %get-tuple-element.13.own_d, bf16[4,8,80,128]{3,2,1,0:T(8,128)(2,1)S(1)} %get-tuple-element.14.own_a, ...), custom_call_target="tpu_custom_call" | custom-call | tf_op jit(solution)/shard_map/pack/pallas_call | solution.py:332
  8.6 3.1 %collective-permute-start.2 = (bf16[1456,128]{1,0:T(8,128)(2,1)S(1)}, bf16[1456,128]{1,0:T(8,128)(2,1)S(1)}, u32[]{:S(2)}, u32[]{:S(2)}) collective-permute-start(bf16[1456,128]{1,0:T(8,128)(2,1)S(1)} %get-tuple-element.18), channel_id=1, source_target_pairs={{0,4},{4,8},{8,12},{12,0},{1,5},{5,9},{9,13},{13,1},{2,6},{6,10},{... | collective-permute-start | bytes 1118216 | tf_op jit(solution)/shard_map/ppermute | solution.py:296
  11.7 2.6 %collective-permute-start.3 = (bf16[1456,128]{1,0:T(8,128)(2,1)S(1)}, bf16[1456,128]{1,0:T(8,128)(2,1)S(1)}, u32[]{:S(2)}, u32[]{:S(2)}) collective-permute-start(bf16[1456,128]{1,0:T(8,128)(2,1)S(1)} %get-tuple-element.19), channel_id=1, source_target_pairs={{0,8},{4,12},{8,0},{12,4},{1,9},{5,13},{9,1},{13,5},{2,10},{6,14},... | collective-permute-start | bytes 1118216 | tf_op jit(solution)/shard_map/ppermute | solution.py:296
  14.3 1.3 %collective-permute-start.4 = (bf16[1456,128]{1,0:T(8,128)(2,1)S(1)}, bf16[1456,128]{1,0:T(8,128)(2,1)S(1)}, u32[]{:S(2)}, u32[]{:S(2)}) collective-permute-start(bf16[1456,128]{1,0:T(8,128)(2,1)S(1)} %get-tuple-element.20), channel_id=1, source_target_pairs={{0,12},{4,0},{8,4},{12,8},{1,13},{5,1},{9,5},{13,9},{2,14},{6,2},{... | collective-permute-start | bytes 1118216 | tf_op jit(solution)/shard_map/ppermute | solution.py:296
  15.6 7.7 %collective-permute-done.2.refs_1_ = bf16[1456,128]{1,0:T(8,128)(2,1)S(1)} collective-permute-done((bf16[1456,128]{1,0:T(8,128)(2,1)S(1)}, bf16[1456,128]{1,0:T(8,128)(2,1)S(1)}, u32[]{:S(2)}, u32[]{:S(2)}) %collective-permute-start.2) | collective-permute-done | bytes 372768 | tf_op jit(solution)/shard_map/ppermute | solution.py:296
  23.3 15.3 %collective-permute-done.3.refs_2_ = bf16[1456,128]{1,0:T(8,128)(2,1)S(1)} collective-permute-done((bf16[1456,128]{1,0:T(8,128)(2,1)S(1)}, bf16[1456,128]{1,0:T(8,128)(2,1)S(1)}, u32[]{:S(2)}, u32[]{:S(2)}) %collective-permute-start.3) | collective-permute-done | bytes 372768 | tf_op jit(solution)/shard_map/ppermute | solution.py:296
  38.7 0.0 collective-permute-done.4.refs_3_
  38.7 7.7 %triads.1 = f32[8,2,40,128]{3,2,1,0:T(8,128)S(1)} custom-call(s32[1]{0:T(128)} %bitcast.mode, bf16[1456,128]{1,0:T(8,128)(2,1)S(1)} %get-tuple-element.17.refs_0_, bf16[1456,128]{1,0:T(8,128)(2,1)S(1)} %collective-permute-done.2.refs_1_, bf16[1456,128]{1,0:T(8,128)(2,1)S(1)} %collective-permute-done.3.refs_2_, ...), custom_call_target="tpu_custom_call" | custom-call | tf_op jit(solution)/shard_map/triads/pallas_call | solution.py:347
  46.4 21.7 %all_to_all.5.came = f32[8,2,40,128]{3,2,1,0:T(8,128)S(1)} all-to-all(f32[8,2,40,128]{3,2,1,0:T(8,128)S(1)} %triads.1), channel_id=1, replica_groups=mesh['case'=2,'mode'=4,'harm'=2,'rad'=2] {'mode','harm'}, dimensions={0} | all-to-all | bytes 655360 | tf_op jit(solution)/shard_map/all_to_all | solution.py:368
  68.1 0.9 %unpack.1 = f32[8,40,128]{2,1,0:T(8,128)} custom-call(f32[8,2,40,128]{3,2,1,0:T(8,128)S(1)} %all_to_all.5.came), custom_call_target="tpu_custom_call" | custom-call | tf_op jit(solution)/shard_map/unpack/pallas_call | solution.py:370
Async XLA Ops:
  0.0 5.8 %collective-permute-start = (bf16[4,8,80,128]{3,2,1,0:T(8,128)(2,1)}, bf16[4,8,80,128]{3,2,1,0:T(8,128)(2,1)S(1)}, u32[]{:S(2)}, u32[]{:S(2)}) collective-permute-start(bf16[4,8,80,128]{3,2,1,0:T(8,128)(2,1)} %bitcast.5), channel_id=1, source_target_pairs={{0,1},{1,0},{2,3},{3,2},{4,5},{5,4},{6,7},{7,6},{8,9},{9,8},{10,11... | collective-permute-start | bytes 1966088 | tf_op jit(solution)/shard_map/ppermute | solution.py:312
  0.5 5.4 %collective-permute-start.1 = (bf16[4,8,80,128]{3,2,1,0:T(8,128)(2,1)}, bf16[4,8,80,128]{3,2,1,0:T(8,128)(2,1)S(1)}, u32[]{:S(2)}, u32[]{:S(2)}) collective-permute-start(bf16[4,8,80,128]{3,2,1,0:T(8,128)(2,1)} %bitcast.7), channel_id=1, source_target_pairs={{0,1},{1,0},{2,3},{3,2},{4,5},{5,4},{6,7},{7,6},{8,9},{9,8},{10,11... | collective-permute-start | bytes 1966088 | tf_op jit(solution)/shard_map/ppermute | solution.py:313
  0.5 0.7 copy-start.2
  1.4 1.1 %copy-start = (bf16[4,4,2,5,16,128]{5,4,3,2,1,0:T(8,128)(2,1)S(1)}, bf16[4,4,2,5,16,128]{5,4,3,2,1,0:T(8,128)(2,1)}, u32[]{:S(2)}) copy-start(bf16[4,4,2,5,16,128]{5,4,3,2,1,0:T(8,128)(2,1)} %param.3) | copy-start | bytes 1966084
  2.5 1.1 %copy-start.1 = (bf16[4,4,2,5,16,128]{5,4,3,2,1,0:T(8,128)(2,1)S(1)}, bf16[4,4,2,5,16,128]{5,4,3,2,1,0:T(8,128)(2,1)}, u32[]{:S(2)}) copy-start(bf16[4,4,2,5,16,128]{5,4,3,2,1,0:T(8,128)(2,1)} %param.4) | copy-start | bytes 1966084
  8.6 14.7 %collective-permute-start.2 = (bf16[1456,128]{1,0:T(8,128)(2,1)S(1)}, bf16[1456,128]{1,0:T(8,128)(2,1)S(1)}, u32[]{:S(2)}, u32[]{:S(2)}) collective-permute-start(bf16[1456,128]{1,0:T(8,128)(2,1)S(1)} %get-tuple-element.18), channel_id=1, source_target_pairs={{0,4},{4,8},{8,12},{12,0},{1,5},{5,9},{9,13},{13,1},{2,6},{6,10},{... | collective-permute-start | bytes 1118216 | tf_op jit(solution)/shard_map/ppermute | solution.py:296
  11.7 27.0 %collective-permute-start.3 = (bf16[1456,128]{1,0:T(8,128)(2,1)S(1)}, bf16[1456,128]{1,0:T(8,128)(2,1)S(1)}, u32[]{:S(2)}, u32[]{:S(2)}) collective-permute-start(bf16[1456,128]{1,0:T(8,128)(2,1)S(1)} %get-tuple-element.19), channel_id=1, source_target_pairs={{0,8},{4,12},{8,0},{12,4},{1,9},{5,13},{9,1},{13,5},{2,10},{6,14},... | collective-permute-start | bytes 1118216 | tf_op jit(solution)/shard_map/ppermute | solution.py:296
  14.3 24.4 %collective-permute-start.4 = (bf16[1456,128]{1,0:T(8,128)(2,1)S(1)}, bf16[1456,128]{1,0:T(8,128)(2,1)S(1)}, u32[]{:S(2)}, u32[]{:S(2)}) collective-permute-start(bf16[1456,128]{1,0:T(8,128)(2,1)S(1)} %get-tuple-element.20), channel_id=1, source_target_pairs={{0,12},{4,0},{8,4},{12,8},{1,13},{5,1},{9,5},{13,9},{2,14},{6,2},{... | collective-permute-start | bytes 1118216 | tf_op jit(solution)/shard_map/ppermute | solution.py:296

commit v7 on v6

--- a/solution.py
+++ b/solution.py
@@ -42,15 +42,8 @@
     return jnp.concatenate([ref[k, group, rows, :] for k in range(ref.shape[0])], axis=1)
 
 
-def matrix_kernel(sizes, groups, mode, rad, direct, adjoint, main_m, halo_m, own_d, own_a, sems):
+def matrix_kernel(sizes, groups, mode, rad, main_m, halo_m):
     harms, blocks, width = sizes
-    loads = [
-        pltpu.make_async_copy(source.at[k], target.at[k], sems.at[array, k])
-        for array, (source, target) in enumerate(((direct, own_d), (adjoint, own_a)))
-        for k in range(harms)
-    ]
-    for load in loads:
-        load.start()
     harm_in, cell_in, owner, lane = columns(harms, blocks, mode[0])
     main_m[...] = one_hot(
         (lane // width == harm_in) & (cell_in == owner * width + lane % width)
@@ -63,8 +56,6 @@
     same = (part // HALO == harm_in) & (lane < groups * span_h)
     halo_m[0:depth, :] = one_hot(same & (cell_in == wanted))
     halo_m[depth:, :] = one_hot(same & (cell_in + shift == wanted))
-    for load in loads:
-        load.wait()
 
 
 def pack_kernel(sizes, cells, slots, own_d, own_a, far_d, far_a, main_m, halo_m, *outs):
@@ -314,20 +305,17 @@
 
     sizes = (harms, blocks, width)
     depth, span = harms * LANES, blocks * LANES
-    main_m, halo_m, own_direct, own_adjoint = pl.pallas_call(
+    matrices = pl.pallas_call(
         functools.partial(matrix_kernel, sizes, groups),
         out_shape=[
             jax.ShapeDtypeStruct((depth, span), jnp.bfloat16),
             jax.ShapeDtypeStruct((2 * depth, span), jnp.bfloat16),
-            jax.ShapeDtypeStruct(direct.shape, jnp.bfloat16),
-            jax.ShapeDtypeStruct(direct.shape, jnp.bfloat16),
         ],
-        in_specs=smem(2) + [pl.BlockSpec(memory_space=pl.ANY)] * 2,
-        out_specs=vmem(4),
-        scratch_shapes=[pltpu.SemaphoreType.DMA((2, harms))],
+        in_specs=smem(2),
+        out_specs=vmem(2),
         compiler_params=params,
         name="matrices",
-    )(mode, rad, direct, adjoint)
+    )(mode, rad)
     payload_rows = 2 * fields * tile + 2 * group_rows + SLOT_ROWS
     slabs = pl.pallas_call(
         functools.partial(pack_kernel, sizes, cells),
@@ -336,7 +324,7 @@
         out_specs=vmem(blocks),
         compiler_params=params,
         name="pack",
-    )(triad_slots.reshape(-1), own_direct, own_adjoint, far_direct, far_adjoint, main_m, halo_m)
+    )(triad_slots.reshape(-1), direct, adjoint, far_direct, far_adjoint, *matrices)
     came = moved_up(slabs, "mode")
 
     per_harm, own_cells = blocks // harm_devices, cells // blocks

time: 69.2 us -> 69.1 us (level)
  Pallas kernels: 13.6 us -> 11.8 us
  waiting for transfers between devices: 23 us -> 24.6 us
    pallas_call x1, Pallas kernels: 2.25 us -> 0.52 us  [body(): pl.pallas_call(functools.partial(matrix_kernel, sizes, groups), out_shape...]
    ppermute x1, waiting for transfers between devices: 0.01 us -> 0.94 us  [body(): far_adjoint = lax.ppermute(adjoint, 'rad', swap)]
  transfers between devices with their start and end apart: 5 -> 5, of which waited for: 2 -> 4; matrix products, arithmetic and copies ran while one was open for 0% -> 0% of each run, Pallas kernels for 3% -> 1%
where the time goes in v7:
time: 69.1 us; the launch traced here: 68.9 us
  waiting for transfers between devices  24.6 us (36%)
  blocking collectives  21.9 us (32%)
  Pallas kernels  11.8 us (17%)
  starting transfers between devices  7.44 us (11%)
  local copies, waits for them, and re-layouts  3.06 us (4%)
    ppermute x3, waiting for transfers between devices, moved_up(): result.append(lax.ppermute(values[step], axis, pairs))  23.2 us
    all_to_all x1, blocking collectives, body(): lax.all_to_all(sent, ('mode', 'harm'), split_axis=0, concat_axis=0, tiled...  21.9 us
    pallas_call x1, Pallas kernels, body(): pl.pallas_call(functools.partial(triad_kernel, sizes), out_shape=jax.Shap...  7.72 us
    ppermute x3, starting transfers between devices, moved_up(): result.append(lax.ppermute(values[step], axis, pairs))  6.93 us
    unnamed x7, local copies, waits for them, and re-layouts  2.97 us
    pallas_call x1, Pallas kernels, body(): pl.pallas_call(functools.partial(pack_kernel, sizes, cells), out_shape=[j...  2.74 us
  transfers between devices with their start and end apart: 5, of which 4 were waited for; matrix products, arithmetic and copies ran while one was open for 0% of the time, Pallas kernels for 1%

profile of v7, /device:TPU:0, one launch (start us, length us, event | category | flops | bytes accessed | tf_op | source)
XLA Modules:
  0.0 68.9 jit_solution(3028762979508795083)
XLA Ops:
  0.0 0.5 collective-permute-start
  0.5 0.1 collective-permute-start.1
  0.5 0.0 copy-start.2
  0.5 0.7 copy-done.2
  1.2 0.1 copy.5
  1.3 0.1 reshape.19.slots
  1.4 0.5 matrices.1
  1.9 0.5 collective-permute-done.far_d
  2.4 0.9 %collective-permute-done.1.far_a = bf16[4,8,80,128]{3,2,1,0:T(8,128)(2,1)S(1)} collective-permute-done((bf16[4,8,80,128]{3,2,1,0:T(8,128)(2,1)}, bf16[4,8,80,128]{3,2,1,0:T(8,128)(2,1)S(1)}, u32[]{:S(2)}, u32[]{:S(2)}) %collective-permute-start.1) | collective-permute-done | bytes 655392 | tf_op jit(solution)/shard_map/ppermute | solution.py:304
  3.3 0.0 copy-start
  3.3 1.1 %copy-done = bf16[4,4,2,5,16,128]{5,4,3,2,1,0:T(8,128)(2,1)S(1)} copy-done((bf16[4,4,2,5,16,128]{5,4,3,2,1,0:T(8,128)(2,1)S(1)}, bf16[4,4,2,5,16,128]{5,4,3,2,1,0:T(8,128)(2,1)}, u32[]{:S(2)}) %copy-start) | copy-done | bytes 655384
  4.4 0.0 copy-start.1
  4.4 1.1 %copy-done.1 = bf16[4,4,2,5,16,128]{5,4,3,2,1,0:T(8,128)(2,1)S(1)} copy-done((bf16[4,4,2,5,16,128]{5,4,3,2,1,0:T(8,128)(2,1)S(1)}, bf16[4,4,2,5,16,128]{5,4,3,2,1,0:T(8,128)(2,1)}, u32[]{:S(2)}) %copy-start.1) | copy-done | bytes 655384
  5.5 2.7 %pack.1 = (bf16[1456,128]{1,0:T(8,128)(2,1)S(1)}, bf16[1456,128]{1,0:T(8,128)(2,1)S(1)}, bf16[1456,128]{1,0:T(8,128)(2,1)S(1)}, bf16[1456,128]{1,0:T(8,128)(2,1)S(1)}) custom-call(s32[32]{0:T(128)S(1)} %reshape.19.slots, bf16[4,8,80,128]{3,2,1,0:T(8,128)(2,1)S(1)} %bitcast.6, bf16[4,8,80,128]{3,2,1,0:T(8,128)(2,1)S(1)} %bitcast.8, ...), custom_call_target="tpu_custom_call" | custom-call | tf_op jit(solution)/shard_map/pack/pallas_call | solution.py:320
  8.2 3.0 %collective-permute-start.2 = (bf16[1456,128]{1,0:T(8,128)(2,1)S(1)}, bf16[1456,128]{1,0:T(8,128)(2,1)S(1)}, u32[]{:S(2)}, u32[]{:S(2)}) collective-permute-start(bf16[1456,128]{1,0:T(8,128)(2,1)S(1)} %get-tuple-element.14), channel_id=1, source_target_pairs={{0,4},{4,8},{8,12},{12,0},{1,5},{5,9},{9,13},{13,1},{2,6},{6,10},{... | collective-permute-start | bytes 1118216 | tf_op jit(solution)/shard_map/ppermute | solution.py:287
  11.2 2.6 %collective-permute-start.3 = (bf16[1456,128]{1,0:T(8,128)(2,1)S(1)}, bf16[1456,128]{1,0:T(8,128)(2,1)S(1)}, u32[]{:S(2)}, u32[]{:S(2)}) collective-permute-start(bf16[1456,128]{1,0:T(8,128)(2,1)S(1)} %get-tuple-element.15), channel_id=1, source_target_pairs={{0,8},{4,12},{8,0},{12,4},{1,9},{5,13},{9,1},{13,5},{2,10},{6,14},... | collective-permute-start | bytes 1118216 | tf_op jit(solution)/shard_map/ppermute | solution.py:287
  13.8 1.3 %collective-permute-start.4 = (bf16[1456,128]{1,0:T(8,128)(2,1)S(1)}, bf16[1456,128]{1,0:T(8,128)(2,1)S(1)}, u32[]{:S(2)}, u32[]{:S(2)}) collective-permute-start(bf16[1456,128]{1,0:T(8,128)(2,1)S(1)} %get-tuple-element.16), channel_id=1, source_target_pairs={{0,12},{4,0},{8,4},{12,8},{1,13},{5,1},{9,5},{13,9},{2,14},{6,2},{... | collective-permute-start | bytes 1118216 | tf_op jit(solution)/shard_map/ppermute | solution.py:287
  15.2 7.7 %collective-permute-done.2.refs_1_ = bf16[1456,128]{1,0:T(8,128)(2,1)S(1)} collective-permute-done((bf16[1456,128]{1,0:T(8,128)(2,1)S(1)}, bf16[1456,128]{1,0:T(8,128)(2,1)S(1)}, u32[]{:S(2)}, u32[]{:S(2)}) %collective-permute-start.2) | collective-permute-done | bytes 372768 | tf_op jit(solution)/shard_map/ppermute | solution.py:287
  22.9 15.5 %collective-permute-done.3.refs_2_ = bf16[1456,128]{1,0:T(8,128)(2,1)S(1)} collective-permute-done((bf16[1456,128]{1,0:T(8,128)(2,1)S(1)}, bf16[1456,128]{1,0:T(8,128)(2,1)S(1)}, u32[]{:S(2)}, u32[]{:S(2)}) %collective-permute-start.3) | collective-permute-done | bytes 372768 | tf_op jit(solution)/shard_map/ppermute | solution.py:287
  38.4 0.0 collective-permute-done.4.refs_3_
  38.4 7.7 %triads.1 = f32[8,2,40,128]{3,2,1,0:T(8,128)S(1)} custom-call(s32[1]{0:T(128)} %bitcast.mode, bf16[1456,128]{1,0:T(8,128)(2,1)S(1)} %get-tuple-element.13.refs_0_, bf16[1456,128]{1,0:T(8,128)(2,1)S(1)} %collective-permute-done.2.refs_1_, bf16[1456,128]{1,0:T(8,128)(2,1)S(1)} %collective-permute-done.3.refs_2_, ...), custom_call_target="tpu_custom_call" | custom-call | tf_op jit(solution)/shard_map/triads/pallas_call | solution.py:335
  46.1 21.9 %all_to_all.5.came = f32[8,2,40,128]{3,2,1,0:T(8,128)S(1)} all-to-all(f32[8,2,40,128]{3,2,1,0:T(8,128)S(1)} %triads.1), channel_id=1, replica_groups=mesh['case'=2,'mode'=4,'harm'=2,'rad'=2] {'mode','harm'}, dimensions={0} | all-to-all | bytes 655360 | tf_op jit(solution)/shard_map/all_to_all | solution.py:356
  68.0 0.9 %unpack.1 = f32[8,40,128]{2,1,0:T(8,128)} custom-call(f32[8,2,40,128]{3,2,1,0:T(8,128)S(1)} %all_to_all.5.came), custom_call_target="tpu_custom_call" | custom-call | tf_op jit(solution)/shard_map/unpack/pallas_call | solution.py:358
Async XLA Ops:
  0.0 2.4 %collective-permute-start = (bf16[4,8,80,128]{3,2,1,0:T(8,128)(2,1)}, bf16[4,8,80,128]{3,2,1,0:T(8,128)(2,1)S(1)}, u32[]{:S(2)}, u32[]{:S(2)}) collective-permute-start(bf16[4,8,80,128]{3,2,1,0:T(8,128)(2,1)} %bitcast.5), channel_id=1, source_target_pairs={{0,1},{1,0},{2,3},{3,2},{4,5},{5,4},{6,7},{7,6},{8,9},{9,8},{10,11... | collective-permute-start | bytes 1966088 | tf_op jit(solution)/shard_map/ppermute | solution.py:303
  0.5 2.9 %collective-permute-start.1 = (bf16[4,8,80,128]{3,2,1,0:T(8,128)(2,1)}, bf16[4,8,80,128]{3,2,1,0:T(8,128)(2,1)S(1)}, u32[]{:S(2)}, u32[]{:S(2)}) collective-permute-start(bf16[4,8,80,128]{3,2,1,0:T(8,128)(2,1)} %bitcast.7), channel_id=1, source_target_pairs={{0,1},{1,0},{2,3},{3,2},{4,5},{5,4},{6,7},{7,6},{8,9},{9,8},{10,11... | collective-permute-start | bytes 1966088 | tf_op jit(solution)/shard_map/ppermute | solution.py:304
  0.5 0.7 copy-start.2
  3.3 1.1 %copy-start = (bf16[4,4,2,5,16,128]{5,4,3,2,1,0:T(8,128)(2,1)S(1)}, bf16[4,4,2,5,16,128]{5,4,3,2,1,0:T(8,128)(2,1)}, u32[]{:S(2)}) copy-start(bf16[4,4,2,5,16,128]{5,4,3,2,1,0:T(8,128)(2,1)} %param.3) | copy-start | bytes 1966084
  4.4 1.1 %copy-start.1 = (bf16[4,4,2,5,16,128]{5,4,3,2,1,0:T(8,128)(2,1)S(1)}, bf16[4,4,2,5,16,128]{5,4,3,2,1,0:T(8,128)(2,1)}, u32[]{:S(2)}) copy-start(bf16[4,4,2,5,16,128]{5,4,3,2,1,0:T(8,128)(2,1)} %param.4) | copy-start | bytes 1966084
  8.2 14.6 %collective-permute-start.2 = (bf16[1456,128]{1,0:T(8,128)(2,1)S(1)}, bf16[1456,128]{1,0:T(8,128)(2,1)S(1)}, u32[]{:S(2)}, u32[]{:S(2)}) collective-permute-start(bf16[1456,128]{1,0:T(8,128)(2,1)S(1)} %get-tuple-element.14), channel_id=1, source_target_pairs={{0,4},{4,8},{8,12},{12,0},{1,5},{5,9},{9,13},{13,1},{2,6},{6,10},{... | collective-permute-start | bytes 1118216 | tf_op jit(solution)/shard_map/ppermute | solution.py:287
  11.2 27.1 %collective-permute-start.3 = (bf16[1456,128]{1,0:T(8,128)(2,1)S(1)}, bf16[1456,128]{1,0:T(8,128)(2,1)S(1)}, u32[]{:S(2)}, u32[]{:S(2)}) collective-permute-start(bf16[1456,128]{1,0:T(8,128)(2,1)S(1)} %get-tuple-element.15), channel_id=1, source_target_pairs={{0,8},{4,12},{8,0},{12,4},{1,9},{5,13},{9,1},{13,5},{2,10},{6,14},... | collective-permute-start | bytes 1118216 | tf_op jit(solution)/shard_map/ppermute | solution.py:287
  13.8 24.5 %collective-permute-start.4 = (bf16[1456,128]{1,0:T(8,128)(2,1)S(1)}, bf16[1456,128]{1,0:T(8,128)(2,1)S(1)}, u32[]{:S(2)}, u32[]{:S(2)}) collective-permute-start(bf16[1456,128]{1,0:T(8,128)(2,1)S(1)} %get-tuple-element.16), channel_id=1, source_target_pairs={{0,12},{4,0},{8,4},{12,8},{1,13},{5,1},{9,5},{13,9},{2,14},{6,2},{... | collective-permute-start | bytes 1118216 | tf_op jit(solution)/shard_map/ppermute | solution.py:287

commit v8 on v7

--- a/solution.py
+++ b/solution.py
@@ -42,7 +42,7 @@
     return jnp.concatenate([ref[k, group, rows, :] for k in range(ref.shape[0])], axis=1)
 
 
-def matrix_kernel(sizes, groups, mode, rad, main_m, halo_m):
+def matrix_kernel(sizes, groups, mode, rad, _direct, _adjoint, main_m, halo_m):
     harms, blocks, width = sizes
     harm_in, cell_in, owner, lane = columns(harms, blocks, mode[0])
     main_m[...] = one_hot(
@@ -311,11 +311,11 @@
             jax.ShapeDtypeStruct((depth, span), jnp.bfloat16),
             jax.ShapeDtypeStruct((2 * depth, span), jnp.bfloat16),
         ],
-        in_specs=smem(2),
+        in_specs=smem(2) + vmem(2),
         out_specs=vmem(2),
         compiler_params=params,
         name="matrices",
-    )(mode, rad)
+    )(mode, rad, direct, adjoint)
     payload_rows = 2 * fields * tile + 2 * group_rows + SLOT_ROWS
     slabs = pl.pallas_call(
         functools.partial(pack_kernel, sizes, cells),

time: 69.1 us -> 68.3 us (0.988)
  waiting for transfers between devices: 24.6 us -> 23 us
  local copies, waits for them, and re-layouts: 3.06 us -> 3.81 us
    ppermute x1, waiting for transfers between devices: 0.94 us -> 0.01 us  [body(): far_adjoint = lax.ppermute(adjoint, 'rad', swap)]
    unnamed x7 -> x11, local copies, waits for them, and re-layouts: 2.97 us -> 3.71 us
  transfers between devices with their start and end apart: 5 -> 5, of which waited for: 4 -> 2; matrix products, arithmetic and copies ran while one was open for 0% -> 0% of each run, Pallas kernels for 1% -> 1%
where the time goes in v8:
time: 68.3 us; the launch traced here: 68 us
  waiting for transfers between devices  23 us (34%)
  blocking collectives  21.7 us (32%)
  Pallas kernels  11.8 us (17%)
  starting transfers between devices  7.52 us (11%)
  local copies, waits for them, and re-layouts  3.81 us (6%)
    ppermute x3, waiting for transfers between devices, moved_up(): result.append(lax.ppermute(values[step], axis, pairs))  23 us
    all_to_all x1, blocking collectives, body(): lax.all_to_all(sent, ('mode', 'harm'), split_axis=0, concat_axis=0, tiled...  21.7 us
    pallas_call x1, Pallas kernels, body(): pl.pallas_call(functools.partial(triad_kernel, sizes), out_shape=jax.Shap...  7.72 us
    ppermute x3, starting transfers between devices, moved_up(): result.append(lax.ppermute(values[step], axis, pairs))  7.01 us
    unnamed x11, local copies, waits for them, and re-layouts  3.71 us
    pallas_call x1, Pallas kernels, body(): pl.pallas_call(functools.partial(pack_kernel, sizes, cells), out_shape=[j...  2.74 us
  transfers between devices with their start and end apart: 5, of which 2 were waited for; matrix products, arithmetic and copies ran while one was open for 0% of the time, Pallas kernels for 1%

profile of v8, /device:TPU:0, one launch (start us, length us, event | category | flops | bytes accessed | tf_op | source)
XLA Modules:
  0.0 68.0 jit_solution(12452564694465593294)
XLA Ops:
  0.0 0.5 collective-permute-start
  0.5 0.1 collective-permute-start.1
  0.5 0.0 copy-start.4
  0.5 0.7 %copy-done.4 = s32[4,4,2]{1,2,0:T(2,128)S(1)} copy-done((s32[4,4,2]{1,2,0:T(2,128)S(1)}, s32[4,4,2]{1,2,0:T(2,128)}, u32[]{:S(2)}) %copy-start.4) | copy-done | bytes 152
  1.2 0.1 copy.5
  1.3 0.1 reshape.19.slots
  1.4 0.0 copy-start
  1.4 1.1 %copy-done = bf16[4,4,2,5,16,128]{5,4,3,2,1,0:T(8,128)(2,1)S(1)} copy-done((bf16[4,4,2,5,16,128]{5,4,3,2,1,0:T(8,128)(2,1)S(1)}, bf16[4,4,2,5,16,128]{5,4,3,2,1,0:T(8,128)(2,1)}, u32[]{:S(2)}) %copy-start) | copy-done | bytes 655384
  2.5 0.0 copy-start.2
  2.5 1.1 %copy-done.2 = bf16[4,4,2,5,16,128]{5,4,3,2,1,0:T(8,128)(2,1)S(1)} copy-done((bf16[4,4,2,5,16,128]{5,4,3,2,1,0:T(8,128)(2,1)S(1)}, bf16[4,4,2,5,16,128]{5,4,3,2,1,0:T(8,128)(2,1)}, u32[]{:S(2)}) %copy-start.2) | copy-done | bytes 655384
  3.6 0.0 copy-start.1
  3.6 0.0 copy-start.3
  3.6 0.5 matrices.1
  4.1 0.0 collective-permute-done.far_d
  4.1 0.0 collective-permute-done.1.far_a
  4.1 0.5 copy-done.1
  4.7 0.2 copy-done.3
  4.9 2.7 %pack.1 = (bf16[1456,128]{1,0:T(8,128)(2,1)S(1)}, bf16[1456,128]{1,0:T(8,128)(2,1)S(1)}, bf16[1456,128]{1,0:T(8,128)(2,1)S(1)}, bf16[1456,128]{1,0:T(8,128)(2,1)S(1)}) custom-call(s32[32]{0:T(128)S(1)} %reshape.19.slots, bf16[4,8,80,128]{3,2,1,0:T(8,128)(2,1)S(1)} %bitcast.7, bf16[4,8,80,128]{3,2,1,0:T(8,128)(2,1)S(1)} %bitcast.10, ...), custom_call_target="tpu_custom_call" | custom-call | tf_op jit(solution)/shard_map/pack/pallas_call | solution.py:320
  7.6 3.1 %collective-permute-start.2 = (bf16[1456,128]{1,0:T(8,128)(2,1)S(1)}, bf16[1456,128]{1,0:T(8,128)(2,1)S(1)}, u32[]{:S(2)}, u32[]{:S(2)}) collective-permute-start(bf16[1456,128]{1,0:T(8,128)(2,1)S(1)} %get-tuple-element.14), channel_id=1, source_target_pairs={{0,4},{4,8},{8,12},{12,0},{1,5},{5,9},{9,13},{13,1},{2,6},{6,10},{... | collective-permute-start | bytes 1118216 | tf_op jit(solution)/shard_map/ppermute | solution.py:287
  10.7 2.6 %collective-permute-start.3 = (bf16[1456,128]{1,0:T(8,128)(2,1)S(1)}, bf16[1456,128]{1,0:T(8,128)(2,1)S(1)}, u32[]{:S(2)}, u32[]{:S(2)}) collective-permute-start(bf16[1456,128]{1,0:T(8,128)(2,1)S(1)} %get-tuple-element.15), channel_id=1, source_target_pairs={{0,8},{4,12},{8,0},{12,4},{1,9},{5,13},{9,1},{13,5},{2,10},{6,14},... | collective-permute-start | bytes 1118216 | tf_op jit(solution)/shard_map/ppermute | solution.py:287
  13.3 1.3 %collective-permute-start.4 = (bf16[1456,128]{1,0:T(8,128)(2,1)S(1)}, bf16[1456,128]{1,0:T(8,128)(2,1)S(1)}, u32[]{:S(2)}, u32[]{:S(2)}) collective-permute-start(bf16[1456,128]{1,0:T(8,128)(2,1)S(1)} %get-tuple-element.16), channel_id=1, source_target_pairs={{0,12},{4,0},{8,4},{12,8},{1,13},{5,1},{9,5},{13,9},{2,14},{6,2},{... | collective-permute-start | bytes 1118216 | tf_op jit(solution)/shard_map/ppermute | solution.py:287
  14.6 7.7 %collective-permute-done.2.refs_1_ = bf16[1456,128]{1,0:T(8,128)(2,1)S(1)} collective-permute-done((bf16[1456,128]{1,0:T(8,128)(2,1)S(1)}, bf16[1456,128]{1,0:T(8,128)(2,1)S(1)}, u32[]{:S(2)}, u32[]{:S(2)}) %collective-permute-start.2) | collective-permute-done | bytes 372768 | tf_op jit(solution)/shard_map/ppermute | solution.py:287
  22.3 15.3 %collective-permute-done.3.refs_2_ = bf16[1456,128]{1,0:T(8,128)(2,1)S(1)} collective-permute-done((bf16[1456,128]{1,0:T(8,128)(2,1)S(1)}, bf16[1456,128]{1,0:T(8,128)(2,1)S(1)}, u32[]{:S(2)}, u32[]{:S(2)}) %collective-permute-start.3) | collective-permute-done | bytes 372768 | tf_op jit(solution)/shard_map/ppermute | solution.py:287
  37.7 0.0 collective-permute-done.4.refs_3_
  37.7 7.7 %triads.1 = f32[8,2,40,128]{3,2,1,0:T(8,128)S(1)} custom-call(s32[1]{0:T(128)} %bitcast.mode, bf16[1456,128]{1,0:T(8,128)(2,1)S(1)} %get-tuple-element.13.refs_0_, bf16[1456,128]{1,0:T(8,128)(2,1)S(1)} %collective-permute-done.2.refs_1_, bf16[1456,128]{1,0:T(8,128)(2,1)S(1)} %collective-permute-done.3.refs_2_, ...), custom_call_target="tpu_custom_call" | custom-call | tf_op jit(solution)/shard_map/triads/pallas_call | solution.py:335
  45.4 21.7 %all_to_all.5.came = f32[8,2,40,128]{3,2,1,0:T(8,128)S(1)} all-to-all(f32[8,2,40,128]{3,2,1,0:T(8,128)S(1)} %triads.1), channel_id=1, replica_groups=mesh['case'=2,'mode'=4,'harm'=2,'rad'=2] {'mode','harm'}, dimensions={0} | all-to-all | bytes 655360 | tf_op jit(solution)/shard_map/all_to_all | solution.py:356
  67.1 0.9 %unpack.1 = f32[8,40,128]{2,1,0:T(8,128)} custom-call(f32[8,2,40,128]{3,2,1,0:T(8,128)S(1)} %all_to_all.5.came), custom_call_target="tpu_custom_call" | custom-call | tf_op jit(solution)/shard_map/unpack/pallas_call | solution.py:358
Async XLA Ops:
  0.0 4.1 %collective-permute-start = (bf16[4,8,80,128]{3,2,1,0:T(8,128)(2,1)}, bf16[4,8,80,128]{3,2,1,0:T(8,128)(2,1)S(1)}, u32[]{:S(2)}, u32[]{:S(2)}) collective-permute-start(bf16[4,8,80,128]{3,2,1,0:T(8,128)(2,1)} %bitcast.5), channel_id=1, source_target_pairs={{0,1},{1,0},{2,3},{3,2},{4,5},{5,4},{6,7},{7,6},{8,9},{9,8},{10,11... | collective-permute-start | bytes 1966088 | tf_op jit(solution)/shard_map/ppermute | solution.py:303
  0.5 3.7 %collective-permute-start.1 = (bf16[4,8,80,128]{3,2,1,0:T(8,128)(2,1)}, bf16[4,8,80,128]{3,2,1,0:T(8,128)(2,1)S(1)}, u32[]{:S(2)}, u32[]{:S(2)}) collective-permute-start(bf16[4,8,80,128]{3,2,1,0:T(8,128)(2,1)} %bitcast.8), channel_id=1, source_target_pairs={{0,1},{1,0},{2,3},{3,2},{4,5},{5,4},{6,7},{7,6},{8,9},{9,8},{10,11... | collective-permute-start | bytes 1966088 | tf_op jit(solution)/shard_map/ppermute | solution.py:304
  0.5 0.7 %copy-start.4 = (s32[4,4,2]{1,2,0:T(2,128)S(1)}, s32[4,4,2]{1,2,0:T(2,128)}, u32[]{:S(2)}) copy-start(s32[4,4,2]{1,2,0:T(2,128)} %param.5) | copy-start | bytes 388
  1.4 1.1 %copy-start = (bf16[4,4,2,5,16,128]{5,4,3,2,1,0:T(8,128)(2,1)S(1)}, bf16[4,4,2,5,16,128]{5,4,3,2,1,0:T(8,128)(2,1)}, u32[]{:S(2)}) copy-start(bf16[4,4,2,5,16,128]{5,4,3,2,1,0:T(8,128)(2,1)} %param.3) | copy-start | bytes 1966084
  2.5 1.1 %copy-start.2 = (bf16[4,4,2,5,16,128]{5,4,3,2,1,0:T(8,128)(2,1)S(1)}, bf16[4,4,2,5,16,128]{5,4,3,2,1,0:T(8,128)(2,1)}, u32[]{:S(2)}) copy-start(bf16[4,4,2,5,16,128]{5,4,3,2,1,0:T(8,128)(2,1)} %param.4) | copy-start | bytes 1966084
  3.6 1.1 %copy-start.1 = (bf16[4,4,2,5,16,128]{5,4,3,2,1,0:T(8,128)(2,1)S(1)}, bf16[4,4,2,5,16,128]{5,4,3,2,1,0:T(8,128)(2,1)}, u32[]{:S(2)}) copy-start(bf16[4,4,2,5,16,128]{5,4,3,2,1,0:T(8,128)(2,1)} %param.3) | copy-start | bytes 1966084
  3.6 1.3 %copy-start.3 = (bf16[4,4,2,5,16,128]{5,4,3,2,1,0:T(8,128)(2,1)S(1)}, bf16[4,4,2,5,16,128]{5,4,3,2,1,0:T(8,128)(2,1)}, u32[]{:S(2)}) copy-start(bf16[4,4,2,5,16,128]{5,4,3,2,1,0:T(8,128)(2,1)} %param.4) | copy-start | bytes 1966084
  7.6 14.7 %collective-permute-start.2 = (bf16[1456,128]{1,0:T(8,128)(2,1)S(1)}, bf16[1456,128]{1,0:T(8,128)(2,1)S(1)}, u32[]{:S(2)}, u32[]{:S(2)}) collective-permute-start(bf16[1456,128]{1,0:T(8,128)(2,1)S(1)} %get-tuple-element.14), channel_id=1, source_target_pairs={{0,4},{4,8},{8,12},{12,0},{1,5},{5,9},{9,13},{13,1},{2,6},{6,10},{... | collective-permute-start | bytes 1118216 | tf_op jit(solution)/shard_map/ppermute | solution.py:287
  10.7 27.0 %collective-permute-start.3 = (bf16[1456,128]{1,0:T(8,128)(2,1)S(1)}, bf16[1456,128]{1,0:T(8,128)(2,1)S(1)}, u32[]{:S(2)}, u32[]{:S(2)}) collective-permute-start(bf16[1456,128]{1,0:T(8,128)(2,1)S(1)} %get-tuple-element.15), channel_id=1, source_target_pairs={{0,8},{4,12},{8,0},{12,4},{1,9},{5,13},{9,1},{13,5},{2,10},{6,14},... | collective-permute-start | bytes 1118216 | tf_op jit(solution)/shard_map/ppermute | solution.py:287
  13.3 24.4 %collective-permute-start.4 = (bf16[1456,128]{1,0:T(8,128)(2,1)S(1)}, bf16[1456,128]{1,0:T(8,128)(2,1)S(1)}, u32[]{:S(2)}, u32[]{:S(2)}) collective-permute-start(bf16[1456,128]{1,0:T(8,128)(2,1)S(1)} %get-tuple-element.16), channel_id=1, source_target_pairs={{0,12},{4,0},{8,4},{12,8},{1,13},{5,1},{9,5},{13,9},{2,14},{6,2},{... | collective-permute-start | bytes 1118216 | tf_op jit(solution)/shard_map/ppermute | solution.py:287

commit v9 on v8

--- a/solution.py
+++ b/solution.py
@@ -1,4 +1,5 @@
 import functools
+import itertools
 import math
 
 import jax
@@ -96,8 +97,9 @@
             out[start : start + group_rows, :] = held[:, lanes].astype(jnp.bfloat16)
     lane = iota((SLOT_ROWS, LANES), 1)
     listed = jnp.zeros((SLOT_ROWS, LANES), jnp.int32)
-    for index in range(slots.shape[0]):
-        listed = jnp.where(lane == index, slots[index], listed)
+    for at, which, stop in itertools.product(*map(range, slots.shape)):
+        index = (at * slots.shape[2] + stop) * 2 + which
+        listed = jnp.where(lane == index, slots[at, which, stop], listed)
     for out in outs:
         out[base + 2 * group_rows :, :] = listed.astype(jnp.float32).astype(jnp.bfloat16)
 
@@ -324,7 +326,7 @@
         out_specs=vmem(blocks),
         compiler_params=params,
         name="pack",
-    )(triad_slots.reshape(-1), direct, adjoint, far_direct, far_adjoint, *matrices)
+    )(jnp.swapaxes(triad_slots, 1, 2), direct, adjoint, far_direct, far_adjoint, *matrices)
     came = moved_up(slabs, "mode")
 
     per_harm, own_cells = blocks // harm_devices, cells // blocks

time: 68.3 us -> 67.4 us (0.987)
  local copies, waits for them, and re-layouts: 3.81 us -> 2.83 us
    unnamed x11 -> x10, local copies, waits for them, and re-layouts: 3.71 us -> 2.83 us
  transfers between devices with their start and end apart: 5 -> 5, of which waited for: 2 -> 3; matrix products, arithmetic and copies ran while one was open for 0% -> 0% of each run, Pallas kernels for 1% -> 1%
where the time goes in v9:
time: 67.4 us; the launch traced here: 67.1 us
  waiting for transfers between devices  23.1 us (34%)
  blocking collectives  21.7 us (32%)
  Pallas kernels  11.9 us (18%)
  starting transfers between devices  7.52 us (11%)
  local copies, waits for them, and re-layouts  2.83 us (4%)
    ppermute x3, waiting for transfers between devices, moved_up(): result.append(lax.ppermute(values[step], axis, pairs))  23 us
    all_to_all x1, blocking collectives, body(): lax.all_to_all(sent, ('mode', 'harm'), split_axis=0, concat_axis=0, tiled...  21.7 us
    pallas_call x1, Pallas kernels, body(): pl.pallas_call(functools.partial(triad_kernel, sizes), out_shape=jax.Shap...  7.72 us
    ppermute x3, starting transfers between devices, moved_up(): result.append(lax.ppermute(values[step], axis, pairs))  7.01 us
    unnamed x10, local copies, waits for them, and re-layouts  2.83 us
    pallas_call x1, Pallas kernels, body(): pl.pallas_call(functools.partial(pack_kernel, sizes, cells), out_shape=[j...  2.8 us
  transfers between devices with their start and end apart: 5, of which 3 were waited for; matrix products, arithmetic and copies ran while one was open for 0% of the time, Pallas kernels for 1%

profile of v9, /device:TPU:0, one launch (start us, length us, event | category | flops | bytes accessed | tf_op | source)
XLA Modules:
  0.0 67.1 jit_solution(15336595687283907297)
XLA Ops:
  0.0 0.5 collective-permute-start
  0.5 0.1 collective-permute-start.1
  0.5 0.0 copy-start
  0.5 1.1 %copy-done = bf16[4,4,2,5,16,128]{5,4,3,2,1,0:T(8,128)(2,1)S(1)} copy-done((bf16[4,4,2,5,16,128]{5,4,3,2,1,0:T(8,128)(2,1)S(1)}, bf16[4,4,2,5,16,128]{5,4,3,2,1,0:T(8,128)(2,1)}, u32[]{:S(2)}) %copy-start) | copy-done | bytes 655384
  1.6 0.0 copy-start.2
  1.6 1.1 %copy-done.2 = bf16[4,4,2,5,16,128]{5,4,3,2,1,0:T(8,128)(2,1)S(1)} copy-done((bf16[4,4,2,5,16,128]{5,4,3,2,1,0:T(8,128)(2,1)S(1)}, bf16[4,4,2,5,16,128]{5,4,3,2,1,0:T(8,128)(2,1)}, u32[]{:S(2)}) %copy-start.2) | copy-done | bytes 655384
  2.7 0.0 copy-start.1
  2.7 0.0 copy-start.3
  2.7 0.5 matrices.1
  3.2 0.0 copy-start.4
  3.2 0.0 collective-permute-done.far_d
  3.2 0.1 collective-permute-done.1.far_a
  3.3 0.4 copy-done.1
  3.8 0.2 copy-done.3
  4.0 0.0 copy-done.4
  4.0 2.8 %pack.1 = (bf16[1456,128]{1,0:T(8,128)(2,1)S(1)}, bf16[1456,128]{1,0:T(8,128)(2,1)S(1)}, bf16[1456,128]{1,0:T(8,128)(2,1)S(1)}, bf16[1456,128]{1,0:T(8,128)(2,1)S(1)}) custom-call(s32[4,2,4]{2,1,0:T(2,128)S(1)} %bitcast.12, bf16[4,8,80,128]{3,2,1,0:T(8,128)(2,1)S(1)} %bitcast.8, bf16[4,8,80,128]{3,2,1,0:T(8,128)(2,1)S(1)} %bitcast.11, ...), custom_call_target="tpu_custom_call" | custom-call | tf_op jit(solution)/shard_map/pack/pallas_call | solution.py:322
  6.8 3.1 %collective-permute-start.2 = (bf16[1456,128]{1,0:T(8,128)(2,1)S(1)}, bf16[1456,128]{1,0:T(8,128)(2,1)S(1)}, u32[]{:S(2)}, u32[]{:S(2)}) collective-permute-start(bf16[1456,128]{1,0:T(8,128)(2,1)S(1)} %get-tuple-element.14), channel_id=1, source_target_pairs={{0,4},{4,8},{8,12},{12,0},{1,5},{5,9},{9,13},{13,1},{2,6},{6,10},{... | collective-permute-start | bytes 1118216 | tf_op jit(solution)/shard_map/ppermute | solution.py:289
  9.9 2.6 %collective-permute-start.3 = (bf16[1456,128]{1,0:T(8,128)(2,1)S(1)}, bf16[1456,128]{1,0:T(8,128)(2,1)S(1)}, u32[]{:S(2)}, u32[]{:S(2)}) collective-permute-start(bf16[1456,128]{1,0:T(8,128)(2,1)S(1)} %get-tuple-element.15), channel_id=1, source_target_pairs={{0,8},{4,12},{8,0},{12,4},{1,9},{5,13},{9,1},{13,5},{2,10},{6,14},... | collective-permute-start | bytes 1118216 | tf_op jit(solution)/shard_map/ppermute | solution.py:289
  12.4 1.3 %collective-permute-start.4 = (bf16[1456,128]{1,0:T(8,128)(2,1)S(1)}, bf16[1456,128]{1,0:T(8,128)(2,1)S(1)}, u32[]{:S(2)}, u32[]{:S(2)}) collective-permute-start(bf16[1456,128]{1,0:T(8,128)(2,1)S(1)} %get-tuple-element.16), channel_id=1, source_target_pairs={{0,12},{4,0},{8,4},{12,8},{1,13},{5,1},{9,5},{13,9},{2,14},{6,2},{... | collective-permute-start | bytes 1118216 | tf_op jit(solution)/shard_map/ppermute | solution.py:289
  13.8 7.7 %collective-permute-done.2.refs_1_ = bf16[1456,128]{1,0:T(8,128)(2,1)S(1)} collective-permute-done((bf16[1456,128]{1,0:T(8,128)(2,1)S(1)}, bf16[1456,128]{1,0:T(8,128)(2,1)S(1)}, u32[]{:S(2)}, u32[]{:S(2)}) %collective-permute-start.2) | collective-permute-done | bytes 372768 | tf_op jit(solution)/shard_map/ppermute | solution.py:289
  21.5 15.3 %collective-permute-done.3.refs_2_ = bf16[1456,128]{1,0:T(8,128)(2,1)S(1)} collective-permute-done((bf16[1456,128]{1,0:T(8,128)(2,1)S(1)}, bf16[1456,128]{1,0:T(8,128)(2,1)S(1)}, u32[]{:S(2)}, u32[]{:S(2)}) %collective-permute-start.3) | collective-permute-done | bytes 372768 | tf_op jit(solution)/shard_map/ppermute | solution.py:289
  36.8 0.0 collective-permute-done.4.refs_3_
  36.8 7.7 %triads.1 = f32[8,2,40,128]{3,2,1,0:T(8,128)S(1)} custom-call(s32[1]{0:T(128)} %bitcast.mode, bf16[1456,128]{1,0:T(8,128)(2,1)S(1)} %get-tuple-element.13.refs_0_, bf16[1456,128]{1,0:T(8,128)(2,1)S(1)} %collective-permute-done.2.refs_1_, bf16[1456,128]{1,0:T(8,128)(2,1)S(1)} %collective-permute-done.3.refs_2_, ...), custom_call_target="tpu_custom_call" | custom-call | tf_op jit(solution)/shard_map/triads/pallas_call | solution.py:337
  44.6 21.7 %all_to_all.5.came = f32[8,2,40,128]{3,2,1,0:T(8,128)S(1)} all-to-all(f32[8,2,40,128]{3,2,1,0:T(8,128)S(1)} %triads.1), channel_id=1, replica_groups=mesh['case'=2,'mode'=4,'harm'=2,'rad'=2] {'mode','harm'}, dimensions={0} | all-to-all | bytes 655360 | tf_op jit(solution)/shard_map/all_to_all | solution.py:358
  66.3 0.9 %unpack.1 = f32[8,40,128]{2,1,0:T(8,128)} custom-call(f32[8,2,40,128]{3,2,1,0:T(8,128)S(1)} %all_to_all.5.came), custom_call_target="tpu_custom_call" | custom-call | tf_op jit(solution)/shard_map/unpack/pallas_call | solution.py:360
Async XLA Ops:
  0.0 3.2 %collective-permute-start = (bf16[4,8,80,128]{3,2,1,0:T(8,128)(2,1)}, bf16[4,8,80,128]{3,2,1,0:T(8,128)(2,1)S(1)}, u32[]{:S(2)}, u32[]{:S(2)}) collective-permute-start(bf16[4,8,80,128]{3,2,1,0:T(8,128)(2,1)} %bitcast.6), channel_id=1, source_target_pairs={{0,1},{1,0},{2,3},{3,2},{4,5},{5,4},{6,7},{7,6},{8,9},{9,8},{10,11... | collective-permute-start | bytes 1966088 | tf_op jit(solution)/shard_map/ppermute | solution.py:305
  0.5 2.9 %collective-permute-start.1 = (bf16[4,8,80,128]{3,2,1,0:T(8,128)(2,1)}, bf16[4,8,80,128]{3,2,1,0:T(8,128)(2,1)S(1)}, u32[]{:S(2)}, u32[]{:S(2)}) collective-permute-start(bf16[4,8,80,128]{3,2,1,0:T(8,128)(2,1)} %bitcast.9), channel_id=1, source_target_pairs={{0,1},{1,0},{2,3},{3,2},{4,5},{5,4},{6,7},{7,6},{8,9},{9,8},{10,11... | collective-permute-start | bytes 1966088 | tf_op jit(solution)/shard_map/ppermute | solution.py:306
  0.5 1.1 %copy-start = (bf16[4,4,2,5,16,128]{5,4,3,2,1,0:T(8,128)(2,1)S(1)}, bf16[4,4,2,5,16,128]{5,4,3,2,1,0:T(8,128)(2,1)}, u32[]{:S(2)}) copy-start(bf16[4,4,2,5,16,128]{5,4,3,2,1,0:T(8,128)(2,1)} %param.3) | copy-start | bytes 1966084
  1.6 1.1 %copy-start.2 = (bf16[4,4,2,5,16,128]{5,4,3,2,1,0:T(8,128)(2,1)S(1)}, bf16[4,4,2,5,16,128]{5,4,3,2,1,0:T(8,128)(2,1)}, u32[]{:S(2)}) copy-start(bf16[4,4,2,5,16,128]{5,4,3,2,1,0:T(8,128)(2,1)} %param.4) | copy-start | bytes 1966084
  2.7 1.1 %copy-start.1 = (bf16[4,4,2,5,16,128]{5,4,3,2,1,0:T(8,128)(2,1)S(1)}, bf16[4,4,2,5,16,128]{5,4,3,2,1,0:T(8,128)(2,1)}, u32[]{:S(2)}) copy-start(bf16[4,4,2,5,16,128]{5,4,3,2,1,0:T(8,128)(2,1)} %param.3) | copy-start | bytes 1966084
  2.7 1.3 %copy-start.3 = (bf16[4,4,2,5,16,128]{5,4,3,2,1,0:T(8,128)(2,1)S(1)}, bf16[4,4,2,5,16,128]{5,4,3,2,1,0:T(8,128)(2,1)}, u32[]{:S(2)}) copy-start(bf16[4,4,2,5,16,128]{5,4,3,2,1,0:T(8,128)(2,1)} %param.4) | copy-start | bytes 1966084
  3.2 0.8 %copy-start.4 = (s32[4,4,2]{1,2,0:T(2,128)S(1)}, s32[4,4,2]{1,2,0:T(2,128)}, u32[]{:S(2)}) copy-start(s32[4,4,2]{1,2,0:T(2,128)} %param.5) | copy-start | bytes 388
  6.8 14.7 %collective-permute-start.2 = (bf16[1456,128]{1,0:T(8,128)(2,1)S(1)}, bf16[1456,128]{1,0:T(8,128)(2,1)S(1)}, u32[]{:S(2)}, u32[]{:S(2)}) collective-permute-start(bf16[1456,128]{1,0:T(8,128)(2,1)S(1)} %get-tuple-element.14), channel_id=1, source_target_pairs={{0,4},{4,8},{8,12},{12,0},{1,5},{5,9},{9,13},{13,1},{2,6},{6,10},{... | collective-permute-start | bytes 1118216 | tf_op jit(solution)/shard_map/ppermute | solution.py:289
  9.9 27.0 %collective-permute-start.3 = (bf16[1456,128]{1,0:T(8,128)(2,1)S(1)}, bf16[1456,128]{1,0:T(8,128)(2,1)S(1)}, u32[]{:S(2)}, u32[]{:S(2)}) collective-permute-start(bf16[1456,128]{1,0:T(8,128)(2,1)S(1)} %get-tuple-element.15), channel_id=1, source_target_pairs={{0,8},{4,12},{8,0},{12,4},{1,9},{5,13},{9,1},{13,5},{2,10},{6,14},... | collective-permute-start | bytes 1118216 | tf_op jit(solution)/shard_map/ppermute | solution.py:289
  12.4 24.4 %collective-permute-start.4 = (bf16[1456,128]{1,0:T(8,128)(2,1)S(1)}, bf16[1456,128]{1,0:T(8,128)(2,1)S(1)}, u32[]{:S(2)}, u32[]{:S(2)}) collective-permute-start(bf16[1456,128]{1,0:T(8,128)(2,1)S(1)} %get-tuple-element.16), channel_id=1, source_target_pairs={{0,12},{4,0},{8,4},{12,8},{1,13},{5,1},{9,5},{13,9},{2,14},{6,2},{... | collective-permute-start | bytes 1118216 | tf_op jit(solution)/shard_map/ppermute | solution.py:289
